TPU v7x, 32 devices: a whole 2x2x4 slice. The times are simulated.
32 devices in a mesh: rep: 2 (over x), shard: 16 (over z, y, core).
Axes of the slice: x: 2, y: 2, z: 4, core: 2. Of those that a mesh axis runs over, the one named last changes fastest.
Arguments:
- tokens: bfloat16 [4096, 768], P(('rep', 'shard')), may hold values from -6 to 6
- cotangent: bfloat16 [4096, 768], P(('rep', 'shard')), may hold values from -6 to 6
- lengths: int32 [32, 3], P(('rep', 'shard')), may hold values from 1 to 96, 128 in all within a row
- routes: int32 [4096, 1], P(('rep', 'shard')), may hold values from 0 to 1; in each aligned block of 128 rows (0 to 127, 128 to 255, ...) at most 80 rows name the same one
- bucket_ids: int32 [255], replicated, may hold values from 0 to 31
- attn_in: bfloat16 [3, 768, 768], P(None, 'shard'), may hold values from -0.21875 to 0.21875
- attn_out: bfloat16 [768, 768], P('shard'), may hold values from -0.875 to 0.875
- gains: bfloat16 [2, 768], P(None, 'shard'), may hold values from 0.25 to 1.75
- router: bfloat16 [768, 2], P('shard'), may hold values from -0.109375 to 0.109375
- rel_table: bfloat16 [32, 12], P('shard'), may hold values from -4 to 4
- expert_in: bfloat16 [2, 768, 3072], P(None, 'shard'), may hold values from -0.21875 to 0.21875
- expert_out: bfloat16 [2, 3072, 768], P(None, 'shard'), may hold values from -0.21875 to 0.21875
Outputs:
- layer_out: bfloat16 [4096, 768], P(('rep', 'shard'))
- input_grad: float32 [4096, 768], P(('rep', 'shard'))
- grad_attn_in: float32 [3, 768, 768], P(None, 'shard')
- grad_attn_out: float32 [768, 768], P('shard')
- grad_gains: float32 [2, 768], P(None, 'shard')
- grad_router: float32 [768, 2], P('shard')
- grad_rel_table: float32 [32, 12], P('shard')
- grad_expert_in: float32 [2, 768, 3072], P(None, 'shard')
- grad_expert_out: float32 [2, 3072, 768], P(None, 'shard')
Inputs may be any that keep to these rules, and one draw needn't show every extreme that they name: Row b holds the lengths of the 3 sequences of device block b; they sum to 128, and some block has one of exactly 96. `routes`: within the 128 rows of one device no expert is named more than 80 times, and in every draw some device names some expert exactly 80 times.
All inputs are finite; a program needn't handle non-finite values.
Results may differ from a plain program's by a relative error of at most 0.012.
Values may be sent and summed in bfloat16 or wider, within the bound.
A program may use at most 192 MiB of HBM per device.

v0:
```python
import functools

import jax
import jax.numpy as jnp
from jax import lax
from jax.experimental import pallas as pl
from jax.experimental.pallas import tpu as pltpu
from jax.sharding import PartitionSpec as P

BUCKETS = 32
CAP = 80


epsilon = 1e-06


def rms_norm(values, gain):
    return values * lax.rsqrt(jnp.mean(values * values, axis=-1, keepdims=True) + epsilon) * gain


def gelu_tanh(values):
    return jax.nn.gelu(values, approximate=True)


def swap(array, size):
    return lax.ppermute(array, "shard", [(i, i ^ 1) for i in range(size)])


def pair_order(core, mine, other, axis):
    first = jnp.where(core == 0, mine, other)
    second = jnp.where(core == 0, other, mine)
    return jnp.concatenate([first, second], axis=axis)


def rep_sum(array, reps):
    if reps == 2:
        other = lax.ppermute(array, "rep", [(0, 1), (1, 0)])
        return array.astype(jnp.float32) + other.astype(jnp.float32)
    return lax.psum(array.astype(jnp.float32), "rep")


def pick(array, index, axis=0):
    return lax.dynamic_index_in_dim(array, index, axis, keepdims=False)


def pad_row(values, width):
    flat = values.reshape(-1)
    return jnp.pad(flat, (0, width - flat.shape[0])).reshape(1, width)


def grid_of(size):
    chips = size // 2
    outer = 4 if chips % 4 == 0 else 1
    return outer, chips // outer


def place_of(size):
    outer, inner = grid_of(size)
    me = lax.axis_index("shard")
    core = lax.rem(me, 2)
    chip = lax.div(me, 2)
    z = lax.div(chip, inner)
    y = lax.rem(chip, inner)

    def device(far, near):
        return {"shard": (far * inner + near) * 2 + core}

    return z, y, device


def greet(size):
    outer, inner = grid_of(size)
    z, y, device = place_of(size)
    barrier = pltpu.get_barrier_semaphore()
    for d in range(1, outer):
        pl.semaphore_signal(
            barrier,
            inc=1,
            device_id=device(lax.rem(z + d, outer), y),
            device_id_type=pl.DeviceIdType.MESH,
        )
    for e in range(1, inner):
        pl.semaphore_signal(
            barrier,
            inc=1,
            device_id=device(z, lax.rem(y + e, inner)),
            device_id_type=pl.DeviceIdType.MESH,
        )
    pl.semaphore_wait(barrier, outer + inner - 2)


def send(src, dst, send_sem, recv_sem, target):
    copy = pltpu.make_async_remote_copy(
        src_ref=src,
        dst_ref=dst,
        send_sem=send_sem,
        recv_sem=recv_sem,
        device_id=target,
        device_id_type=pl.DeviceIdType.MESH,
    )
    copy.start()
    return copy


def gather_kernel(size, x_ref, o_ref, own_sem, z_send, z_recv, y_send, y_recv):
    outer, inner = grid_of(size)
    z, y, device = place_of(size)
    chip = z * inner + y
    greet(size)
    own = pltpu.make_async_copy(x_ref, o_ref.at[chip], own_sem)
    own.start()
    along = []
    for d in range(1, outer):
        target = device(lax.rem(z + d, outer), y)
        along.append(send(x_ref, o_ref.at[chip], z_send.at[d - 1], z_recv.at[d - 1], target))
    across = []
    for e in range(1, inner):
        target = device(z, lax.rem(y + e, inner))
        across.append(send(x_ref, o_ref.at[chip], y_send.at[0, e - 1], y_recv.at[0, e - 1], target))
    for d in range(1, outer):
        along[d - 1].wait_recv()
        source = lax.rem(z + outer - d, outer) * inner + y
        for e in range(1, inner):
            target = device(z, lax.rem(y + e, inner))
            across.append(
                send(
                    o_ref.at[source],
                    o_ref.at[source],
                    y_send.at[d, e - 1],
                    y_recv.at[d, e - 1],
                    target,
                )
            )
    own.wait()
    for copy in across:
        copy.wait_recv()
    for copy in along + across:
        copy.wait_send()


def gather_chips(block, size, collective_id):
    outer, inner = grid_of(size)
    return pl.pallas_call(
        functools.partial(gather_kernel, size),
        out_shape=jax.ShapeDtypeStruct((size // 2,) + block.shape, block.dtype),
        in_specs=[pl.BlockSpec(memory_space=pltpu.VMEM)],
        out_specs=pl.BlockSpec(memory_space=pltpu.VMEM),
        scratch_shapes=[
            pltpu.SemaphoreType.DMA,
            pltpu.SemaphoreType.DMA((max(outer - 1, 1),)),
            pltpu.SemaphoreType.DMA((max(outer - 1, 1),)),
            pltpu.SemaphoreType.DMA((outer, max(inner - 1, 1))),
            pltpu.SemaphoreType.DMA((outer, max(inner - 1, 1))),
        ],
        compiler_params=pltpu.CompilerParams(
            collective_id=collective_id, has_side_effects=True, vmem_limit_bytes=40 << 20
        ),
    )(block)


def scatter_kernel(
    size, p_ref, o_ref, y_buf, z_out, z_in, total, y_send, y_recv, z_send, z_recv
):
    outer, inner = grid_of(size)
    z, y, device = place_of(size)
    rows = o_ref.shape[0]
    step = 16
    greet(size)
    across = {}
    order = [*range(1, outer), 0]
    for d in order:
        far = lax.rem(z + d, outer)
        for e in range(1, inner):
            near = lax.rem(y + e, inner)
            across[d, e] = send(
                p_ref.at[far * inner + near],
                y_buf.at[e - 1, d],
                y_send.at[d, e - 1],
                y_recv.at[d, e - 1],
                device(z, near),
            )
    along = []
    for d in order:
        far = lax.rem(z + d, outer)
        for e in range(1, inner):
            across[d, e].wait_recv()

        def add(i, carry):
            at = pl.ds(pl.multiple_of(i * step, step), step)
            value = p_ref[far * inner + y, at].astype(jnp.float32)
            for e in range(1, inner):
                value = value + y_buf[e - 1, d, at].astype(jnp.float32)
            if d == 0:
                total[at] = value
            else:
                z_out[d - 1, at] = value.astype(z_out.dtype)
            return carry

        lax.fori_loop(0, rows // step, add, 0)
        if d > 0:
            along.append(
                send(
                    z_out.at[d - 1],
                    z_in.at[d - 1],
                    z_send.at[d - 1],
                    z_recv.at[d - 1],
                    device(far, y),
                )
            )
    for copy in along:
        copy.wait_recv()

    def finish(i, carry):
        at = pl.ds(pl.multiple_of(i * step, step), step)
        value = total[at]
        for d in range(1, outer):
            value = value + z_in[d - 1, at].astype(jnp.float32)
        o_ref[at] = value.astype(o_ref.dtype)
        return carry

    lax.fori_loop(0, rows // step, finish, 0)
    for copy in [*along, *across.values()]:
        copy.wait_send()


def scatter_chips(partial, size, collective_id):
    outer, inner = grid_of(size)
    rows, width = partial.shape[1:]
    steps = max(outer - 1, 1)
    sides = max(inner - 1, 1)
    return pl.pallas_call(
        functools.partial(scatter_kernel, size),
        out_shape=jax.ShapeDtypeStruct((rows, width), partial.dtype),
        in_specs=[pl.BlockSpec(memory_space=pltpu.VMEM)],
        out_specs=pl.BlockSpec(memory_space=pltpu.VMEM),
        scratch_shapes=[
            pltpu.VMEM((sides, outer, rows, width), partial.dtype),
            pltpu.VMEM((steps, rows, width), partial.dtype),
            pltpu.VMEM((steps, rows, width), partial.dtype),
            pltpu.VMEM((rows, width), jnp.float32),
            pltpu.SemaphoreType.DMA((outer, sides)),
            pltpu.SemaphoreType.DMA((outer, sides)),
            pltpu.SemaphoreType.DMA((steps,)),
            pltpu.SemaphoreType.DMA((steps,)),
        ],
        compiler_params=pltpu.CompilerParams(
            collective_id=collective_id, has_side_effects=True, vmem_limit_bytes=48 << 20
        ),
    )(partial)


def attend_kernel(heads, head_size, p_ref, bias_ref, down_ref, across_ref, c_ref, probs_ref):
    length = p_ref.shape[1]
    allowed = down_ref[...] == across_ref[...]
    parts = []
    for h in range(heads):
        at = slice(h * head_size, (h + 1) * head_size)
        raw = lax.dot_general(
            p_ref[0, :, at],
            p_ref[1, :, at],
            (((1,), (1,)), ((), ())),
            preferred_element_type=jnp.float32,
        )
        spread = jnp.broadcast_to(bias_ref[h : h + 1, :], (length, 2 * length))
        skewed = pltpu.roll(spread, length + 1, 1, stride=1, stride_axis=0)
        scores = jnp.where(allowed, raw * 0.125 + skewed[:, :length], -1e30)
        expo = jnp.exp(scores - jnp.max(scores, axis=1, keepdims=True))
        probs = expo / jnp.sum(expo, axis=1, keepdims=True)
        probs_ref[h] = probs
        parts.append(
            jnp.dot(
                probs.astype(jnp.bfloat16), p_ref[2, :, at], preferred_element_type=jnp.float32
            )
        )
    c_ref[...] = jnp.concatenate(parts, axis=1).astype(c_ref.dtype)


def attend(projected, offset_bias, segment, heads):
    length, width = projected.shape[1:]
    return pl.pallas_call(
        functools.partial(attend_kernel, heads, width // heads),
        out_shape=(
            jax.ShapeDtypeStruct((length, width), jnp.bfloat16),
            jax.ShapeDtypeStruct((heads, length, length), jnp.float32),
        ),
        compiler_params=pltpu.CompilerParams(vmem_limit_bytes=32 << 20),
    )(projected, offset_bias, segment[:, None], segment[None, :])


def attend_back_kernel(heads, head_size, p_ref, probs_ref, g_ref, o_ref, diag_ref):
    length = p_ref.shape[1]
    row = lax.broadcasted_iota(jnp.int32, (length, length), 0)
    col = lax.broadcasted_iota(jnp.int32, (length, length), 1)
    mirror = jnp.where(row + col == length - 1, 1.0, 0.0).astype(jnp.bfloat16)
    blank = jnp.zeros((length, length), jnp.float32)
    down = (((0,), (0,)), ((), ()))
    parts = [[], [], []]
    for h in range(heads):
        at = slice(h * head_size, (h + 1) * head_size)
        grad = g_ref[:, at]
        probs = probs_ref[h]
        prob_grad = lax.dot_general(
            grad, p_ref[2, :, at], (((1,), (1,)), ((), ())), preferred_element_type=jnp.float32
        )
        total = jnp.sum(probs * prob_grad, axis=1, keepdims=True)
        low = (probs * (prob_grad - total)).astype(jnp.bfloat16)
        flipped = jnp.dot(low, mirror, preferred_element_type=jnp.float32)
        skewed = pltpu.roll(
            jnp.concatenate([flipped, blank], axis=1), 0, 1, stride=1, stride_axis=0
        )
        diag_ref[h : h + 1, :] = jnp.sum(skewed, axis=0, keepdims=True)
        parts[0].append(
            jnp.dot(low, p_ref[1, :, at], preferred_element_type=jnp.float32) * 0.125
        )
        parts[1].append(
            lax.dot_general(low, p_ref[0, :, at], down, preferred_element_type=jnp.float32) * 0.125
        )
        parts[2].append(
            lax.dot_general(
                probs.astype(jnp.bfloat16), grad, down, preferred_element_type=jnp.float32
            )
        )
    for k in range(3):
        o_ref[k] = jnp.concatenate(parts[k], axis=1).astype(o_ref.dtype)


def attend_back(projected, probs, context_grad):
    heads, length = probs.shape[:2]
    width = context_grad.shape[1]
    return pl.pallas_call(
        functools.partial(attend_back_kernel, heads, width // heads),
        out_shape=(
            jax.ShapeDtypeStruct((3, length, width), jnp.bfloat16),
            jax.ShapeDtypeStruct((heads, 2 * length), jnp.float32),
        ),
        compiler_params=pltpu.CompilerParams(vmem_limit_bytes=32 << 20),
    )(projected, probs, context_grad)


def shards(
    size,
    reps,
    tokens,
    cotangent,
    lengths,
    routes,
    bucket_ids,
    attn_in,
    attn_out,
    gains,
    router,
    rel_table,
    expert_in,
    expert_out,
):
    highest = lax.Precision.HIGHEST
    low = jnp.bfloat16
    length, width = tokens.shape
    heads = rel_table.shape[1]
    experts = expert_in.shape[0]
    capacity = CAP
    bucket_count = BUCKETS
    chips = size // 2
    rows = width // size
    hidden_units = expert_in.shape[2]
    strip = hidden_units // chips
    groups = [[2 * j + c for j in range(chips)] for c in range(2)]
    core = lax.axis_index("shard") % 2

    places = jnp.arange(length, dtype=jnp.int32)
    chosen = routes[:, 0]
    picked = chosen[:, None] == jnp.arange(experts, dtype=jnp.int32)[None, :]
    earlier = (places[None, :] < places[:, None]).astype(low)
    ranks = jnp.dot(earlier, picked.astype(low), preferred_element_type=jnp.float32)
    rank = jnp.sum(jnp.where(picked, ranks, 0.0), axis=1).astype(jnp.int32)
    slot = chosen * capacity + rank
    dispatch = (jnp.arange(experts * capacity, dtype=jnp.int32)[:, None] == slot[None, :]).astype(
        low
    )
    up_sent = jnp.dot(dispatch, cotangent, preferred_element_type=jnp.float32).astype(low)
    up_sent = up_sent.reshape(experts, capacity, width)
    up_mine = pick(up_sent, core)
    up_other = swap(pick(up_sent, 1 - core), size)
    up_block = jnp.concatenate([up_mine, up_other], axis=0)
    up_slots = lax.all_gather(up_block, "shard", axis=0, tiled=True, axis_index_groups=groups)

    packed = jnp.concatenate(
        [
            attn_in.reshape(3 * rows, width),
            attn_out,
            pad_row(gains, width),
            pad_row(router, width),
            pad_row(rel_table, width),
        ],
        axis=0,
    )
    depth = packed.shape[0]
    extra = -depth % 16
    packed = jnp.pad(packed, ((0, extra), (0, 0)))
    depth = depth + extra
    same = gather_chips(packed, size, 0)
    other = swap(same, size)
    whole = jnp.stack(
        [jnp.where(core == 0, same, other), jnp.where(core == 0, other, same)], axis=1
    ).reshape(size, depth, width)
    full_in = whole[:, : 3 * rows].reshape(size, 3, rows, width)
    full_in = jnp.transpose(full_in, (1, 0, 2, 3)).reshape(3, width, width)
    full_out = whole[:, 3 * rows : 4 * rows].reshape(width, width)
    spot = 4 * rows
    full_gains = whole[:, spot, : 2 * rows].reshape(size, 2, rows)
    full_gains = jnp.transpose(full_gains, (1, 0, 2)).reshape(2, width)
    full_router = whole[:, spot + 1, : experts * rows].reshape(width, experts)
    table_rows = bucket_count // size
    full_table = whole[:, spot + 2, : table_rows * heads].reshape(bucket_count, heads)

    in_mine = pick(expert_in, core)
    in_other = swap(pick(expert_in, 1 - core), size)
    in_rows = pair_order(core, in_mine, in_other, 0).reshape(2 * rows, chips, strip)
    in_rows = jnp.transpose(in_rows, (1, 0, 2))
    in_strip = lax.all_to_all(
        in_rows, "shard", 0, 0, axis_index_groups=groups, tiled=True
    ).reshape(width, strip)
    out_mine = pick(expert_out, core)
    out_other = swap(pick(expert_out, 1 - core), size)
    out_strip = pair_order(core, out_mine, out_other, 0)

    inputs = tokens.astype(jnp.float32)
    upstream = cotangent.astype(jnp.float32)
    gain_attn = full_gains[0].astype(jnp.float32)
    gain_ffn = full_gains[1].astype(jnp.float32)
    normed = rms_norm(inputs, gain_attn).astype(low)
    projected = jnp.einsum(
        "td,kde->kte", normed, full_in, preferred_element_type=jnp.float32
    ).astype(low)
    offset_onehot = (
        jnp.pad(bucket_ids, (0, 1), constant_values=-1)[:, None] == jnp.arange(bucket_count, dtype=jnp.int32)[None, :]
    ).astype(jnp.float32)
    offset_bias = jnp.einsum(
        "ob,bh->ho", offset_onehot, full_table.astype(jnp.float32), precision=highest
    )
    seqs = jnp.arange(lengths.shape[1], dtype=jnp.int32)
    ends = jnp.sum(jnp.where(seqs[None, :] <= seqs[:, None], lengths[0][None, :], 0), axis=1)
    segment = jnp.sum((places[:, None] >= ends[None, :]).astype(jnp.int32), axis=1)
    context, probs = attend(projected, offset_bias, segment, heads)
    hidden = inputs + jnp.dot(context, full_out, preferred_element_type=jnp.float32)
    normed_ffn = rms_norm(hidden, gain_ffn).astype(low)
    logits = jnp.dot(normed_ffn, full_router, preferred_element_type=jnp.float32)
    gate_probs = jax.nn.softmax(logits, axis=-1)
    gate = jnp.sum(jnp.where(picked, gate_probs, 0.0), axis=1)
    sent = jnp.dot(dispatch, normed_ffn, preferred_element_type=jnp.float32).astype(low)
    sent = sent.reshape(experts, capacity, width)
    sent_mine = pick(sent, core)
    sent_other = swap(pick(sent, 1 - core), size)
    block = jnp.concatenate([sent_mine, sent_other], axis=0)
    batch = gather_chips(block, size, 1).reshape(2 * chips * capacity, width)
    slot_logits = jnp.dot(batch, full_router, preferred_element_type=jnp.float32)
    slot_gate = pick(jax.nn.softmax(slot_logits, axis=-1), core, 1)
    out_grad = (slot_gate[:, None] * up_slots.astype(jnp.float32)).astype(low)
    before = jnp.dot(batch, in_strip, preferred_element_type=jnp.float32)
    active_wide, pull = jax.vjp(gelu_tanh, before)
    active = active_wide.astype(low)
    returned = jnp.dot(active, out_strip, preferred_element_type=jnp.float32)
    active_grad = jnp.einsum("cd,fd->cf", out_grad, out_strip, preferred_element_type=jnp.float32)
    before_grad = pull(active_grad)[0].astype(low)
    batch_grad = jnp.einsum("cf,df->cd", before_grad, in_strip, preferred_element_type=jnp.float32)
    partial = jnp.concatenate([returned.astype(low), batch_grad.astype(low)], axis=1)
    summed = scatter_chips(partial.reshape(chips, 2 * capacity, 2 * width), size, 2)
    back_mine = summed[:capacity]
    back_other = swap(summed[capacity:], size)
    back = pair_order(core, back_mine, back_other, 0)

    in_grad = jnp.einsum("cd,cf->df", batch, before_grad, preferred_element_type=jnp.float32)
    outer_grad = jnp.einsum("cf,cd->fd", active, out_grad, preferred_element_type=jnp.float32)
    in_grad = lax.all_to_all(
        in_grad.astype(low).reshape(chips, 2 * rows, strip),
        "shard",
        0,
        0,
        axis_index_groups=groups,
        tiled=True,
    )
    in_grad = rep_sum(in_grad, reps)
    in_grad = jnp.transpose(in_grad, (1, 0, 2)).reshape(2, rows, hidden_units)
    grad_mine = pick(in_grad, core)
    grad_other = swap(pick(in_grad, 1 - core).astype(low), size).astype(jnp.float32)
    expert_in_grad = pair_order(core, grad_mine[None], grad_other[None], 0)
    outer_grad = rep_sum(outer_grad.astype(low), reps).reshape(2, strip // 2, width)
    outer_mine = pick(outer_grad, core)
    outer_other = swap(pick(outer_grad, 1 - core).astype(low), size).astype(jnp.float32)
    expert_out_grad = pair_order(core, outer_mine[None], outer_other[None], 0)

    gathered_all = jnp.einsum("st,sd->td", dispatch, back, preferred_element_type=jnp.float32)
    gathered = gathered_all[:, :width]
    ffn_normed_grad = gathered_all[:, width:]
    layer_out = (hidden + gate[:, None] * gathered).astype(low)
    gate_grad = jnp.sum(upstream * gathered, axis=1)
    prob_grad = jnp.where(picked, gate_grad[:, None], 0.0)
    logit_grad = gate_probs * (prob_grad - jnp.sum(gate_probs * prob_grad, axis=1, keepdims=True))
    normed_wide = normed_ffn.astype(jnp.float32)
    router_grad = jnp.einsum("td,te->de", normed_wide, logit_grad, precision=highest)
    ffn_normed_grad = ffn_normed_grad + jnp.einsum(
        "te,de->td", logit_grad, full_router.astype(jnp.float32), precision=highest
    )
    norm_pull = jax.vjp(rms_norm, hidden, gain_ffn)[1]
    hidden_from_norm, gain_ffn_grad = norm_pull(ffn_normed_grad)
    hidden_grad = upstream + hidden_from_norm
    attn_grad = hidden_grad.astype(low)
    attn_out_grad = jnp.einsum("td,te->de", context, attn_grad, preferred_element_type=jnp.float32)
    context_grad = jnp.einsum("te,de->td", attn_grad, full_out, preferred_element_type=jnp.float32)
    context_grad = context_grad.astype(low)
    projected_grad, diagonal = attend_back(projected, probs, context_grad)
    offset_grad = diagonal[:, : 2 * length - 1][:, ::-1]
    table_grad = jnp.einsum(
        "ho,ob->bh", offset_grad, offset_onehot[: 2 * length - 1], precision=highest
    )
    attn_in_grad = jnp.einsum(
        "td,kte->kde", normed, projected_grad, preferred_element_type=jnp.float32
    )
    normed_grad = jnp.einsum(
        "kte,kde->td", projected_grad, full_in, preferred_element_type=jnp.float32
    )
    input_pull = jax.vjp(rms_norm, inputs, gain_attn)[1]
    input_from_norm, gain_attn_grad = input_pull(normed_grad)
    input_grad = hidden_grad + input_from_norm
    gains_grad = jnp.stack([gain_attn_grad, gain_ffn_grad])

    def spread(values):
        flat = values.reshape(size, 1, -1)
        return jnp.pad(flat, ((0, 0), (0, 0), (0, width - flat.shape[2])))

    small = jnp.concatenate(
        [
            spread(jnp.transpose(gains_grad.reshape(2, size, rows), (1, 0, 2))),
            spread(router_grad),
            spread(table_grad),
            jnp.zeros((size, extra, width), jnp.float32),
        ],
        axis=1,
    ).astype(low)
    attn_in_grad = attn_in_grad.astype(low).reshape(3, size, rows, width)
    grads = jnp.concatenate(
        [
            attn_in_grad[0],
            attn_in_grad[1],
            attn_in_grad[2],
            attn_out_grad.astype(low).reshape(size, rows, width),
            small,
        ],
        axis=1,
    ).reshape(chips, 2, depth, width)
    kept = pick(grads, core, 1)
    given = swap(pick(grads, 1 - core, 1), size)
    kept = (kept.astype(jnp.float32) + given.astype(jnp.float32)).astype(low)
    mine = scatter_chips(kept, size, 3)
    mine = rep_sum(mine, reps)
    in_shard = mine[: 3 * rows].reshape(3, rows, width)
    out_shard = mine[3 * rows : 4 * rows]
    gains_shard = mine[spot, : 2 * rows].reshape(2, rows)
    router_shard = mine[spot + 1, : experts * rows].reshape(rows, experts)
    table_shard = mine[spot + 2, : table_rows * heads].reshape(table_rows, heads)
    return (
        layer_out,
        input_grad,
        in_shard,
        out_shard,
        gains_shard,
        router_shard,
        table_shard,
        expert_in_grad,
        expert_out_grad,
    )


def solution(mesh):
    placed = (
        P(("rep", "shard"), None),
        P(("rep", "shard"), None),
        P(("rep", "shard"), None),
        P(("rep", "shard"), None),
        P(),
        P(None, "shard", None),
        P("shard", None),
        P(None, "shard"),
        P("shard", None),
        P("shard", None),
        P(None, "shard", None),
        P(None, "shard", None),
    )
    return jax.shard_map(
        functools.partial(shards, mesh.shape["shard"], mesh.shape["rep"]),
        mesh=mesh,
        in_specs=placed,
        out_specs=(
            P(("rep", "shard"), None),
            P(("rep", "shard"), None),
            P(None, "shard", None),
            P("shard", None),
            P(None, "shard"),
            P("shard", None),
            P("shard", None),
            P(None, "shard", None),
            P(None, "shard", None),
        ),
        check_vma=False,
    )
```

profile of v0, /device:TPU:0, one launch (start us, length us, event | category | flops | bytes accessed | tf_op | source)
XLA Modules:
  0.0 385.4 jit_solution(10492342199056981618)
XLA Ops:
  15.5 43.2 %shard_map.187 = bf16[8,208,768]{2,1,0:T(8,128)(2,1)S(1)} custom-call(bf16[208,768]{1,0:T(8,128)(2,1)S(1)} %pad.36.x_ref), custom_call_target="tpu_custom_call" | custom-call | tf_op jit(solution)/shard_map/pallas_call | solution.py:143
  66.8 10.1 %all-to-all-start = ((bf16[8,96,384]{2,1,0:T(8,128)(2,1)}), bf16[8,96,384]{2,1,0:T(8,128)(2,1)}, u32[]{:S(2)}, u32[]{:S(2)}) async-start(bf16[8,96,384]{2,1,0:T(8,128)(2,1)} %copy.96), calls=%async_computation | async-start | bytes 1179648 | tf_op jit(solution)/shard_map/all_to_all | solution.py:420
  81.4 2.6 copy.91
  86.5 2.4 slice.93
  88.9 2.2 slice.91
  96.1 4.3 %shard_map.188 = (bf16[128,768]{1,0:T(8,128)(2,1)S(1)}, f32[12,128,128]{2,1,0:T(8,128)S(1)}) custom-call(bf16[3,128,768]{2,1,0:T(8,128)(2,1)S(1)} %fusion.8.p_ref, f32[12,256]{1,0:T(8,128)S(1)} %fusion.36.bias_ref, s32[128,1]{1,0:T(8,128)S(1)} %copy-done.1, s32[1,128]{1,0:T(1,128)S(1)} %bitcast.119), custom_call_target="tpu_custom_call" | custom-call | tf_op jit(solution)/shard_map/pallas_call | solution.py:280
  102.9 46.8 %shard_map.189 = bf16[8,160,768]{2,1,0:T(8,128)(2,1)S(1)} custom-call(bf16[160,768]{1,0:T(8,128)(2,1)S(1)} %pad_maximum_fusion.8.x_ref), custom_call_target="tpu_custom_call" | custom-call | tf_op jit(solution)/shard_map/pallas_call | solution.py:143
  151.0 2.3 fusion.58
  154.6 2.7 convolution_convert_fusion.1
  157.3 4.6 %fusion.7 = bf16[1280,384]{1,0:T(8,128)(2,1)S(1)} fusion(f32[1280,384]{1,0:T(8,128)} %copy-done.45, bf16[1280,768]{1,0:T(8,128)(2,1)} %all-gather.2.cloned.1.call-done, f32[1280]{0:T(1024)} %divide_reduce_fusion, bf16[192,768]{1,0:T(8,128)(2,1)} %get-tuple-element.87, bf16[192,768]{1,0:T(8,128)(2,1)} %get-tuple-element.86), kind=kOutput, calls=%fused_computation.19 | convolution fusion | flops 768933888 | bytes 5510144 | tf_op jit(solution)/shard_map/cd,fd->cf/dot_general | solution.py:463
  163.9 3.7 convolution_convert_fusion
  167.7 9.4 %all-to-all-start.1 = ((bf16[8,96,384]{2,1,0:T(8,128)(2,1)}), bf16[8,96,384]{2,1,0:T(8,128)(2,1)}, u32[]{:S(2)}, u32[]{:S(2)}) async-start(bf16[8,96,384]{2,1,0:T(8,128)(2,1)} %bitcast.135), calls=%async_computation.1 | async-start | bytes 1179648 | tf_op jit(solution)/shard_map/all_to_all | solution.py:474
  177.1 3.7 pad_maximum_fusion.1
  180.7 6.3 %copy.97 = bf16[1280,1536]{1,0:T(8,128)(2,1)} copy(bf16[1280,1536]{0,1:T(8,128)(2,1)} %pad_maximum_fusion.1) | data formatting | bytes 7864320 | tf_op jit(solution)/shard_map/concatenate | solution.py:466
  189.1 57.3 %shard_map.190 = bf16[160,1536]{1,0:T(8,128)(2,1)S(1)} custom-call(bf16[8,160,1536]{2,1,0:T(8,128)(2,1)S(1)} %bitcast.114), custom_call_target="tpu_custom_call" | custom-call | tf_op jit(solution)/shard_map/pallas_call | solution.py:231
  246.5 2.2 convolution_convert_fusion.4
  255.8 4.6 %shard_map.191 = (bf16[3,128,768]{2,1,0:T(8,128)(2,1)S(1)}, f32[12,256]{1,0:T(8,128)S(1)}) custom-call(bf16[3,128,768]{2,1,0:T(8,128)(2,1)S(1)} %fusion.8.p_ref, f32[12,128,128]{2,1,0:T(8,128)S(1)} %get-tuple-element.14.probs_ref, bf16[128,768]{1,0:T(8,128)(2,1)S(1)} %convolution_convert_fusion.8.g_ref), custom_call_target="tpu_custom_call" | custom-call | tf_op jit(solution)/shard_map/pallas_call | solution.py:330
  260.5 4.1 %fusion.18 = (bf16[768]{0:T(1024)(128)(2,1)S(1)}, f32[128]{0:T(128)S(1)}, f32[128,768]{1,0:T(8,128)}) fusion(bf16[128,768]{1,0:T(8,128)(2,1)S(1)} %copy-done.7, f32[128]{0:T(128)S(1)} %copy-done.28, f32[768]{0:T(1024)S(1)} %reshape.228, bf16[3,128,768]{2,1,0:T(8,128)(2,1)S(1)} %get-tuple-element.15, bf16[3,768,768]{2,1,0:T(8,128)(2,1)} %bitcast.121), kind=kOutput, calls=%fused_computation.64 | convolution fusion | flops 453672064 | bytes 4724224 | tf_op jit(solution)/shard_map/kte,kde->td/dot_general | solution.py:519
  270.7 28.8 %concatenate.65 = bf16[8,2,208,768]{3,2,0,1:T(8,128)(2,1)} concatenate(bf16[8,2,48,768]{3,2,0,1:T(8,128)(2,1)} %copy.102, bf16[8,2,48,768]{3,2,0,1:T(8,128)(2,1)} %copy.103, bf16[8,2,48,768]{3,2,0,1:T(8,128)(2,1)S(1)} %copy.104, bf16[8,2,48,768]{3,2,0,1:T(8,128)(2,1)S(1)} %copy.105, bf16[8,2,1,768]{3,2,0,1:T(2,128)(2,1)S(1)} %copy.106, bf16[8,2,1,768]{3,2,0,1:T(2,128)(2,1)S(1)} %copy-done.23, ...), dimensions={2} | concatenate | bytes 10223616 | tf_op jit(solution)/shard_map/concatenate | solution.py:541
  299.5 3.5 dynamic-slice_bitcast_fusion
  307.0 12.0 %collective-permute-done.8 = bf16[8,96,384]{2,1,0:T(8,128)(2,1)S(1)} collective-permute-done((bf16[8,96,384]{2,1,0:T(8,128)(2,1)}, bf16[8,96,384]{2,1,0:T(8,128)(2,1)S(1)}, u32[]{:S(2)}, u32[]{:S(2)}) %collective-permute-start.8) | collective-permute-done | bytes 589856 | tf_op jit(solution)/shard_map/ppermute | solution.py:37
  323.5 3.1 fusion.p_ref
  326.7 39.9 %shard_map.192 = bf16[208,768]{1,0:T(8,128)(2,1)S(1)} custom-call(bf16[8,208,768]{2,1,0:T(8,128)(2,1)S(1)} %fusion.p_ref), custom_call_target="tpu_custom_call" | custom-call | tf_op jit(solution)/shard_map/pallas_call | solution.py:231
  368.3 6.7 %collective-permute-done.7 = bf16[208,768]{1,0:T(8,128)(2,1)S(1)} collective-permute-done((bf16[208,768]{1,0:T(8,128)(2,1)S(1)}, bf16[208,768]{1,0:T(8,128)(2,1)S(1)}, u32[]{:S(2)}, u32[]{:S(2)}) %collective-permute-start.7) | collective-permute-done | bytes 319520 | tf_op jit(solution)/shard_map/ppermute | solution.py:37
  (236 shorter events, 64.1 us)
Async XLA Ops:
  7.2 150.1 %all-gather.2.cloned.1.call-start = ((), (), s32[]{:S(2)}) async-start(), calls=%async_computation.2 | async-start | bytes 2211840 | tf_op jit(solution)/shard_map/all_gather | solution.py:385
  10.6 51.9 %collective-permute-start.4 = (bf16[80,768]{1,0:T(8,128)(2,1)}, bf16[80,768]{1,0:T(8,128)(2,1)}, u32[]{:S(2)}, u32[]{:S(2)}) collective-permute-start(bf16[80,768]{1,0:T(8,128)(2,1)} %get-tuple-element.95), channel_id=1, source_target_pairs={{0,1},{1,0},{2,3},{3,2},{4,5},{5,4},{6,7},{7,6},{8,9},{9,8},{10,11... | collective-permute-start | bytes 368648 | tf_op jit(solution)/shard_map/ppermute | solution.py:26
  13.5 45.3 %copy-start.20 = (bf16[2,192,768]{2,1,0:T(8,128)(2,1)S(1)}, bf16[2,192,768]{2,1,0:T(8,128)(2,1)}, u32[]{:S(2)}) copy-start(bf16[2,192,768]{2,1,0:T(8,128)(2,1)} %param.23) | copy-start | bytes 1769476
  15.5 44.6 %copy-start.19 = (bf16[2,48,3072]{2,1,0:T(8,128)(2,1)S(1)}, bf16[2,48,3072]{2,1,0:T(8,128)(2,1)}, u32[]{:S(2)}) copy-start(bf16[2,48,3072]{2,1,0:T(8,128)(2,1)} %param.22) | copy-start | bytes 1769476
  15.5 44.7 %copy-start.44 = (s32[1,3]{1,0:T(1,128)S(1)}, s32[1,3]{1,0:T(1,128)}, u32[]{:S(2)}) copy-start(s32[1,3]{1,0:T(1,128)} %param.14) | copy-start | bytes 40
  15.5 45.6 %copy-start.38 = (s32[255]{0:T(256)S(1)}, s32[255]{0:T(256)}, u32[]{:S(2)}) copy-start(s32[255]{0:T(256)} %param.16) | copy-start | bytes 3064
  15.5 45.6 %copy-start.5 = (bf16[128,768]{1,0:T(8,128)(2,1)S(1)}, bf16[128,768]{1,0:T(8,128)(2,1)}, u32[]{:S(2)}) copy-start(bf16[128,768]{1,0:T(8,128)(2,1)} %param.12) | copy-start | bytes 589828
  58.7 20.1 %collective-permute-start = (bf16[8,208,768]{2,1,0:T(8,128)(2,1)S(1)}, bf16[8,208,768]{2,1,0:T(8,128)(2,1)}, u32[]{:S(2)}, u32[]{:S(2)}) collective-permute-start(bf16[8,208,768]{2,1,0:T(8,128)(2,1)S(1)} %shard_map.187), channel_id=1, source_target_pairs={{0,1},{1,0},{2,3},{3,2},{4,5},{5,4},{6,7},{7,6},{8,9},{9,8},{10,11... | collective-permute-start | bytes 7667720 | tf_op jit(solution)/shard_map/ppermute | solution.py:26
  59.6 17.3 %collective-permute-start.3 = (bf16[192,768]{1,0:T(8,128)(2,1)}, bf16[192,768]{1,0:T(8,128)(2,1)}, u32[]{:S(2)}, u32[]{:S(2)}) collective-permute-start(bf16[192,768]{1,0:T(8,128)(2,1)} %dynamic-slice_bitcast_fusion.1), channel_id=1, source_target_pairs={{0,1},{1,0},{2,3},{3,2},{4,5},{5,4},{6,7},{7,6},{8,9},{9,8},{10,11... | collective-permute-start | bytes 884744 | tf_op jit(solution)/shard_map/ppermute | solution.py:26
  60.1 4.5 %collective-permute-start.2 = (bf16[48,3072]{1,0:T(8,128)(2,1)S(1)}, bf16[48,3072]{1,0:T(8,128)(2,1)}, u32[]{:S(2)}, u32[]{:S(2)}) collective-permute-start(bf16[48,3072]{1,0:T(8,128)(2,1)S(1)} %dynamic-slice_bitcast_fusion.2), channel_id=1, source_target_pairs={{0,1},{1,0},{2,3},{3,2},{4,5},{5,4},{6,7},{7,6},{8,9},{9,8},{10,11... | collective-permute-start | bytes 884744 | tf_op jit(solution)/shard_map/ppermute | solution.py:26
  66.8 84.3 %all-to-all-start = ((bf16[8,96,384]{2,1,0:T(8,128)(2,1)}), bf16[8,96,384]{2,1,0:T(8,128)(2,1)}, u32[]{:S(2)}, u32[]{:S(2)}) async-start(bf16[8,96,384]{2,1,0:T(8,128)(2,1)} %copy.96), calls=%async_computation | async-start | bytes 1179648 | tf_op jit(solution)/shard_map/all_to_all | solution.py:420
  101.5 1.3 collective-permute-start.1
  163.9 13.1 %copy-start.16 = (bf16[1280,768]{0,1:T(8,128)(2,1)S(1)}, bf16[1280,768]{0,1:T(8,128)(2,1)}, u32[]{:S(2)}) copy-start(bf16[1280,768]{0,1:T(8,128)(2,1)} %convolution_convert_fusion.1) | copy-start | bytes 5898244
  167.7 135.5 %all-to-all-start.1 = ((bf16[8,96,384]{2,1,0:T(8,128)(2,1)}), bf16[8,96,384]{2,1,0:T(8,128)(2,1)}, u32[]{:S(2)}, u32[]{:S(2)}) async-start(bf16[8,96,384]{2,1,0:T(8,128)(2,1)} %bitcast.135), calls=%async_computation.1 | async-start | bytes 1179648 | tf_op jit(solution)/shard_map/all_to_all | solution.py:474
  189.1 57.4 %copy-start.26 = (f32[1280]{0:T(1024)S(1)}, f32[1280]{0:T(1024)}, u32[]{:S(2)}) copy-start(f32[1280]{0:T(1024)} %divide_reduce_fusion) | copy-start | bytes 15364
  189.1 57.4 %copy-start.43 = (bf16[1280,768]{1,0:T(8,128)(2,1)S(1)}, bf16[1280,768]{1,0:T(8,128)(2,1)}, u32[]{:S(2)}) copy-start(bf16[1280,768]{1,0:T(8,128)(2,1)} %all-gather.2.cloned.1.call-done) | copy-start | bytes 5898244
  189.1 57.4 %copy-start.46 = (f32[1280,384]{1,0:T(8,128)S(1)}, f32[1280,384]{1,0:T(8,128)}, u32[]{:S(2)}) copy-start(f32[1280,384]{1,0:T(8,128)} %copy-done.45) | copy-start | bytes 5898244
  246.4 3.9 %collective-permute-start.5 = (bf16[80,1536]{1,0:T(8,128)(2,1)S(1)}, bf16[80,1536]{1,0:T(8,128)(2,1)S(1)}, u32[]{:S(2)}, u32[]{:S(2)}) collective-permute-start(bf16[80,1536]{1,0:T(8,128)(2,1)S(1)} %slice.76), channel_id=1, source_target_pairs={{0,1},{1,0},{2,3},{3,2},{4,5},{5,4},{6,7},{7,6},{8,9},{9,8},{10,11... | collective-permute-start | bytes 737288 | tf_op jit(solution)/shard_map/ppermute | solution.py:26
  248.8 56.1 %collective-permute-start.10 = (bf16[384,768]{1,0:T(8,128)(2,1)}, bf16[384,768]{1,0:T(8,128)(2,1)}, u32[]{:S(2)}, u32[]{:S(2)}) collective-permute-start(bf16[384,768]{1,0:T(8,128)(2,1)} %convolution_convert_fusion.4), channel_id=1, source_target_pairs={{0,16},{16,0},{1,17},{17,1},{2,18},{18,2},{3,19},{19,3},{4,20},{20... | collective-permute-start | bytes 1769480 | tf_op jit(solution)/shard_map/ppermute | solution.py:37
  303.0 20.5 %collective-permute-start.6 = (bf16[8,208,768]{2,1,0:T(8,128)(2,1)}, bf16[8,208,768]{2,1,0:T(8,128)(2,1)}, u32[]{:S(2)}, u32[]{:S(2)}) collective-permute-start(bf16[8,208,768]{2,1,0:T(8,128)(2,1)} %dynamic-slice_bitcast_fusion), channel_id=1, source_target_pairs={{0,1},{1,0},{2,3},{3,2},{4,5},{5,4},{6,7},{7,6},{8,9},{9,8},{10,11... | collective-permute-start | bytes 7667720 | tf_op jit(solution)/shard_map/ppermute | solution.py:26
  303.2 15.8 %collective-permute-start.8 = (bf16[8,96,384]{2,1,0:T(8,128)(2,1)}, bf16[8,96,384]{2,1,0:T(8,128)(2,1)S(1)}, u32[]{:S(2)}, u32[]{:S(2)}) collective-permute-start(bf16[8,96,384]{2,1,0:T(8,128)(2,1)} %all-to-all-done.1), channel_id=1, source_target_pairs={{0,16},{16,0},{1,17},{17,1},{2,18},{18,2},{3,19},{19,3},{4,20},{20... | collective-permute-start | bytes 1769480 | tf_op jit(solution)/shard_map/ppermute | solution.py:37
  307.0 14.2 %collective-permute-start.11 = (bf16[192,768]{1,0:T(8,128)(2,1)}, bf16[192,768]{1,0:T(8,128)(2,1)}, u32[]{:S(2)}, u32[]{:S(2)}) collective-permute-start(bf16[192,768]{1,0:T(8,128)(2,1)} %fusion.24), channel_id=1, source_target_pairs={{0,1},{1,0},{2,3},{3,2},{4,5},{5,4},{6,7},{7,6},{8,9},{9,8},{10,11... | collective-permute-start | bytes 884744 | tf_op jit(solution)/shard_map/ppermute | solution.py:26
  321.2 2.2 collective-permute-start.9
  366.5 8.4 %collective-permute-start.7 = (bf16[208,768]{1,0:T(8,128)(2,1)S(1)}, bf16[208,768]{1,0:T(8,128)(2,1)S(1)}, u32[]{:S(2)}, u32[]{:S(2)}) collective-permute-start(bf16[208,768]{1,0:T(8,128)(2,1)S(1)} %shard_map.192), channel_id=1, source_target_pairs={{0,16},{16,0},{1,17},{17,1},{2,18},{18,2},{3,19},{19,3},{4,20},{20... | collective-permute-start | bytes 958472 | tf_op jit(solution)/shard_map/ppermute | solution.py:37
  (38 other events, 113.5 us)
Sparse Core Ops, SparseCore 0:
  64.3 75.8 all-gather.1
where the time goes:
time: 388 us; the launch traced here: 385 us
  Pallas kernels  196 us (51%)
  local copies, waits for them, and re-layouts  74.1 us (19%)
  matrix products  30.5 us (8%)
  other arithmetic  26.2 us (7%)
  starting transfers between devices  23.9 us (6%)
  waiting for transfers between devices  19.7 us (5%)
  between operations  14.9 us (4%)
    pallas_call x2, Pallas kernels, scatter_chips(): pl.pallas_call(functools.partial(scatter_kernel, size), out_shape=jax.Sha...  97.1 us
    pallas_call x2, Pallas kernels, gather_chips(): pl.pallas_call(functools.partial(gather_kernel, size), out_shape=jax.Shap...  90 us
    concatenate x5, local copies, waits for them, and re-layouts, shards(): jnp.concatenate([attn_in_grad[0], attn_in_grad[1], attn_in_grad[2], attn_...  32.4 us
    ppermute x3, waiting for transfers between devices, rep_sum(): other = lax.ppermute(array, 'rep', [(0, 1), (1, 0)])  18.7 us
    all_to_all x1, starting transfers between devices, shards(): lax.all_to_all(in_rows, 'shard', 0, 0, axis_index_groups=groups, tiled=True)  10.1 us
    all_to_all x1, starting transfers between devices, shards(): lax.all_to_all(in_grad.astype(low).reshape(chips, 2 * rows, strip), 'shar...  9.4 us
  transfers between devices with their start and end apart: 15, of which 4 were waited for; matrix products, arithmetic and copies ran while one was open for 27% of the time, Pallas kernels for 41%

commit v1 on v0

v1 whole, which is shorter than its diff:
```python
import functools

import jax
import jax.numpy as jnp
from jax import lax
from jax.experimental import pallas as pl
from jax.experimental.pallas import tpu as pltpu
from jax.sharding import PartitionSpec as P

EPSILON = 1e-06
SMALL = 16
LOW = jnp.bfloat16
WIDE = jnp.float32
NT = (((1,), (1,)), ((), ()))
TN = (((0,), (0,)), ((), ()))
MESH = pl.DeviceIdType.MESH
VMEM = pl.BlockSpec(memory_space=pltpu.VMEM)
SMEM = pl.BlockSpec(memory_space=pltpu.SMEM)
DMA = pltpu.SemaphoreType.DMA


def grid_of(size):
    chips = size // 2
    outer = 4 if chips % 4 == 0 else 1
    return outer, chips // outer


class Place:
    def __init__(self, size):
        self.size = size
        self.outer, self.inner = grid_of(size)
        self.chips = size // 2
        me = lax.axis_index("shard")
        self.core = lax.rem(me, 2)
        self.chip = lax.div(me, 2)
        self.z = lax.div(self.chip, self.inner)
        self.y = lax.rem(self.chip, self.inner)

    def at(self, dz, dy):
        far = lax.rem(self.z + dz + self.outer, self.outer)
        near = lax.rem(self.y + dy + self.inner, self.inner)
        return far * self.inner + near

    def device(self, chip):
        return {"shard": chip * 2 + self.core}

    def partner(self):
        return {"shard": self.chip * 2 + 1 - self.core}

    def step(self, d, e):
        if d == 0:
            return e
        if e == 0:
            return self.inner + d - 1
        return self.inner + self.outer - 1 + (d - 1) * (self.inner - 1) + e - 1

    def pairs(self):
        order = [(0, e) for e in range(self.inner)]
        order += [(d, 0) for d in range(1, self.outer)]
        order += [(d, e) for d in range(1, self.outer) for e in range(1, self.inner)]
        return order

    def pair(self, i):
        inner, outer = self.inner, self.outer
        j = i - (inner + outer - 1)
        side = max(inner - 1, 1)
        d = jnp.where(i < inner, 0, jnp.where(j < 0, i - inner + 1, 1 + lax.div(j, side)))
        e = jnp.where(i < inner, i, jnp.where(j < 0, 0, 1 + lax.rem(j, side)))
        return d, e

    def greet(self, chips, reps):
        barrier = pltpu.get_barrier_semaphore()
        count = 0

        def signal(target):
            pl.semaphore_signal(barrier, inc=1, device_id=target, device_id_type=MESH)

        for dz, dy in self.pairs()[1:]:
            if chips or dz == 0 or dy == 0:
                signal(self.device(self.at(dz, dy)))
                count += 1
        signal(self.partner())
        count += 1
        for f in range(1, reps):
            signal({"rep": lax.rem(lax.axis_index("rep") + f, reps)})
            count += 1
        pl.semaphore_wait(barrier, count)


def remote(src, dst, send_sem, recv_sem, target):
    return pltpu.make_async_remote_copy(
        src_ref=src,
        dst_ref=dst,
        send_sem=send_sem,
        recv_sem=recv_sem,
        device_id=target,
        device_id_type=MESH,
    )


def dot(a, b, dims=None):
    if dims is None:
        return jnp.dot(a, b, preferred_element_type=WIDE)
    return lax.dot_general(a, b, dims, preferred_element_type=WIDE)


def joined(ref, first, rows, pad):
    chips, _, _, width = ref.shape
    if rows == pad:
        return ref[:, :, first : first + rows, :].reshape(chips * 2 * rows, width)
    parts = [ref[j // 2, j % 2, first : first + rows, :].astype(WIDE) for j in range(chips * 2)]
    return jnp.concatenate(parts, axis=0).astype(LOW)


def split(ref, first, rows, pad, values):
    chips, _, _, width = ref.shape
    if rows == pad:
        ref[:, :, first : first + rows, :] = values.reshape(chips, 2, rows, width).astype(LOW)
        return
    for j in range(chips * 2):
        ref[j // 2, j % 2, first : first + rows, :] = values[j * rows : (j + 1) * rows].astype(LOW)


def rms_scale(values):
    return lax.rsqrt(jnp.mean(values * values, axis=1, keepdims=True) + EPSILON)


def gate_of(logits, route):
    first, second = logits[:, 2:3], logits[:, 3:4]
    top = jnp.maximum(first, second)
    first, second = jnp.exp(first - top), jnp.exp(second - top)
    total = first + second
    first, second = first / total, second / total
    return first, second, jnp.where(route > 0.5, second, first)


def gather_start(place, own, slots, send_sem, recv_sem):
    for d, e in place.pairs()[1:]:
        if d == 0 or e == 0:
            i = place.step(d, e)
            target = place.device(place.at(d, e))
            remote(own, slots.at[place.chip], send_sem.at[i], recv_sem.at[i], target).start()


def gather_arrive(place, i, own, slots, send_sem, recv_sem):
    d, e = place.pair(i)
    source = place.at(-d, -e)
    remote(own, slots.at[source], send_sem.at[i], recv_sem.at[i], place.device(source)).wait_recv()

    @pl.when(jnp.logical_and(d > 0, e == 0))
    def _():
        for side in range(1, place.inner):
            j = place.inner + place.outer - 1 + (d - 1) * (place.inner - 1) + side - 1
            target = place.device(place.at(0, side))
            remote(
                slots.at[source], slots.at[source], send_sem.at[j], recv_sem.at[j], target
            ).start()

    return source


def front_kernel(
    size,
    heads,
    tok_ref,
    in_ref,
    out_ref,
    small_ref,
    strip_ref,
    half_ref,
    bucket_ref,
    length_ref,
    whole_ref,
    w1_ref,
    w2_ref,
    normed_ref,
    proj_ref,
    probs_ref,
    context_ref,
    hidden_ref,
    ffn_ref,
    sum_ref,
    route_ref,
    g_send,
    g_recv,
    c_send,
    c_recv,
    s_send,
    s_recv,
    d_send,
    d_recv,
    h_send,
    h_recv,
    own_sem,
):
    place = Place(size)
    chips = place.chips
    core, chip = place.core, place.chip
    length, width = tok_ref.shape
    rows = out_ref.shape[0]
    pad = w1_ref.shape[2]
    head_size = width // heads
    mine = whole_ref.at[chip, core]
    for k in range(3):
        whole_ref[chip, core, k * pad : k * pad + rows, :] = in_ref[k]
    whole_ref[chip, core, 3 * pad : 3 * pad + rows, :] = out_ref[...]
    whole_ref[chip, core, 4 * pad : 4 * pad + SMALL, :] = small_ref[...]
    place.greet(True, 1)
    partner = place.partner()
    slots = whole_ref.at[:, core]
    gather_start(place, mine, slots, g_send, g_recv)

    def dup(i, source):
        return remote(
            whole_ref.at[source, core],
            whole_ref.at[source, core],
            c_send.at[i],
            c_recv.at[i],
            partner,
        )

    dup(0, chip).start()
    local = [
        pltpu.make_async_copy(strip_ref.at[chip], w1_ref.at[chip, core], own_sem.at[0]),
        pltpu.make_async_copy(half_ref, w2_ref.at[:, core], own_sem.at[1]),
    ]
    for copy in local:
        copy.start()
    halves = remote(half_ref, w2_ref.at[:, core], h_send, h_recv, partner)
    halves.start()

    def arrive(i, carry):
        source = gather_arrive(place, i, mine, slots, g_send, g_recv)
        dup(i, source).start()
        return carry

    lax.fori_loop(1, place.inner + place.outer - 1, arrive, 0)
    strips = []
    for i, (d, e) in enumerate(place.pairs()):
        if i > 0:
            target = place.at(d, e)
            copy = remote(
                strip_ref.at[target],
                w1_ref.at[chip, core],
                s_send.at[i],
                s_recv.at[i],
                place.device(target),
            )
            copy.start()
            strips.append(copy)
    lax.fori_loop(place.inner + place.outer - 1, chips, arrive, 0)

    def other(i, carry):
        d, e = place.pair(i)
        source = place.at(-d, -e)
        remote(
            whole_ref.at[source, core],
            whole_ref.at[source, 1 - core],
            c_send.at[i],
            c_recv.at[i],
            partner,
        ).wait_recv()
        return carry

    lax.fori_loop(0, chips, other, 0)

    total = jnp.zeros((SMALL, width), WIDE)
    for j in range(size):
        total = total + whole_ref[j // 2, j % 2, 4 * pad : 4 * pad + SMALL, :].astype(WIDE)
    sum_ref[...] = total
    lines = [
        whole_ref[k, core, 4 * pad : 4 * pad + SMALL, length : 2 * length].astype(WIDE)[4:5]
        for k in range(chips)
    ]
    lines.append(jnp.zeros((length - chips, length), WIDE))
    route_ref[...] = jnp.transpose(jnp.concatenate(lines, axis=0))

    inputs = tok_ref[...].astype(WIDE)
    normed = (inputs * rms_scale(inputs) * total[0:1]).astype(LOW)
    normed_ref[...] = normed
    for k in range(3):
        proj_ref[k] = dot(normed, joined(whole_ref, k * pad, rows, pad)).astype(LOW)
    spots = lax.broadcasted_iota(jnp.int32, (length, 2 * length), 0)
    onehot = jnp.where(bucket_ref[...] == spots, 1.0, 0.0).astype(LOW)
    table = total[:, :length].astype(LOW)
    bias = dot(table, onehot)
    down = lax.broadcasted_iota(jnp.int32, (length, length), 0)
    across = lax.broadcasted_iota(jnp.int32, (length, length), 1)
    part_q = jnp.zeros((length, length), jnp.int32)
    part_k = jnp.zeros((length, length), jnp.int32)
    end = jnp.int32(0)
    for s in range(length_ref.shape[1]):
        end = end + length_ref[0, s]
        part_q = part_q + jnp.where(down >= end, 1, 0)
        part_k = part_k + jnp.where(across >= end, 1, 0)
    allowed = part_q == part_k
    parts = []
    for h in range(heads):
        at = slice(h * head_size, (h + 1) * head_size)
        raw = dot(proj_ref[0, :, at], proj_ref[1, :, at], NT)
        spread = jnp.broadcast_to(bias[4 + h : 5 + h, :], (length, 2 * length))
        skewed = pltpu.roll(spread, length + 1, 1, stride=1, stride_axis=0)
        scores = jnp.where(allowed, raw * 0.125 + skewed[:, :length], -1e30)
        expo = jnp.exp(scores - jnp.max(scores, axis=1, keepdims=True))
        probs = expo / jnp.sum(expo, axis=1, keepdims=True)
        probs_ref[h] = probs
        parts.append(dot(probs.astype(LOW), proj_ref[2, :, at]))
    context = jnp.concatenate(parts, axis=1).astype(LOW)
    context_ref[...] = context
    hidden = inputs + dot(context, joined(whole_ref, 3 * pad, rows, pad))
    hidden_ref[...] = hidden
    ffn_ref[...] = (hidden * rms_scale(hidden) * total[1:2]).astype(LOW)

    def pass_on(i, carry):
        d, e = place.pair(i)
        source = place.at(-d, -e)
        block = w1_ref.at[source, core]
        remote(block, block, s_send.at[i], s_recv.at[i], partner).wait_recv()
        remote(block, block, d_send.at[i], d_recv.at[i], partner).start()
        return carry

    local[0].wait()
    remote(w1_ref.at[chip, core], w1_ref.at[chip, core], d_send.at[0], d_recv.at[0], partner).start()
    lax.fori_loop(1, chips, pass_on, 0)

    def last(i, carry):
        d, e = place.pair(i)
        source = place.at(-d, -e)
        block = w1_ref.at[source, 1 - core]
        sent = w1_ref.at[source, core]
        remote(sent, block, d_send.at[i], d_recv.at[i], partner).wait()
        remote(
            whole_ref.at[source, core], whole_ref.at[source, core], c_send.at[i], c_recv.at[i], partner
        ).wait_send()
        return carry

    lax.fori_loop(0, chips, last, 0)

    def sent(i, carry):
        remote(mine, mine, g_send.at[i], g_recv.at[i], partner).wait_send()
        remote(
            strip_ref.at[0], w1_ref.at[chip, core], s_send.at[i], s_recv.at[i], partner
        ).wait_send()
        return carry

    lax.fori_loop(1, chips, sent, 0)
    local[1].wait()
    halves.wait()


def front(size, tokens, attn_in, attn_out, small, strips, halves, buckets, lengths, heads):
    chips = size // 2
    length, width = tokens.shape
    rows = attn_out.shape[0]
    pad = strips.shape[1]
    cols = strips.shape[2]
    depth = 4 * pad + SMALL
    sems = [DMA((chips,))] * 8
    return pl.pallas_call(
        functools.partial(front_kernel, size, heads),
        out_shape=(
            jax.ShapeDtypeStruct((chips, 2, depth, width), LOW),
            jax.ShapeDtypeStruct((chips, 2, pad, cols), LOW),
            jax.ShapeDtypeStruct((2, 2) + halves.shape[1:], LOW),
            jax.ShapeDtypeStruct((length, width), LOW),
            jax.ShapeDtypeStruct((3, length, width), LOW),
            jax.ShapeDtypeStruct((heads, length, length), WIDE),
            jax.ShapeDtypeStruct((length, width), LOW),
            jax.ShapeDtypeStruct((length, width), WIDE),
            jax.ShapeDtypeStruct((length, width), LOW),
            jax.ShapeDtypeStruct((SMALL, width), WIDE),
            jax.ShapeDtypeStruct((length, length), WIDE),
        ),
        in_specs=[VMEM] * 7 + [SMEM],
        out_specs=[VMEM] * 11,
        scratch_shapes=[*sems, DMA, DMA, DMA((2,))],
        compiler_params=pltpu.CompilerParams(
            collective_id=0, has_side_effects=True, vmem_limit_bytes=50 << 20
        ),
    )(tokens, attn_in, attn_out, small, strips, halves, buckets, lengths)


def expert_kernel(
    size,
    reps,
    rows,
    x_ref,
    u_ref,
    w1_ref,
    w2_ref,
    sum_ref,
    route_ref,
    ret_ref,
    back_ref,
    g1_ref,
    g2_ref,
    xs,
    us,
    act,
    slope,
    scaled,
    before_grad,
    part,
    y_buf,
    z_out,
    z_in,
    g1_own,
    g1_got,
    g2_own,
    g2_got,
    g2_all,
    x_send,
    x_recv,
    u_send,
    u_recv,
    y_send,
    y_recv,
    z_send,
    z_recv,
    p_send,
    p_recv,
    r_send,
    r_recv,
    own_sem,
):
    place = Place(size)
    chips, outer, inner = place.chips, place.outer, place.inner
    core, chip = place.core, place.chip
    rep = lax.axis_index("rep")
    length, width = x_ref.shape
    cols = w1_ref.shape[1]
    strip = cols // 2
    pad = g1_own.shape[2]
    place.greet(False, reps)
    partner = place.partner()
    gather_start(place, x_ref, xs, x_send, x_recv)
    own = [
        pltpu.make_async_copy(x_ref, xs.at[chip], own_sem.at[0]),
        pltpu.make_async_copy(u_ref, us.at[chip], own_sem.at[1]),
    ]
    for copy in own:
        copy.start()
    for copy in own:
        copy.wait()
    lane = lax.broadcasted_iota(jnp.int32, (length, length), 1)
    side = lax.broadcasted_iota(jnp.int32, (length, cols), 1) >= strip
    router = sum_ref[...].astype(LOW)

    def route_of(k):
        return jnp.sum(jnp.where(lane == k, route_ref[...], 0.0), axis=1, keepdims=True)

    def y_copy(q, i, d, e):
        k = place.at(-d, -e)
        return remote(
            part.at[q, k],
            y_buf.at[q, i],
            y_send.at[q, i],
            y_recv.at[q, i],
            place.device(place.at(0, -e)),
        )

    def z_copy(q, d):
        return remote(
            z_out.at[q, d - 1],
            z_in.at[q, d - 1],
            z_send.at[q, d - 1],
            z_recv.at[q, d - 1],
            place.device(place.at(-d, 0)),
        )

    def forward(i, carry):
        @pl.when(i > 0)
        def _():
            gather_arrive(place, i, x_ref, xs, x_send, x_recv)

        d, e = place.pair(i)
        k = place.at(-d, -e)
        before = dot(xs[k], w1_ref[...])
        keep = jnp.logical_xor(side, route_of(k) < 0.5)
        square = before * before
        bent = jnp.tanh(0.7978845608 * before * (1.0 + 0.044715 * square))
        half = 0.5 * (1.0 + bent)
        rise = half + 0.5 * before * (1.0 - bent * bent) * 0.7978845608 * (
            1.0 + 0.134145 * square
        )
        active = jnp.where(keep, before * half, 0.0).astype(LOW)
        act[k] = active
        slope[k] = jnp.where(keep, rise, 0.0)
        part[0, k] = dot(active, w2_ref[...]).astype(LOW)

        @pl.when(e > 0)
        def _():
            y_copy(0, i, d, e).start()

        return carry

    lax.fori_loop(0, inner + 1, forward, 0)
    gather_start(place, u_ref, us, u_send, u_recv)
    lax.fori_loop(inner + 1, chips, forward, 0)

    def collect(q, d):
        def add(k, carry):
            at = pl.ds(pl.multiple_of(k * 16, 16), 16)
            value = part[q, place.at(-d, 0), at].astype(WIDE)
            for e in range(1, inner):
                value = value + y_buf[q, place.step(d, e), at].astype(WIDE)
            if d == 0:
                target = ret_ref if q == 0 else back_ref
                target[at] = value
            else:
                z_out[q, d - 1, at] = value.astype(LOW)
            return carry

        for e in range(1, inner):
            y_copy(q, place.step(d, e), d, e).wait_recv()
        lax.fori_loop(0, length // 16, add, 0, unroll=True)
        if d > 0:
            z_copy(q, d).start()

    def backward(i, carry):
        @pl.when(i > 0)
        def _():
            gather_arrive(place, i, u_ref, us, u_send, u_recv)

        d, e = place.pair(i)
        k = place.at(-d, -e)
        gate = gate_of(dot(xs[k], router, NT), route_of(k))[2]
        low = (gate * us[k].astype(WIDE)).astype(LOW)
        scaled[k] = low
        grad = (dot(low, w2_ref[...], NT) * slope[k]).astype(LOW)
        before_grad[k] = grad
        part[1, k] = dot(grad, w1_ref[...], NT).astype(LOW)

        @pl.when(e > 0)
        def _():
            y_copy(1, i, d, e).start()

        return carry

    lax.fori_loop(0, inner + outer - 1, backward, 0)
    for d in range(1, outer):
        collect(0, d)
    lax.fori_loop(inner + outer - 1, chips, backward, 0)
    collect(0, 0)

    def flat(ref):
        return ref[...].reshape(chips * length, ref.shape[2])

    g2 = dot(flat(act), flat(scaled), TN)
    g2_own[...] = g2.astype(LOW).reshape(g2_own.shape)
    g2_swap = remote(g2_own.at[:, 1 - core], g2_got, p_send.at[0], p_recv.at[0], partner)
    g2_swap.start()
    for d in range(1, outer):
        collect(1, d)
    g2_swap.wait()
    g2_all[rep] = (g2_own[:, core].astype(WIDE) + g2_got[...].astype(WIDE)).astype(LOW)
    swaps = []
    for f in range(1, reps):
        swaps.append(
            remote(
                g2_all.at[rep],
                g2_all.at[rep],
                r_send.at[f - 1],
                r_recv.at[f - 1],
                {"rep": lax.rem(rep + f, reps)},
            )
        )
        swaps[-1].start()
    g1 = dot(flat(xs), flat(before_grad), TN)
    split(g1_own, 0, rows, pad, g1)
    g1_swap = remote(g1_own.at[:, 1 - core], g1_got, p_send.at[1], p_recv.at[1], partner)
    g1_swap.start()
    collect(1, 0)

    def finish(q, target):
        for d in range(1, outer):
            z_copy(q, d).wait()

        def add(k, carry):
            at = pl.ds(pl.multiple_of(k * 16, 16), 16)
            value = target[at]
            for d in range(1, outer):
                value = value + z_in[q, d - 1, at].astype(WIDE)
            target[at] = value
            return carry

        lax.fori_loop(0, length // 16, add, 0, unroll=True)

    finish(0, ret_ref)
    g1_swap.wait()
    g1_ref[...] = (g1_own[:, core].astype(WIDE) + g1_got[...].astype(WIDE)).astype(LOW)
    for copy in swaps:
        copy.wait()
    value = g2_all[0].astype(WIDE)
    for r in range(1, reps):
        value = value + g2_all[r].astype(WIDE)
    g2_ref[...] = value
    finish(1, back_ref)

    def sent(i, carry):
        remote(x_ref, xs.at[0], x_send.at[i], x_recv.at[i], partner).wait_send()
        remote(u_ref, us.at[0], u_send.at[i], u_recv.at[i], partner).wait_send()
        d, e = place.pair(i)

        @pl.when(e > 0)
        def _():
            y_copy(0, i, d, e).wait_send()
            y_copy(1, i, d, e).wait_send()

        return carry

    lax.fori_loop(1, chips, sent, 0)


def expert(size, reps, rows, pad, x, u, w1, w2, small, routes):
    chips = size // 2
    outer = grid_of(size)[0]
    steps = max(outer - 1, 1)
    length, width = x.shape
    cols = w1.shape[1]
    half = cols // 4
    block = (chips, length, width)
    wide = (chips, length, cols)
    return pl.pallas_call(
        functools.partial(expert_kernel, size, reps, rows),
        out_shape=(
            jax.ShapeDtypeStruct((length, width), WIDE),
            jax.ShapeDtypeStruct((length, width), WIDE),
            jax.ShapeDtypeStruct((chips, pad, cols), LOW),
            jax.ShapeDtypeStruct((2, half, width), WIDE),
        ),
        in_specs=[VMEM] * 6,
        out_specs=[VMEM] * 4,
        scratch_shapes=[
            pltpu.VMEM(block, LOW),
            pltpu.VMEM(block, LOW),
            pltpu.VMEM(wide, LOW),
            pltpu.VMEM(wide, WIDE),
            pltpu.VMEM(block, LOW),
            pltpu.VMEM(wide, LOW),
            pltpu.VMEM((2,) + block, LOW),
            pltpu.VMEM((2,) + block, LOW),
            pltpu.VMEM((2, steps, length, width), LOW),
            pltpu.VMEM((2, steps, length, width), LOW),
            pltpu.VMEM((chips, 2, pad, cols), LOW),
            pltpu.VMEM((chips, pad, cols), LOW),
            pltpu.VMEM((2, 2, half, width), LOW),
            pltpu.VMEM((2, half, width), LOW),
            pltpu.VMEM((reps, 2, half, width), LOW),
            DMA((chips,)),
            DMA((chips,)),
            DMA((chips,)),
            DMA((chips,)),
            DMA((2, chips)),
            DMA((2, chips)),
            DMA((2, steps)),
            DMA((2, steps)),
            DMA((2,)),
            DMA((2,)),
            DMA((max(reps - 1, 1),)),
            DMA((max(reps - 1, 1),)),
            DMA((2,)),
        ],
        compiler_params=pltpu.CompilerParams(
            collective_id=1, has_side_effects=True, vmem_limit_bytes=56 << 20
        ),
    )(x, u, w1, w2, small, routes)


def back_kernel(
    size,
    reps,
    heads,
    rows,
    tok_ref,
    u_ref,
    hidden_ref,
    ffn_ref,
    normed_ref,
    proj_ref,
    probs_ref,
    context_ref,
    whole_ref,
    sum_ref,
    route_ref,
    turned_ref,
    ret_ref,
    norm_ref,
    g1_ref,
    layer_ref,
    input_ref,
    mine_ref,
    g1_out_ref,
    grads,
    got,
    kept,
    y_buf,
    z_out,
    z_in,
    total,
    rep_all,
    strips,
    s_send,
    s_recv,
    t_send,
    t_recv,
    p_send,
    p_recv,
    y_send,
    y_recv,
    z_send,
    z_recv,
    r_send,
    r_recv,
    own_sem,
):
    place = Place(size)
    chips, outer, inner = place.chips, place.outer, place.inner
    core, chip = place.core, place.chip
    rep = lax.axis_index("rep")
    length, width = tok_ref.shape
    head_size = width // heads
    depth = mine_ref.shape[0]
    pad = (depth - SMALL) // 4
    place.greet(True, reps)
    partner = place.partner()
    moves = []
    own = pltpu.make_async_copy(g1_ref.at[chip], strips.at[rep, chip], own_sem)
    own.start()
    for i, (d, e) in enumerate(place.pairs()):
        if i > 0:
            target = place.at(d, e)
            moves.append(
                remote(
                    g1_ref.at[target],
                    strips.at[rep, chip],
                    s_send.at[i],
                    s_recv.at[i],
                    place.device(target),
                )
            )
            moves[-1].start()

    router = sum_ref[2:4, :]
    upstream = u_ref[...].astype(WIDE)
    hidden = hidden_ref[...]
    returned = ret_ref[...]
    route = route_ref[...].astype(WIDE)
    logits = dot(ffn_ref[...], sum_ref[...].astype(LOW), NT)
    first, second, gate = gate_of(logits, route)
    layer_ref[...] = (hidden + gate * returned).astype(LOW)
    gate_grad = jnp.sum(upstream * returned, axis=1, keepdims=True)
    scaled = gate * gate_grad
    first_grad = first * (jnp.where(route > 0.5, 0.0, gate_grad) - scaled)
    second_grad = second * (jnp.where(route > 0.5, gate_grad, 0.0) - scaled)
    ffn = ffn_ref[...].astype(WIDE)
    router_grad = jnp.concatenate(
        [
            jnp.sum(ffn * first_grad, axis=0, keepdims=True),
            jnp.sum(ffn * second_grad, axis=0, keepdims=True),
        ],
        axis=0,
    )
    norm_grad = norm_ref[...] + first_grad * router[0:1] + second_grad * router[1:2]
    scale = rms_scale(hidden)
    gain_ffn_grad = jnp.sum(norm_grad * hidden * scale, axis=0, keepdims=True)
    bent = norm_grad * sum_ref[1:2, :]
    hidden_grad = (
        upstream
        + scale * bent
        - hidden * (scale * scale * scale) * jnp.mean(bent * hidden, axis=1, keepdims=True)
    )
    attn_grad = hidden_grad.astype(LOW)
    split(grads, 3 * pad, rows, pad, dot(context_ref[...], attn_grad, TN))
    context_grad = dot(attn_grad, joined(whole_ref, 3 * pad, rows, pad), NT).astype(LOW)

    row = lax.broadcasted_iota(jnp.int32, (length, length), 0)
    col = lax.broadcasted_iota(jnp.int32, (length, length), 1)
    mirror = jnp.where(row + col == length - 1, 1.0, 0.0).astype(LOW)
    blank = jnp.zeros((length, length), WIDE)
    parts = [[], [], []]
    diagonals = []
    for h in range(heads):
        at = slice(h * head_size, (h + 1) * head_size)
        grad = context_grad[:, at]
        probs = probs_ref[h]
        prob_grad = dot(grad, proj_ref[2, :, at], NT)
        summed = jnp.sum(probs * prob_grad, axis=1, keepdims=True)
        low = (probs * (prob_grad - summed)).astype(LOW)
        flipped = dot(low, mirror)
        skewed = pltpu.roll(
            jnp.concatenate([flipped, blank], axis=1), 0, 1, stride=1, stride_axis=0
        )
        diagonals.append(jnp.sum(skewed, axis=0, keepdims=True))
        parts[0].append(dot(low, proj_ref[1, :, at]) * 0.125)
        parts[1].append(dot(low, proj_ref[0, :, at], TN) * 0.125)
        parts[2].append(dot(probs.astype(LOW), grad, TN))
    diagonal = jnp.concatenate(diagonals, axis=0)
    spots = lax.broadcasted_iota(jnp.int32, (length, 2 * length), 0)
    onehot = jnp.where(turned_ref[...] == spots, 1.0, 0.0).astype(LOW)
    high = diagonal.astype(LOW)
    rest = (diagonal - high.astype(WIDE)).astype(LOW)
    table_grad = dot(high, onehot, NT) + dot(rest, onehot, NT)
    normed = normed_ref[...]
    normed_grad = jnp.zeros((length, width), WIDE)
    for k in range(3):
        projected = jnp.concatenate(parts[k], axis=1).astype(LOW)
        split(grads, k * pad, rows, pad, dot(normed, projected, TN))
        normed_grad = normed_grad + dot(projected, joined(whole_ref, k * pad, rows, pad), NT)
    inputs = tok_ref[...].astype(WIDE)
    scale = rms_scale(inputs)
    gain_attn_grad = jnp.sum(normed_grad * inputs * scale, axis=0, keepdims=True)
    small = jnp.concatenate(
        [
            gain_attn_grad,
            gain_ffn_grad,
            router_grad,
            jnp.concatenate(
                [table_grad, jnp.zeros((heads, width - length), WIDE)], axis=1
            ),
        ],
        axis=0,
    ).astype(LOW)
    for j in range(size):
        grads[j // 2, j % 2, 4 * pad : 4 * pad + SMALL, :] = small

    def swap(i, d, e):
        k = place.at(-d, -e)
        return remote(
            grads.at[k, 1 - core], got.at[k], p_send.at[i], p_recv.at[i], partner
        )

    order = place.pairs()
    order = [p for p in order if p[1] > 0] + [p for p in order[1:] if p[1] == 0] + [(0, 0)]
    for d, e in order:
        swap(place.step(d, e), d, e).start()
    bent = normed_grad * sum_ref[0:1, :]
    input_ref[...] = (
        hidden_grad
        + scale * bent
        - inputs * (scale * scale * scale) * jnp.mean(bent * inputs, axis=1, keepdims=True)
    )

    own.wait()
    for copy in moves:
        copy.wait_recv()
    turns = []
    for f in range(1, reps):
        turns.append(
            remote(
                strips.at[rep],
                strips.at[rep],
                t_send.at[f - 1],
                t_recv.at[f - 1],
                {"rep": lax.rem(rep + f, reps)},
            )
        )
        turns[-1].start()

    def y_copy(d, e):
        i = place.step(d, e)
        k = place.at(-d, -e)
        return remote(
            kept.at[k],
            y_buf.at[i],
            y_send.at[i],
            y_recv.at[i],
            place.device(place.at(0, -e)),
        )

    def z_copy(d):
        return remote(
            z_out.at[d - 1],
            z_in.at[d - 1],
            z_send.at[d - 1],
            z_recv.at[d - 1],
            place.device(place.at(-d, 0)),
        )

    for d, e in order:
        i = place.step(d, e)
        k = place.at(-d, -e)
        swap(i, d, e).wait_recv()

        def add(n, carry):
            at = pl.ds(pl.multiple_of(n * 16, 16), 16)
            value = grads[k, core, at].astype(WIDE) + got[k, at].astype(WIDE)
            if e == 0:
                for s in range(1, inner):
                    value = value + y_buf[place.step(d, s), at].astype(WIDE)
            if e > 0:
                kept[k, at] = value.astype(LOW)
            elif d > 0:
                z_out[d - 1, at] = value.astype(LOW)
            else:
                total[at] = value
            return carry

        if e == 0:
            for s in range(1, inner):
                y_copy(d, s).wait_recv()
        lax.fori_loop(0, depth // 16, add, 0, unroll=True)
        if e > 0:
            y_copy(d, e).start()
        elif d > 0:
            z_copy(d).start()
    for d in range(1, outer):
        z_copy(d).wait()

    def finish(n, carry):
        at = pl.ds(pl.multiple_of(n * 16, 16), 16)
        value = total[at]
        for d in range(1, outer):
            value = value + z_in[d - 1, at].astype(WIDE)
        rep_all[rep, at] = value.astype(LOW)
        return carry

    lax.fori_loop(0, depth // 16, finish, 0, unroll=True)
    swaps = []
    for f in range(1, reps):
        swaps.append(
            remote(
                rep_all.at[rep],
                rep_all.at[rep],
                r_send.at[f - 1],
                r_recv.at[f - 1],
                {"rep": lax.rem(rep + f, reps)},
            )
        )
        swaps[-1].start()
    for copy in turns:
        copy.wait()
    strip = g1_ref.shape[2] // 2
    for k in range(chips):
        value = strips[0, k].astype(WIDE)
        for r in range(1, reps):
            value = value + strips[r, k].astype(WIDE)
        for e in range(2):
            g1_out_ref[e, :, k * strip : (k + 1) * strip] = value[:, e * strip : (e + 1) * strip]
    for copy in swaps:
        copy.wait()
    value = rep_all[0].astype(WIDE)
    for r in range(1, reps):
        value = value + rep_all[r].astype(WIDE)
    mine_ref[...] = value
    for copy in moves:
        copy.wait_send()
    for d, e in order:
        swap(place.step(d, e), d, e).wait_send()
        if e > 0:
            y_copy(d, e).wait_send()


def back(size, reps, heads, rows, *operands):
    chips = size // 2
    outer = grid_of(size)[0]
    steps = max(outer - 1, 1)
    length, width = operands[0].shape
    strips = operands[-1]
    pad, cols = strips.shape[1:]
    depth = 4 * pad + SMALL
    block = (chips, depth, width)
    return pl.pallas_call(
        functools.partial(back_kernel, size, reps, heads, rows),
        out_shape=(
            jax.ShapeDtypeStruct((length, width), LOW),
            jax.ShapeDtypeStruct((length, width), WIDE),
            jax.ShapeDtypeStruct((depth, width), WIDE),
            jax.ShapeDtypeStruct((2, pad, chips * cols // 2), WIDE),
        ),
        in_specs=[VMEM] * len(operands),
        out_specs=[VMEM] * 4,
        scratch_shapes=[
            pltpu.VMEM((chips, 2, depth, width), LOW),
            pltpu.VMEM(block, LOW),
            pltpu.VMEM(block, LOW),
            pltpu.VMEM(block, LOW),
            pltpu.VMEM((steps, depth, width), LOW),
            pltpu.VMEM((steps, depth, width), LOW),
            pltpu.VMEM((depth, width), WIDE),
            pltpu.VMEM((reps, depth, width), LOW),
            pltpu.VMEM((reps, chips, pad, cols), LOW),
            DMA((chips,)),
            DMA((chips,)),
            DMA((max(reps - 1, 1),)),
            DMA((max(reps - 1, 1),)),
            DMA((chips,)),
            DMA((chips,)),
            DMA((chips,)),
            DMA((chips,)),
            DMA((steps,)),
            DMA((steps,)),
            DMA((max(reps - 1, 1),)),
            DMA((max(reps - 1, 1),)),
            DMA,
        ],
        compiler_params=pltpu.CompilerParams(
            collective_id=2, has_side_effects=True, vmem_limit_bytes=56 << 20
        ),
    )(*operands)


def shards(
    size,
    reps,
    tokens,
    cotangent,
    lengths,
    routes,
    bucket_ids,
    attn_in,
    attn_out,
    gains,
    router,
    rel_table,
    expert_in,
    expert_out,
):
    length, width = tokens.shape
    heads = rel_table.shape[1]
    table_rows = rel_table.shape[0]
    chips = size // 2
    rows = attn_out.shape[0]
    pad = rows + -rows % 16
    hidden_units = expert_in.shape[2]
    strip = hidden_units // chips
    half = expert_out.shape[1]
    me = lax.axis_index("shard")

    small = jnp.zeros((SMALL, width), LOW)
    small = lax.dynamic_update_slice(
        small, jnp.concatenate([gains, router.T], axis=0), (0, me * rows)
    )
    table_block = lax.dynamic_update_slice(
        jnp.zeros((heads, length), LOW), rel_table.T, (0, me * table_rows)
    )
    upper = small[:4]
    lower = jnp.concatenate(
        [
            table_block,
            jnp.broadcast_to(routes.reshape(1, length).astype(LOW), (heads, length)),
            jnp.zeros((heads, width - 2 * length), LOW),
        ],
        axis=1,
    )
    small = jnp.concatenate([upper, lower], axis=0)
    buckets = jnp.pad(bucket_ids, (0, 1), constant_values=-1).reshape(1, 2 * length)
    turned = jnp.pad(bucket_ids[::-1], (0, 1), constant_values=-1).reshape(1, 2 * length)
    strips = jnp.transpose(expert_in.reshape(2, rows, chips, strip), (2, 1, 0, 3))
    strips = strips.reshape(chips, rows, 2 * strip)
    strips = jnp.pad(strips, ((0, 0), (0, pad - rows), (0, 0)))
    whole, w1, w2, normed, projected, probs, context, hidden, ffn, totals, columns = front(
        size,
        tokens,
        attn_in,
        attn_out,
        small,
        strips,
        expert_out,
        buckets,
        lengths,
        heads,
    )
    w1 = w1[:, :, :rows].reshape(width, 2 * strip)
    w2 = w2.reshape(2 * strip, width)
    returned, norm_grad, strip_grad, expert_out_grad = expert(
        size, reps, rows, pad, ffn, cotangent, w1, w2, totals, columns
    )
    layer_out, input_grad, mine, expert_in_grad = back(
        size,
        reps,
        heads,
        rows,
        tokens,
        cotangent,
        hidden,
        ffn,
        normed,
        projected,
        probs,
        context,
        whole,
        totals,
        routes,
        turned,
        returned,
        norm_grad,
        strip_grad,
    )
    in_shard = mine[: 3 * pad].reshape(3, pad, width)[:, :rows]
    out_shard = mine[3 * pad : 3 * pad + rows]
    sums = mine[4 * pad :]
    picked = lax.dynamic_slice(sums, (0, me * rows), (4, rows))
    table_shard = lax.dynamic_slice(sums, (4, me * table_rows), (heads, table_rows)).T
    return (
        layer_out,
        input_grad,
        in_shard,
        out_shard,
        picked[:2],
        picked[2:].T,
        table_shard,
        expert_in_grad[:, :rows],
        expert_out_grad,
    )


def solution(mesh):
    placed = (
        P(("rep", "shard"), None),
        P(("rep", "shard"), None),
        P(("rep", "shard"), None),
        P(("rep", "shard"), None),
        P(),
        P(None, "shard", None),
        P("shard", None),
        P(None, "shard"),
        P("shard", None),
        P("shard", None),
        P(None, "shard", None),
        P(None, "shard", None),
    )
    return jax.shard_map(
        functools.partial(shards, mesh.shape["shard"], mesh.shape["rep"]),
        mesh=mesh,
        in_specs=placed,
        out_specs=(
            P(("rep", "shard"), None),
            P(("rep", "shard"), None),
            P(None, "shard", None),
            P("shard", None),
            P(None, "shard"),
            P("shard", None),
            P("shard", None),
            P(None, "shard", None),
            P(None, "shard", None),
        ),
        check_vma=False,
    )
```

time: 388 us -> 259 us (0.67)
  local copies, waits for them, and re-layouts: 74.1 us -> 19.7 us
  Pallas kernels: 196 us -> 236 us
  matrix products: 30.5 us -> 0 us
  other arithmetic: 26.2 us -> 1.36 us
  starting transfers between devices: 23.9 us -> 0 us
  waiting for transfers between devices: 19.7 us -> 0 us
  between operations: 14.9 us -> 0.85 us
    concatenate x13 -> x0, local copies, waits for them, and re-layouts: 41.4 us -> none  [the longest x5 32.4 us: shards(): jnp.concatenate([attn_in_grad[0], attn_in_grad[1], attn_in_grad[2], attn_...]
    pallas_call x6 -> x3, Pallas kernels: 196 us -> 236 us  [the longest x1 102 us: expert(): pl.pallas_call(functools.partial(expert_kernel, size, reps, rows), out_sh...]
    dot_general x22 -> x0, matrix products: 30.5 us -> none  [the longest x1 4.56 us: shards(): jnp.einsum('cd,fd->cf', out_grad, out_strip, preferred_element_type=jnp.f...]
    ppermute x12 -> x0, waiting for transfers between devices: 19.7 us -> none  [the longest x3 18.7 us: rep_sum(): other = lax.ppermute(array, 'rep', [(0, 1), (1, 0)])]
    all_to_all x2 -> x0, starting transfers between devices: 19.5 us -> none  [the longest x1 10.1 us: shards(): lax.all_to_all(in_rows, 'shard', 0, 0, axis_index_groups=groups, tiled=True)]
    concatenate x6 -> x2, other arithmetic: 7.52 us -> 0.7 us  [the longest x1 0.68 us: shards(): jnp.concatenate([gains, router.T], axis=0)]
    unnamed x98 -> x46, local copies, waits for them, and re-layouts: 6.22 us -> 12.6 us
    another operation x11 -> x0, local copies, waits for them, and re-layouts: 6.11 us -> none  [the longest x1 2.61 us: shards(): jnp.stack([jnp.where(core == 0, same, other), jnp.where(core == 0, other,...]
  transfers between devices with their start and end apart: 15 -> 0, of which waited for: 4 -> 0; matrix products, arithmetic and copies ran while one was open for 27% -> 0% of each run, Pallas kernels for 41% -> 0%
where the time goes in v1:
time: 259 us; the launch traced here: 258 us
  Pallas kernels  236 us (91%)
  local copies, waits for them, and re-layouts  19.7 us (8%)
    pallas_call x1, Pallas kernels, expert(): pl.pallas_call(functools.partial(expert_kernel, size, reps, rows), out_sh...  102 us
    pallas_call x1, Pallas kernels, back(): pl.pallas_call(functools.partial(back_kernel, size, reps, heads, rows), o...  74.3 us
    pallas_call x1, Pallas kernels, front(): pl.pallas_call(functools.partial(front_kernel, size, heads), out_shape=(j...  59.9 us
    unnamed x46, local copies, waits for them, and re-layouts  12.6 us

profile of v1, /device:TPU:0, one launch (start us, length us, event | category | flops | bytes accessed | tf_op | source)
XLA Modules:
  0.0 258.1 jit_solution(11708166297684810278)
XLA Ops:
  0.6 0.7 copy.21
  1.5 0.7 pad_maximum_fusion
  2.6 0.7 convert_bitcast_fusion
  3.3 1.2 copy.25
  5.7 59.9 %shard_map.187 = (bf16[8,2,208,768]{3,2,1,0:T(8,128)(2,1)}, bf16[8,2,48,768]{3,2,1,0:T(8,128)(2,1)}, bf16[2,2,192,768]{3,2,1,0:T(8,128)(2,1)}, bf16[128,768]{1,0...) custom-call(bf16[128,768]{1,0:T(8,128)(2,1)S(1)} %copy-done.1, ...), custom_call_target="tpu_custom_call" | custom-call | tf_op jit(solution)/shard_map/pallas_call | solution.py:359
  65.6 0.7 copy-done
  66.3 0.8 copy-done.2
  67.1 0.7 copy-done.4
  67.8 0.6 copy-done.6
  68.5 0.7 copy-done.7
  69.1 0.7 copy-done.8
  69.8 0.6 copy-done.10
  70.4 101.9 %shard_map.188 = (f32[128,768]{1,0:T(8,128)}, f32[128,768]{1,0:T(8,128)}, bf16[8,48,768]{2,1,0:T(8,128)(2,1)}, f32[2,192,768]{2,1,0:T(8,128)}) custom-call(bf16[128,768]{1,0:T(8,128)(2,1)} %copy-done, bf16[128,768]{1,0:T(8,128)(2,1)} %u_ref.3, bf16[768,768]{1,0:T(8,128)(2,1)} %bitcast.24, bf16[768,768]{1,0:T(8,128)(2,1)} %bitcast.25, f32[16,768]{1,0:T(8,128)} %copy-done.6, ...), custom_call_target="tpu_custom_call" | custom-call | tf_op jit(solution)/shard_map/pallas_call | solution.py:624
  172.4 0.7 copy.23.route_ref
  173.9 74.3 %shard_map.189 = (bf16[128,768]{1,0:T(8,128)(2,1)}, f32[128,768]{1,0:T(8,128)}, f32[208,768]{1,0:T(8,128)}, f32[2,48,3072]{2,1,0:T(8,128)}) custom-call(bf16[128,768]{1,0:T(8,128)(2,1)} %tok_ref.3, bf16[128,768]{1,0:T(8,128)(2,1)} %u_ref.3, f32[128,768]{1,0:T(8,128)} %copy-done.4, bf16[128,768]{1,0:T(8,128)(2,1)} %copy-done, bf16[128,768]{1,0:T(8,128)(2,1)} %copy-done.7, ...), custom_call_target="tpu_custom_call" | custom-call | tf_op jit(solution)/shard_map/pallas_call | solution.py:963
  248.3 1.9 slice.19
  250.2 1.6 slice.20
  251.8 0.8 slice.21
  252.7 0.7 copy.24
  254.0 0.7 copy.34
  254.6 0.7 copy.35
  255.4 1.0 copy.36
  256.4 0.7 copy-done.12
  257.1 1.0 copy.37
  (45 shorter events, 3.2 us)
Async XLA Ops:
  4.4 1.1 copy-start.16
  4.4 1.1 copy-start.1
  4.4 1.2 copy-start.3
  4.5 1.2 copy-start.5
  4.5 1.2 copy-start.9
  4.5 1.2 copy-start.11
  65.6 0.7 copy-start
  66.3 0.8 copy-start.2
  67.1 0.7 copy-start.4
  67.8 0.6 copy-start.6
  68.5 0.7 copy-start.7
  69.1 0.7 copy-start.8
  69.8 0.6 copy-start.10
  70.4 102.0 %copy-start.17 = (s32[128,1]{0,1:T(1,128)S(1)}, s32[128,1]{0,1:T(1,128)}, u32[]{:S(2)}) copy-start(s32[128,1]{0,1:T(1,128)} %param.15) | copy-start | bytes 1540
  248.2 5.7 %copy-start.15 = (bf16[128,768]{1,0:T(8,128)(2,1)S(1)}, bf16[128,768]{1,0:T(8,128)(2,1)}, u32[]{:S(2)}) copy-start(bf16[128,768]{1,0:T(8,128)(2,1)} %get-tuple-element.67) | copy-start | bytes 589828
  248.3 6.4 %copy-start.14 = (f32[128,768]{1,0:T(8,128)S(1)}, f32[128,768]{1,0:T(8,128)}, u32[]{:S(2)}) copy-start(f32[128,768]{1,0:T(8,128)} %get-tuple-element.68) | copy-start | bytes 1179652
  248.3 7.1 %copy-start.13 = (f32[2,48,3072]{2,1,0:T(8,128)S(1)}, f32[2,48,3072]{2,1,0:T(8,128)}, u32[]{:S(2)}) copy-start(f32[2,48,3072]{2,1,0:T(8,128)} %get-tuple-element.74) | copy-start | bytes 3538948
  255.4 1.7 copy-start.12

commit v2 on v1

--- a/solution.py
+++ b/solution.py
@@ -47,26 +47,26 @@
     def partner(self):
         return {"shard": self.chip * 2 + 1 - self.core}
 
-    def step(self, d, e):
-        if d == 0:
-            return e
-        if e == 0:
-            return self.inner + d - 1
-        return self.inner + self.outer - 1 + (d - 1) * (self.inner - 1) + e - 1
-
     def pairs(self):
-        order = [(0, e) for e in range(self.inner)]
-        order += [(d, 0) for d in range(1, self.outer)]
-        order += [(d, e) for d in range(1, self.outer) for e in range(1, self.inner)]
-        return order
+        return [(d, e) for d in range(self.outer) for e in range(self.inner)]
+
+    def line(self, j):
+        z, top = self.z, self.outer - 1
+        short = jnp.minimum(z, top - z)
+        t = lax.div(j + 1, 2)
+        near = jnp.where(lax.rem(j, 2) == 1, z - t, z + t)
+        far = jnp.where(z <= top - z, z + j - short, z - j + short)
+        return jnp.where(j <= 2 * short, near, far)
+
+    def source(self, far, e):
+        return far * self.inner + lax.rem(self.y - e + self.inner, self.inner)
 
     def pair(self, i):
-        inner, outer = self.inner, self.outer
-        j = i - (inner + outer - 1)
-        side = max(inner - 1, 1)
-        d = jnp.where(i < inner, 0, jnp.where(j < 0, i - inner + 1, 1 + lax.div(j, side)))
-        e = jnp.where(i < inner, i, jnp.where(j < 0, 0, 1 + lax.rem(j, side)))
-        return d, e
+        q, r = lax.div(i + self.inner - 1, self.inner) - 1, lax.rem(i + self.inner - 1, self.inner)
+        last = q == self.outer - 1
+        e = jnp.where(last, r + 1, r)
+        j = jnp.where(last, q, jnp.where(r == 0, q + 1, q))
+        return jnp.where(i == 0, 0, j), jnp.where(i == 0, 0, e)
 
     def greet(self, chips, reps):
         barrier = pltpu.get_barrier_semaphore()
@@ -76,11 +76,24 @@
             pl.semaphore_signal(barrier, inc=1, device_id=target, device_id_type=MESH)
 
         for dz, dy in self.pairs()[1:]:
-            if chips or dz == 0 or dy == 0:
+            if chips or dz == 0:
                 signal(self.device(self.at(dz, dy)))
                 count += 1
         signal(self.partner())
         count += 1
+        if not chips:
+            below = jnp.where(self.z > 0, 1, 0)
+            above = jnp.where(self.z < self.outer - 1, 1, 0)
+
+            @pl.when(self.z > 0)
+            def _():
+                signal(self.device(self.chip - self.inner))
+
+            @pl.when(self.z < self.outer - 1)
+            def _():
+                signal(self.device(self.chip + self.inner))
+
+            count = count + below + above
         for f in range(1, reps):
             signal({"rep": lax.rem(lax.axis_index("rep") + f, reps)})
             count += 1
@@ -134,29 +147,209 @@
     return first, second, jnp.where(route > 0.5, second, first)
 
 
-def gather_start(place, own, slots, send_sem, recv_sem):
-    for d, e in place.pairs()[1:]:
-        if d == 0 or e == 0:
-            i = place.step(d, e)
-            target = place.device(place.at(d, e))
-            remote(own, slots.at[place.chip], send_sem.at[i], recv_sem.at[i], target).start()
-
-
-def gather_arrive(place, i, own, slots, send_sem, recv_sem):
-    d, e = place.pair(i)
-    source = place.at(-d, -e)
-    remote(own, slots.at[source], send_sem.at[i], recv_sem.at[i], place.device(source)).wait_recv()
-
-    @pl.when(jnp.logical_and(d > 0, e == 0))
-    def _():
-        for side in range(1, place.inner):
-            j = place.inner + place.outer - 1 + (d - 1) * (place.inner - 1) + side - 1
-            target = place.device(place.at(0, side))
-            remote(
-                slots.at[source], slots.at[source], send_sem.at[j], recv_sem.at[j], target
-            ).start()
-
-    return source
+class Gather:
+    def __init__(self, place, own, slots, up_send, down_send, z_recv, y_send, y_recv):
+        self.place, self.own, self.slots = place, own, slots
+        self.up_send, self.down_send, self.z_recv = up_send, down_send, z_recv
+        self.y_send, self.y_recv = y_send, y_recv
+
+    @staticmethod
+    def sems(size):
+        outer, inner = grid_of(size)
+        side = max(inner - 1, 1)
+        return [DMA((outer,))] * 3 + [DMA((outer, side))] * 2
+
+    def up(self, src, far):
+        place = self.place
+        slot = self.slots.at[place.source(far, 0)]
+        target = place.device(place.chip + place.inner)
+        return remote(src, slot, self.up_send.at[far], self.z_recv.at[far], target)
+
+    def down(self, src, far):
+        place = self.place
+        slot = self.slots.at[place.source(far, 0)]
+        target = place.device(place.chip - place.inner)
+        return remote(src, slot, self.down_send.at[far], self.z_recv.at[far], target)
+
+    def across(self, src, far, e):
+        place = self.place
+        slot = self.slots.at[place.source(far, 0)]
+        target = place.device(place.at(0, e))
+        return remote(
+            src, slot, self.y_send.at[far, e - 1], self.y_recv.at[far, e - 1], target
+        )
+
+    def spread(self, src, far, own):
+        place = self.place
+
+        @pl.when(place.z < place.outer - 1 if own else jnp.logical_and(far < place.z, place.z < place.outer - 1))
+        def _():
+            self.up(src, far).start()
+
+        @pl.when(place.z > 0 if own else jnp.logical_and(far > place.z, place.z > 0))
+        def _():
+            self.down(src, far).start()
+
+        for e in range(1, place.inner):
+            self.across(src, far, e).start()
+
+    def start(self):
+        self.spread(self.own, self.place.z, True)
+
+    def arrive_z(self, j):
+        far = self.place.line(j)
+        source = self.place.source(far, 0)
+        slot = self.slots.at[source]
+        remote(
+            self.own, slot, self.up_send.at[far], self.z_recv.at[far], self.place.partner()
+        ).wait_recv()
+        self.spread(slot, far, False)
+        return source
+
+    def arrive_y(self, j, e):
+        far = self.place.line(j)
+        source = self.place.source(far, e)
+        remote(
+            self.own,
+            self.slots.at[source],
+            self.y_send.at[far, e - 1],
+            self.y_recv.at[far, e - 1],
+            self.place.partner(),
+        ).wait_recv()
+        return source
+
+    def arrive(self, j, e):
+        @pl.when(jnp.logical_and(j > 0, e == 0))
+        def _():
+            self.arrive_z(j)
+
+        @pl.when(e > 0)
+        def _():
+            self.arrive_y(j, e)
+
+        return self.place.source(self.place.line(j), e)
+
+    def finish(self):
+        place = self.place
+
+        def sent(far, carry):
+            @pl.when(jnp.logical_and(far <= place.z, place.z < place.outer - 1))
+            def _():
+                self.up(self.own, far).wait_send()
+
+            @pl.when(jnp.logical_and(far >= place.z, place.z > 0))
+            def _():
+                self.down(self.own, far).wait_send()
+
+            for e in range(1, place.inner):
+                self.across(self.own, far, e).wait_send()
+            return carry
+
+        lax.fori_loop(0, place.outer, sent, 0)
+
+
+class Scatter:
+    def __init__(self, place, part, y_buf, z_out, z_in, acc, y_send, y_recv, z_send, z_recv):
+        self.place, self.part, self.acc = place, part, acc
+        self.y_buf, self.z_out, self.z_in = y_buf, z_out, z_in
+        self.y_send, self.y_recv, self.z_send, self.z_recv = y_send, y_recv, z_send, z_recv
+
+    @staticmethod
+    def buffers(size, block):
+        outer, inner = grid_of(size)
+        side = max(inner - 1, 1)
+        return [
+            pltpu.VMEM((outer, side) + block, LOW),
+            pltpu.VMEM((outer,) + block, LOW),
+            pltpu.VMEM((2, outer) + block, LOW),
+            pltpu.VMEM(block, WIDE),
+            DMA((outer, side)),
+            DMA((outer, side)),
+            DMA((outer,)),
+            DMA((2, outer)),
+        ]
+
+    def across(self, far, e):
+        place = self.place
+        return remote(
+            self.part.at[place.source(far, e)],
+            self.y_buf.at[far, e - 1],
+            self.y_send.at[far, e - 1],
+            self.y_recv.at[far, e - 1],
+            place.device(place.at(0, -e)),
+        )
+
+    def along(self, far, way):
+        place = self.place
+        target = place.chip + (place.inner if way == 0 else -place.inner)
+        return remote(
+            self.z_out.at[far],
+            self.z_in.at[way, far],
+            self.z_send.at[far],
+            self.z_recv.at[way, far],
+            place.device(target),
+        )
+
+    def collect(self, j, last, first_term, give):
+        place, acc = self.place, self.acc
+        far = place.line(j)
+        count = acc.shape[0] // 16
+        for e in range(1, place.inner):
+            self.across(far, e).wait_recv()
+
+        def rows(n):
+            return pl.ds(pl.multiple_of(n * 16, 16), 16)
+
+        def begin(n, carry):
+            value = first_term(place.source(far, 0), rows(n))
+            for e in range(1, place.inner):
+                value = value + self.y_buf[far, e - 1, rows(n)].astype(WIDE)
+            acc[rows(n)] = value
+            return carry
+
+        lax.fori_loop(0, count, begin, 0, unroll=True)
+        for way in range(2):
+            more = place.z > 0 if way == 0 else place.z < place.outer - 1
+            if not last:
+                more = jnp.logical_and(more, far > place.z if way == 0 else far < place.z)
+
+            @pl.when(more)
+            def _(way=way):
+                self.along(far, way).wait_recv()
+
+                def add(n, carry):
+                    acc[rows(n)] += self.z_in[way, far, rows(n)].astype(WIDE)
+                    return carry
+
+                lax.fori_loop(0, count, add, 0, unroll=True)
+
+        if last:
+            give()
+            return
+        self.z_out[far] = acc[...].astype(LOW)
+
+        @pl.when(far > place.z)
+        def _():
+            self.along(far, 0).start()
+
+        @pl.when(far < place.z)
+        def _():
+            self.along(far, 1).start()
+
+    def finish(self):
+        place = self.place
+
+        def sent(far, carry):
+            for e in range(1, place.inner):
+                self.across(far, e).wait_send()
+
+            @pl.when(far != place.z)
+            def _():
+                self.along(far, 0).wait_send()
+
+            return carry
+
+        lax.fori_loop(0, place.outer, sent, 0)
 
 
 def front_kernel(
@@ -181,6 +374,9 @@
     ffn_ref,
     sum_ref,
     route_ref,
+    g_up,
+    g_down,
+    g_z,
     g_send,
     g_recv,
     c_send,
@@ -207,19 +403,19 @@
     whole_ref[chip, core, 4 * pad : 4 * pad + SMALL, :] = small_ref[...]
     place.greet(True, 1)
     partner = place.partner()
-    slots = whole_ref.at[:, core]
-    gather_start(place, mine, slots, g_send, g_recv)
-
-    def dup(i, source):
+    gather = Gather(place, mine, whole_ref.at[:, core], g_up, g_down, g_z, g_send, g_recv)
+    gather.start()
+
+    def dup(source):
         return remote(
             whole_ref.at[source, core],
             whole_ref.at[source, core],
-            c_send.at[i],
-            c_recv.at[i],
+            c_send.at[source],
+            c_recv.at[source],
             partner,
         )
 
-    dup(0, chip).start()
+    dup(chip).start()
     local = [
         pltpu.make_async_copy(strip_ref.at[chip], w1_ref.at[chip, core], own_sem.at[0]),
         pltpu.make_async_copy(half_ref, w2_ref.at[:, core], own_sem.at[1]),
@@ -230,11 +426,12 @@
     halves.start()
 
     def arrive(i, carry):
-        source = gather_arrive(place, i, mine, slots, g_send, g_recv)
-        dup(i, source).start()
+        j, e = place.pair(i)
+        dup(gather.arrive(j, e)).start()
         return carry
 
-    lax.fori_loop(1, place.inner + place.outer - 1, arrive, 0)
+    late = chips - 2 * (place.inner - 1)
+    lax.fori_loop(1, late, arrive, 0)
     strips = []
     for i, (d, e) in enumerate(place.pairs()):
         if i > 0:
@@ -248,16 +445,14 @@
             )
             copy.start()
             strips.append(copy)
-    lax.fori_loop(place.inner + place.outer - 1, chips, arrive, 0)
-
-    def other(i, carry):
-        d, e = place.pair(i)
-        source = place.at(-d, -e)
+    lax.fori_loop(late, chips, arrive, 0)
+
+    def other(source, carry):
         remote(
             whole_ref.at[source, core],
             whole_ref.at[source, 1 - core],
-            c_send.at[i],
-            c_recv.at[i],
+            c_send.at[source],
+            c_recv.at[source],
             partner,
         ).wait_recv()
         return carry
@@ -311,10 +506,11 @@
     hidden_ref[...] = hidden
     ffn_ref[...] = (hidden * rms_scale(hidden) * total[1:2]).astype(LOW)
 
+    def moved(i):
+        return place.at(-lax.div(i, place.inner), -lax.rem(i, place.inner))
+
     def pass_on(i, carry):
-        d, e = place.pair(i)
-        source = place.at(-d, -e)
-        block = w1_ref.at[source, core]
+        block = w1_ref.at[moved(i), core]
         remote(block, block, s_send.at[i], s_recv.at[i], partner).wait_recv()
         remote(block, block, d_send.at[i], d_recv.at[i], partner).start()
         return carry
@@ -324,26 +520,23 @@
     lax.fori_loop(1, chips, pass_on, 0)
 
     def last(i, carry):
-        d, e = place.pair(i)
-        source = place.at(-d, -e)
+        source = moved(i)
         block = w1_ref.at[source, 1 - core]
         sent = w1_ref.at[source, core]
         remote(sent, block, d_send.at[i], d_recv.at[i], partner).wait()
-        remote(
-            whole_ref.at[source, core], whole_ref.at[source, core], c_send.at[i], c_recv.at[i], partner
-        ).wait_send()
+        dup(source).wait_send()
         return carry
 
     lax.fori_loop(0, chips, last, 0)
 
     def sent(i, carry):
-        remote(mine, mine, g_send.at[i], g_recv.at[i], partner).wait_send()
         remote(
             strip_ref.at[0], w1_ref.at[chip, core], s_send.at[i], s_recv.at[i], partner
         ).wait_send()
         return carry
 
     lax.fori_loop(1, chips, sent, 0)
+    gather.finish()
     local[1].wait()
     halves.wait()
 
@@ -355,7 +548,7 @@
     pad = strips.shape[1]
     cols = strips.shape[2]
     depth = 4 * pad + SMALL
-    sems = [DMA((chips,))] * 8
+    sems = [*Gather.sems(size), *[DMA((chips,))] * 6]
     return pl.pallas_call(
         functools.partial(front_kernel, size, heads),
         out_shape=(
@@ -400,28 +593,19 @@
     slope,
     scaled,
     before_grad,
-    part,
-    y_buf,
-    z_out,
-    z_in,
+    ret_part,
+    back_part,
     g1_own,
     g1_got,
     g2_own,
     g2_got,
     g2_all,
-    x_send,
-    x_recv,
-    u_send,
-    u_recv,
-    y_send,
-    y_recv,
-    z_send,
-    z_recv,
     p_send,
     p_recv,
     r_send,
     r_recv,
     own_sem,
+    *rest,
 ):
     place = Place(size)
     chips, outer, inner = place.chips, place.outer, place.inner
@@ -433,7 +617,11 @@
     pad = g1_own.shape[2]
     place.greet(False, reps)
     partner = place.partner()
-    gather_start(place, x_ref, xs, x_send, x_recv)
+    x_gather = Gather(place, x_ref, xs, *rest[:5])
+    u_gather = Gather(place, u_ref, us, *rest[5:10])
+    ret_scatter = Scatter(place, ret_part, *rest[10:18])
+    back_scatter = Scatter(place, back_part, *rest[18:26])
+    x_gather.start()
     own = [
         pltpu.make_async_copy(x_ref, xs.at[chip], own_sem.at[0]),
         pltpu.make_async_copy(u_ref, us.at[chip], own_sem.at[1]),
@@ -449,32 +637,9 @@
     def route_of(k):
         return jnp.sum(jnp.where(lane == k, route_ref[...], 0.0), axis=1, keepdims=True)
 
-    def y_copy(q, i, d, e):
-        k = place.at(-d, -e)
-        return remote(
-            part.at[q, k],
-            y_buf.at[q, i],
-            y_send.at[q, i],
-            y_recv.at[q, i],
-            place.device(place.at(0, -e)),
-        )
-
-    def z_copy(q, d):
-        return remote(
-            z_out.at[q, d - 1],
-            z_in.at[q, d - 1],
-            z_send.at[q, d - 1],
-            z_recv.at[q, d - 1],
-            place.device(place.at(-d, 0)),
-        )
-
     def forward(i, carry):
-        @pl.when(i > 0)
-        def _():
-            gather_arrive(place, i, x_ref, xs, x_send, x_recv)
-
-        d, e = place.pair(i)
-        k = place.at(-d, -e)
+        j, e = place.pair(i)
+        k = x_gather.arrive(j, e)
         before = dot(xs[k], w1_ref[...])
         keep = jnp.logical_xor(side, route_of(k) < 0.5)
         square = before * before
@@ -486,62 +651,57 @@
         active = jnp.where(keep, before * half, 0.0).astype(LOW)
         act[k] = active
         slope[k] = jnp.where(keep, rise, 0.0)
-        part[0, k] = dot(active, w2_ref[...]).astype(LOW)
-
-        @pl.when(e > 0)
-        def _():
-            y_copy(0, i, d, e).start()
-
+        ret_part[k] = dot(active, w2_ref[...]).astype(LOW)
         return carry
 
-    lax.fori_loop(0, inner + 1, forward, 0)
-    gather_start(place, u_ref, us, u_send, u_recv)
-    lax.fori_loop(inner + 1, chips, forward, 0)
-
-    def collect(q, d):
-        def add(k, carry):
-            at = pl.ds(pl.multiple_of(k * 16, 16), 16)
-            value = part[q, place.at(-d, 0), at].astype(WIDE)
-            for e in range(1, inner):
-                value = value + y_buf[q, place.step(d, e), at].astype(WIDE)
-            if d == 0:
-                target = ret_ref if q == 0 else back_ref
-                target[at] = value
-            else:
-                z_out[q, d - 1, at] = value.astype(LOW)
-            return carry
-
+    late = chips - 2 * (inner - 1)
+    lax.fori_loop(0, late, forward, 0)
+    u_gather.start()
+    lax.fori_loop(late, chips, forward, 0)
+
+    def ret_term(k, at):
+        return ret_part[k, at].astype(WIDE)
+
+    def back_term(k, at):
+        return back_part[k, at].astype(WIDE)
+
+    def ret_give():
+        ret_ref[...] = ret_scatter.acc[...]
+
+    def back_give():
+        back_ref[...] = back_scatter.acc[...]
+
+    for j in range(1, outer):
+        u_gather.arrive_z(j)
         for e in range(1, inner):
-            y_copy(q, place.step(d, e), d, e).wait_recv()
-        lax.fori_loop(0, length // 16, add, 0, unroll=True)
-        if d > 0:
-            z_copy(q, d).start()
-
-    def backward(i, carry):
-        @pl.when(i > 0)
-        def _():
-            gather_arrive(place, i, u_ref, us, u_send, u_recv)
-
-        d, e = place.pair(i)
-        k = place.at(-d, -e)
+            ret_scatter.across(place.line(outer - j), e).start()
+    for e in range(1, inner):
+        ret_scatter.across(place.line(0), e).start()
+
+    def backward(j, e):
+        k = place.source(place.line(j), e)
         gate = gate_of(dot(xs[k], router, NT), route_of(k))[2]
         low = (gate * us[k].astype(WIDE)).astype(LOW)
         scaled[k] = low
         grad = (dot(low, w2_ref[...], NT) * slope[k]).astype(LOW)
         before_grad[k] = grad
-        part[1, k] = dot(grad, w1_ref[...], NT).astype(LOW)
-
-        @pl.when(e > 0)
+        back_part[k] = dot(grad, w1_ref[...], NT).astype(LOW)
+
+    def back_step(n, carry):
+        j = outer - 1 - n
+        for e in range(1, inner):
+            u_gather.arrive_y(j, e)
+            backward(j, e)
+            back_scatter.across(place.line(j), e).start()
+
+        @pl.when(j > 0)
         def _():
-            y_copy(1, i, d, e).start()
-
+            ret_scatter.collect(j, False, ret_term, None)
+
+        backward(j, 0)
         return carry
 
-    lax.fori_loop(0, inner + outer - 1, backward, 0)
-    for d in range(1, outer):
-        collect(0, d)
-    lax.fori_loop(inner + outer - 1, chips, backward, 0)
-    collect(0, 0)
+    lax.fori_loop(0, outer, back_step, 0)
 
     def flat(ref):
         return ref[...].reshape(chips * length, ref.shape[2])
@@ -550,8 +710,8 @@
     g2_own[...] = g2.astype(LOW).reshape(g2_own.shape)
     g2_swap = remote(g2_own.at[:, 1 - core], g2_got, p_send.at[0], p_recv.at[0], partner)
     g2_swap.start()
-    for d in range(1, outer):
-        collect(1, d)
+    for j in range(outer - 1, 1, -1):
+        back_scatter.collect(j, False, back_term, None)
     g2_swap.wait()
     g2_all[rep] = (g2_own[:, core].astype(WIDE) + g2_got[...].astype(WIDE)).astype(LOW)
     swaps = []
@@ -570,23 +730,9 @@
     split(g1_own, 0, rows, pad, g1)
     g1_swap = remote(g1_own.at[:, 1 - core], g1_got, p_send.at[1], p_recv.at[1], partner)
     g1_swap.start()
-    collect(1, 0)
-
-    def finish(q, target):
-        for d in range(1, outer):
-            z_copy(q, d).wait()
-
-        def add(k, carry):
-            at = pl.ds(pl.multiple_of(k * 16, 16), 16)
-            value = target[at]
-            for d in range(1, outer):
-                value = value + z_in[q, d - 1, at].astype(WIDE)
-            target[at] = value
-            return carry
-
-        lax.fori_loop(0, length // 16, add, 0, unroll=True)
-
-    finish(0, ret_ref)
+    if outer > 1:
+        back_scatter.collect(1, False, back_term, None)
+    ret_scatter.collect(0, True, ret_term, ret_give)
     g1_swap.wait()
     g1_ref[...] = (g1_own[:, core].astype(WIDE) + g1_got[...].astype(WIDE)).astype(LOW)
     for copy in swaps:
@@ -595,27 +741,15 @@
     for r in range(1, reps):
         value = value + g2_all[r].astype(WIDE)
     g2_ref[...] = value
-    finish(1, back_ref)
-
-    def sent(i, carry):
-        remote(x_ref, xs.at[0], x_send.at[i], x_recv.at[i], partner).wait_send()
-        remote(u_ref, us.at[0], u_send.at[i], u_recv.at[i], partner).wait_send()
-        d, e = place.pair(i)
-
-        @pl.when(e > 0)
-        def _():
-            y_copy(0, i, d, e).wait_send()
-            y_copy(1, i, d, e).wait_send()
-
-        return carry
-
-    lax.fori_loop(1, chips, sent, 0)
+    back_scatter.collect(0, True, back_term, back_give)
+    x_gather.finish()
+    u_gather.finish()
+    ret_scatter.finish()
+    back_scatter.finish()
 
 
 def expert(size, reps, rows, pad, x, u, w1, w2, small, routes):
     chips = size // 2
-    outer = grid_of(size)[0]
-    steps = max(outer - 1, 1)
     length, width = x.shape
     cols = w1.shape[1]
     half = cols // 4
@@ -638,28 +772,22 @@
             pltpu.VMEM(wide, WIDE),
             pltpu.VMEM(block, LOW),
             pltpu.VMEM(wide, LOW),
-            pltpu.VMEM((2,) + block, LOW),
-            pltpu.VMEM((2,) + block, LOW),
-            pltpu.VMEM((2, steps, length, width), LOW),
-            pltpu.VMEM((2, steps, length, width), LOW),
+            pltpu.VMEM(block, LOW),
+            pltpu.VMEM(block, LOW),
             pltpu.VMEM((chips, 2, pad, cols), LOW),
             pltpu.VMEM((chips, pad, cols), LOW),
             pltpu.VMEM((2, 2, half, width), LOW),
             pltpu.VMEM((2, half, width), LOW),
             pltpu.VMEM((reps, 2, half, width), LOW),
-            DMA((chips,)),
-            DMA((chips,)),
-            DMA((chips,)),
-            DMA((chips,)),
-            DMA((2, chips)),
-            DMA((2, chips)),
-            DMA((2, steps)),
-            DMA((2, steps)),
             DMA((2,)),
             DMA((2,)),
             DMA((max(reps - 1, 1),)),
             DMA((max(reps - 1, 1),)),
             DMA((2,)),
+            *Gather.sems(size),
+            *Gather.sems(size),
+            *Scatter.buffers(size, (length, width)),
+            *Scatter.buffers(size, (length, width)),
         ],
         compiler_params=pltpu.CompilerParams(
             collective_id=1, has_side_effects=True, vmem_limit_bytes=56 << 20
@@ -694,10 +822,6 @@
     grads,
     got,
     kept,
-    y_buf,
-    z_out,
-    z_in,
-    total,
     rep_all,
     strips,
     s_send,
@@ -706,13 +830,10 @@
     t_recv,
     p_send,
     p_recv,
-    y_send,
-    y_recv,
-    z_send,
-    z_recv,
     r_send,
     r_recv,
     own_sem,
+    *rest,
 ):
     place = Place(size)
     chips, outer, inner = place.chips, place.outer, place.inner
@@ -799,8 +920,8 @@
     spots = lax.broadcasted_iota(jnp.int32, (length, 2 * length), 0)
     onehot = jnp.where(turned_ref[...] == spots, 1.0, 0.0).astype(LOW)
     high = diagonal.astype(LOW)
-    rest = (diagonal - high.astype(WIDE)).astype(LOW)
-    table_grad = dot(high, onehot, NT) + dot(rest, onehot, NT)
+    below = (diagonal - high.astype(WIDE)).astype(LOW)
+    table_grad = dot(high, onehot, NT) + dot(below, onehot, NT)
     normed = normed_ref[...]
     normed_grad = jnp.zeros((length, width), WIDE)
     for k in range(3):
@@ -824,16 +945,17 @@
     for j in range(size):
         grads[j // 2, j % 2, 4 * pad : 4 * pad + SMALL, :] = small
 
-    def swap(i, d, e):
-        k = place.at(-d, -e)
+    scatter = Scatter(place, kept, *rest)
+
+    def swap(k):
         return remote(
-            grads.at[k, 1 - core], got.at[k], p_send.at[i], p_recv.at[i], partner
+            grads.at[k, 1 - core], got.at[k], p_send.at[k], p_recv.at[k], partner
         )
 
-    order = place.pairs()
-    order = [p for p in order if p[1] > 0] + [p for p in order[1:] if p[1] == 0] + [(0, 0)]
-    for d, e in order:
-        swap(place.step(d, e), d, e).start()
+    order = [(j, e) for j in range(outer - 1, -1, -1) for e in range(1, inner)]
+    order += [(j, 0) for j in range(outer - 1, -1, -1)]
+    for j, e in order:
+        swap(place.source(place.line(j), e)).start()
     bent = normed_grad * sum_ref[0:1, :]
     input_ref[...] = (
         hidden_grad
@@ -857,65 +979,34 @@
         )
         turns[-1].start()
 
-    def y_copy(d, e):
-        i = place.step(d, e)
-        k = place.at(-d, -e)
-        return remote(
-            kept.at[k],
-            y_buf.at[i],
-            y_send.at[i],
-            y_recv.at[i],
-            place.device(place.at(0, -e)),
-        )
-
-    def z_copy(d):
-        return remote(
-            z_out.at[d - 1],
-            z_in.at[d - 1],
-            z_send.at[d - 1],
-            z_recv.at[d - 1],
-            place.device(place.at(-d, 0)),
-        )
-
-    for d, e in order:
-        i = place.step(d, e)
-        k = place.at(-d, -e)
-        swap(i, d, e).wait_recv()
-
-        def add(n, carry):
-            at = pl.ds(pl.multiple_of(n * 16, 16), 16)
-            value = grads[k, core, at].astype(WIDE) + got[k, at].astype(WIDE)
-            if e == 0:
-                for s in range(1, inner):
-                    value = value + y_buf[place.step(d, s), at].astype(WIDE)
-            if e > 0:
-                kept[k, at] = value.astype(LOW)
-            elif d > 0:
-                z_out[d - 1, at] = value.astype(LOW)
-            else:
-                total[at] = value
-            return carry
-
-        if e == 0:
-            for s in range(1, inner):
-                y_copy(d, s).wait_recv()
-        lax.fori_loop(0, depth // 16, add, 0, unroll=True)
-        if e > 0:
-            y_copy(d, e).start()
-        elif d > 0:
-            z_copy(d).start()
-    for d in range(1, outer):
-        z_copy(d).wait()
-
-    def finish(n, carry):
-        at = pl.ds(pl.multiple_of(n * 16, 16), 16)
-        value = total[at]
-        for d in range(1, outer):
-            value = value + z_in[d - 1, at].astype(WIDE)
-        rep_all[rep, at] = value.astype(LOW)
+    def cross(n, carry):
+        j = outer - 1 - n
+        far = place.line(j)
+        for e in range(1, inner):
+            k = place.source(far, e)
+            swap(k).wait_recv()
+            kept[k] = (grads[k, core].astype(WIDE) + got[k].astype(WIDE)).astype(LOW)
+            scatter.across(far, e).start()
         return carry
 
-    lax.fori_loop(0, depth // 16, finish, 0, unroll=True)
+    lax.fori_loop(0, outer, cross, 0)
+
+    def term(k, at):
+        return grads[k, core, at].astype(WIDE) + got[k, at].astype(WIDE)
+
+    def pass_on(n, carry):
+        j = outer - 1 - n
+        swap(place.source(place.line(j), 0)).wait_recv()
+        scatter.collect(j, False, term, None)
+        return carry
+
+    lax.fori_loop(0, outer - 1, pass_on, 0)
+    swap(chip).wait_recv()
+
+    def give():
+        rep_all[rep] = scatter.acc[...].astype(LOW)
+
+    scatter.collect(0, True, term, give)
     swaps = []
     for f in range(1, reps):
         swaps.append(
@@ -945,16 +1036,13 @@
     mine_ref[...] = value
     for copy in moves:
         copy.wait_send()
-    for d, e in order:
-        swap(place.step(d, e), d, e).wait_send()
-        if e > 0:
-            y_copy(d, e).wait_send()
+    for k in range(chips):
+        swap(k).wait_send()
+    scatter.finish()
 
 
 def back(size, reps, heads, rows, *operands):
     chips = size // 2
-    outer = grid_of(size)[0]
-    steps = max(outer - 1, 1)
     length, width = operands[0].shape
     strips = operands[-1]
     pad, cols = strips.shape[1:]
@@ -974,10 +1062,6 @@
             pltpu.VMEM((chips, 2, depth, width), LOW),
             pltpu.VMEM(block, LOW),
             pltpu.VMEM(block, LOW),
-            pltpu.VMEM(block, LOW),
-            pltpu.VMEM((steps, depth, width), LOW),
-            pltpu.VMEM((steps, depth, width), LOW),
-            pltpu.VMEM((depth, width), WIDE),
             pltpu.VMEM((reps, depth, width), LOW),
             pltpu.VMEM((reps, chips, pad, cols), LOW),
             DMA((chips,)),
@@ -986,13 +1070,10 @@
             DMA((max(reps - 1, 1),)),
             DMA((chips,)),
             DMA((chips,)),
-            DMA((chips,)),
-            DMA((chips,)),
-            DMA((steps,)),
-            DMA((steps,)),
             DMA((max(reps - 1, 1),)),
             DMA((max(reps - 1, 1),)),
             DMA,
+            *Scatter.buffers(size, (depth, width)),
         ],
         compiler_params=pltpu.CompilerParams(
             collective_id=2, has_side_effects=True, vmem_limit_bytes=56 << 20

time: 259 us -> 233 us (0.90)
  Pallas kernels: 236 us -> 211 us
    pallas_call x1, Pallas kernels: 102 us -> 88.5 us  [expert(): pl.pallas_call(functools.partial(expert_kernel, size, reps, rows), out_sh...]
    pallas_call x1, Pallas kernels: 74.3 us -> 67.5 us  [back(): pl.pallas_call(functools.partial(back_kernel, size, reps, heads, rows), o...]
    pallas_call x1, Pallas kernels: 59.9 us -> 55 us  [front(): pl.pallas_call(functools.partial(front_kernel, size, heads), out_shape=(j...]
where the time goes in v2:
time: 233 us
  Pallas kernels  211 us (91%)
  local copies, waits for them, and re-layouts  19.7 us (8%)
    pallas_call x1, Pallas kernels, expert(): pl.pallas_call(functools.partial(expert_kernel, size, reps, rows), out_sh...  88.5 us
    pallas_call x1, Pallas kernels, back(): pl.pallas_call(functools.partial(back_kernel, size, reps, heads, rows), o...  67.5 us
    pallas_call x1, Pallas kernels, front(): pl.pallas_call(functools.partial(front_kernel, size, heads), out_shape=(j...  55 us
    unnamed x46, local copies, waits for them, and re-layouts  12.6 us

profile of v2, /device:TPU:0, one launch (start us, length us, event | category | flops | bytes accessed | tf_op | source)
XLA Modules:
  0.0 232.8 jit_solution(11698898188865056404)
XLA Ops:
  0.6 0.7 copy.21
  1.5 0.7 pad_maximum_fusion
  2.6 0.7 convert_bitcast_fusion
  3.3 1.2 copy.25
  5.7 55.0 %shard_map.187 = (bf16[8,2,208,768]{3,2,1,0:T(8,128)(2,1)}, bf16[8,2,48,768]{3,2,1,0:T(8,128)(2,1)}, bf16[2,2,192,768]{3,2,1,0:T(8,128)(2,1)}, bf16[128,768]{1,0...) custom-call(bf16[128,768]{1,0:T(8,128)(2,1)S(1)} %copy-done.1, ...), custom_call_target="tpu_custom_call" | custom-call | tf_op jit(solution)/shard_map/pallas_call | solution.py:552
  60.7 0.7 copy-done
  61.4 0.8 copy-done.2
  62.2 0.7 copy-done.4
  63.0 0.6 copy-done.6
  63.6 0.7 copy-done.7
  64.3 0.7 copy-done.8
  64.9 0.6 copy-done.10
  65.6 88.5 %shard_map.188 = (f32[128,768]{1,0:T(8,128)}, f32[128,768]{1,0:T(8,128)}, bf16[8,48,768]{2,1,0:T(8,128)(2,1)}, f32[2,192,768]{2,1,0:T(8,128)}) custom-call(bf16[128,768]{1,0:T(8,128)(2,1)} %copy-done, bf16[128,768]{1,0:T(8,128)(2,1)} %u_ref.3, bf16[768,768]{1,0:T(8,128)(2,1)} %bitcast.24, bf16[768,768]{1,0:T(8,128)(2,1)} %bitcast.25, f32[16,768]{1,0:T(8,128)} %copy-done.6, ...), custom_call_target="tpu_custom_call" | custom-call | tf_op jit(solution)/shard_map/pallas_call | solution.py:758
  154.0 0.7 copy.23.route_ref
  155.5 67.5 %shard_map.189 = (bf16[128,768]{1,0:T(8,128)(2,1)}, f32[128,768]{1,0:T(8,128)}, f32[208,768]{1,0:T(8,128)}, f32[2,48,3072]{2,1,0:T(8,128)}) custom-call(bf16[128,768]{1,0:T(8,128)(2,1)} %tok_ref.3, bf16[128,768]{1,0:T(8,128)(2,1)} %u_ref.3, f32[128,768]{1,0:T(8,128)} %copy-done.4, bf16[128,768]{1,0:T(8,128)(2,1)} %copy-done, bf16[128,768]{1,0:T(8,128)(2,1)} %copy-done.7, ...), custom_call_target="tpu_custom_call" | custom-call | tf_op jit(solution)/shard_map/pallas_call | solution.py:1051
  223.0 1.9 slice.19
  224.9 1.6 slice.20
  226.5 0.8 slice.21
  227.4 0.7 copy.24
  228.7 0.7 copy.34
  229.4 0.7 copy.35
  230.1 1.0 copy.36
  231.1 0.7 copy-done.12
  231.8 1.0 copy.37
  (45 shorter events, 3.2 us)
Async XLA Ops:
  4.4 1.1 copy-start.16
  4.4 1.1 copy-start.1
  4.4 1.2 copy-start.3
  4.5 1.2 copy-start.5
  4.5 1.2 copy-start.9
  4.5 1.2 copy-start.11
  60.7 0.7 copy-start
  61.4 0.8 copy-start.2
  62.2 0.7 copy-start.4
  63.0 0.6 copy-start.6
  63.6 0.7 copy-start.7
  64.3 0.7 copy-start.8
  64.9 0.6 copy-start.10
  65.6 88.5 %copy-start.17 = (s32[128,1]{0,1:T(1,128)S(1)}, s32[128,1]{0,1:T(1,128)}, u32[]{:S(2)}) copy-start(s32[128,1]{0,1:T(1,128)} %param.15) | copy-start | bytes 1540
  223.0 5.7 %copy-start.15 = (bf16[128,768]{1,0:T(8,128)(2,1)S(1)}, bf16[128,768]{1,0:T(8,128)(2,1)}, u32[]{:S(2)}) copy-start(bf16[128,768]{1,0:T(8,128)(2,1)} %get-tuple-element.67) | copy-start | bytes 589828
  223.0 6.4 %copy-start.14 = (f32[128,768]{1,0:T(8,128)S(1)}, f32[128,768]{1,0:T(8,128)}, u32[]{:S(2)}) copy-start(f32[128,768]{1,0:T(8,128)} %get-tuple-element.68) | copy-start | bytes 1179652
  223.0 7.1 %copy-start.13 = (f32[2,48,3072]{2,1,0:T(8,128)S(1)}, f32[2,48,3072]{2,1,0:T(8,128)}, u32[]{:S(2)}) copy-start(f32[2,48,3072]{2,1,0:T(8,128)} %get-tuple-element.74) | copy-start | bytes 3538948
  230.1 1.7 copy-start.12

commit v3 on v2

--- a/solution.py
+++ b/solution.py
@@ -31,6 +31,7 @@
         self.outer, self.inner = grid_of(size)
         self.chips = size // 2
         me = lax.axis_index("shard")
+        self.index = me
         self.core = lax.rem(me, 2)
         self.chip = lax.div(me, 2)
         self.z = lax.div(self.chip, self.inner)
@@ -260,8 +261,8 @@
         side = max(inner - 1, 1)
         return [
             pltpu.VMEM((outer, side) + block, LOW),
-            pltpu.VMEM((outer,) + block, LOW),
-            pltpu.VMEM((2, outer) + block, LOW),
+            pltpu.VMEM((max(outer - 1, 1),) + block, LOW),
+            pltpu.VMEM((outer + 1,) + block, LOW),
             pltpu.VMEM(block, WIDE),
             DMA((outer, side)),
             DMA((outer, side)),
@@ -279,12 +280,20 @@
             place.device(place.at(0, -e)),
         )
 
-    def along(self, far, way):
+    def slot(self, far, way, z):
+        return far if way == 0 else jnp.where(far == z, self.place.outer, far)
+
+    def leave(self, far):
+        return jnp.where(far < self.place.z, far, jnp.maximum(far - 1, 0))
+
+    def along(self, far, way, z=None):
         place = self.place
         target = place.chip + (place.inner if way == 0 else -place.inner)
+        if z is None:
+            z = place.z + (1 if way == 0 else -1)
         return remote(
-            self.z_out.at[far],
-            self.z_in.at[way, far],
+            self.z_out.at[self.leave(far)],
+            self.z_in.at[self.slot(far, way, z)],
             self.z_send.at[far],
             self.z_recv.at[way, far],
             place.device(target),
@@ -315,10 +324,10 @@
 
             @pl.when(more)
             def _(way=way):
-                self.along(far, way).wait_recv()
+                self.along(far, way, place.z).wait_recv()
 
                 def add(n, carry):
-                    acc[rows(n)] += self.z_in[way, far, rows(n)].astype(WIDE)
+                    acc[rows(n)] += self.z_in[self.slot(far, way, place.z), rows(n)].astype(WIDE)
                     return carry
 
                 lax.fori_loop(0, count, add, 0, unroll=True)
@@ -326,7 +335,7 @@
         if last:
             give()
             return
-        self.z_out[far] = acc[...].astype(LOW)
+        self.z_out[self.leave(far)] = acc[...].astype(LOW)
 
         @pl.when(far > place.z)
         def _():
@@ -352,13 +361,32 @@
         lax.fori_loop(0, place.outer, sent, 0)
 
 
-def front_kernel(
-    size,
+def shared_rows(depth, reps):
+    return depth * 5 // 256 * 16 if reps == 2 else 0
+
+
+def spot_of(section, pad):
+    return section * pad + (SMALL if section > 1 else 0)
+
+
+def placing(count, width, first):
+    row = lax.broadcasted_iota(jnp.int32, (count, width), 0)
+    col = lax.broadcasted_iota(jnp.int32, (count, width), 1)
+    return jnp.where(col == row + first, 1.0, 0.0).astype(LOW)
+
+
+def front_part(
+    place,
+    reps,
     heads,
+    more,
     tok_ref,
     in_ref,
     out_ref,
-    small_ref,
+    gain_ref,
+    router_ref,
+    table_ref,
+    here_ref,
     strip_ref,
     half_ref,
     bucket_ref,
@@ -381,6 +409,10 @@
     g_recv,
     c_send,
     c_recv,
+    e_send,
+    e_recv,
+    x_send,
+    x_recv,
     s_send,
     s_recv,
     d_send,
@@ -389,35 +421,67 @@
     h_recv,
     own_sem,
 ):
-    place = Place(size)
-    chips = place.chips
+    size, chips = place.size, place.chips
     core, chip = place.core, place.chip
     length, width = tok_ref.shape
     rows = out_ref.shape[0]
-    pad = w1_ref.shape[2]
+    pad = w1_ref.shape[3]
+    strip = w1_ref.shape[4]
     head_size = width // heads
-    mine = whole_ref.at[chip, core]
+    depth = whole_ref.shape[2]
+    shared = shared_rows(depth, reps)
+    rep = lax.axis_index("rep") if shared else 0
+    window = pl.ds(pl.multiple_of(shared * rep, 16), depth - shared)
     for k in range(3):
-        whole_ref[chip, core, k * pad : k * pad + rows, :] = in_ref[k]
-    whole_ref[chip, core, 3 * pad : 3 * pad + rows, :] = out_ref[...]
-    whole_ref[chip, core, 4 * pad : 4 * pad + SMALL, :] = small_ref[...]
-    place.greet(True, 1)
+        whole_ref[chip, core, spot_of(k, pad) : spot_of(k, pad) + rows, :] = in_ref[k]
+    whole_ref[chip, core, spot_of(3, pad) : spot_of(3, pad) + rows, :] = out_ref[...]
+    spot = placing(rows, width, place.index * rows)
+    table_rows = table_ref.shape[0]
+    here = jnp.broadcast_to(here_ref[...].astype(WIDE), (length, length))
+    lower = jnp.concatenate(
+        [
+            dot(table_ref[...], placing(table_rows, length, place.index * table_rows), TN),
+            jnp.transpose(here)[:heads],
+            jnp.zeros((heads, width - 2 * length), WIDE),
+        ],
+        axis=1,
+    )
+    small = jnp.concatenate(
+        [dot(gain_ref[...], spot), dot(router_ref[...], spot, TN), lower], axis=0
+    )
+    whole_ref[chip, core, 2 * pad : 2 * pad + SMALL, :] = small.astype(LOW)
+    place.greet(True, reps)
     partner = place.partner()
-    gather = Gather(place, mine, whole_ref.at[:, core], g_up, g_down, g_z, g_send, g_recv)
+    slots = whole_ref.at[:, core, window]
+    gather = Gather(place, slots.at[chip], slots, g_up, g_down, g_z, g_send, g_recv)
     gather.start()
 
     def dup(source):
-        return remote(
-            whole_ref.at[source, core],
-            whole_ref.at[source, core],
-            c_send.at[source],
-            c_recv.at[source],
-            partner,
-        )
+        block = whole_ref.at[source, core, window]
+        return remote(block, block, c_send.at[source], c_recv.at[source], partner)
+
+    def end(who):
+        return pl.ds(pl.multiple_of((depth - shared) * who, 16), shared)
+
+    def dup_end(source):
+        block = whole_ref.at[source, core, end(1 - rep)]
+        return remote(block, block, e_send.at[source], e_recv.at[source], partner)
+
+    def give(source, who):
+        block = whole_ref.at[source, core, end(who)]
+        target = {"rep": 1 - rep}
+        return remote(block, block, x_send.at[source], x_recv.at[source], target)
+
+    def strip_of(k):
+        if strip % 128 == 0 and rows == pad:
+            return strip_ref.at[:, :, pl.ds(pl.multiple_of(k * strip, 128), strip)]
+        return strip_ref.at[k]
 
     dup(chip).start()
+    if shared:
+        dup_end(chip).start()
     local = [
-        pltpu.make_async_copy(strip_ref.at[chip], w1_ref.at[chip, core], own_sem.at[0]),
+        pltpu.make_async_copy(strip_of(chip), w1_ref.at[:, chip, core], own_sem.at[0]),
         pltpu.make_async_copy(half_ref, w2_ref.at[:, core], own_sem.at[1]),
     ]
     for copy in local:
@@ -427,8 +491,23 @@
 
     def arrive(i, carry):
         j, e = place.pair(i)
-        dup(gather.arrive(j, e)).start()
+        source = gather.arrive(j, e)
+        if shared:
+            give(source, rep).start()
+        dup(source).start()
+        if shared:
+
+            @pl.when(i > 2)
+            def _():
+                take(i - 2)
+
         return carry
+
+    def take(i):
+        j, e = place.pair(i)
+        source = place.source(place.line(j), e)
+        give(source, 1 - rep).wait_recv()
+        dup_end(source).start()
 
     late = chips - 2 * (place.inner - 1)
     lax.fori_loop(1, late, arrive, 0)
@@ -437,8 +516,8 @@
         if i > 0:
             target = place.at(d, e)
             copy = remote(
-                strip_ref.at[target],
-                w1_ref.at[chip, core],
+                strip_of(target),
+                w1_ref.at[:, chip, core],
                 s_send.at[i],
                 s_recv.at[i],
                 place.device(target),
@@ -446,25 +525,27 @@
             copy.start()
             strips.append(copy)
     lax.fori_loop(late, chips, arrive, 0)
+    if shared:
+        for i in range(chips - 2, chips):
+            take(i)
 
     def other(source, carry):
-        remote(
-            whole_ref.at[source, core],
-            whole_ref.at[source, 1 - core],
-            c_send.at[source],
-            c_recv.at[source],
-            partner,
-        ).wait_recv()
+        block = whole_ref.at[source, 1 - core, window]
+        remote(block, block, c_send.at[source], c_recv.at[source], partner).wait_recv()
+        if shared:
+            block = whole_ref.at[source, 1 - core, end(1 - rep)]
+            remote(block, block, e_send.at[source], e_recv.at[source], partner).wait_recv()
         return carry
 
+    more(0)
     lax.fori_loop(0, chips, other, 0)
 
     total = jnp.zeros((SMALL, width), WIDE)
     for j in range(size):
-        total = total + whole_ref[j // 2, j % 2, 4 * pad : 4 * pad + SMALL, :].astype(WIDE)
+        total = total + whole_ref[j // 2, j % 2, 2 * pad : 2 * pad + SMALL, :].astype(WIDE)
     sum_ref[...] = total
     lines = [
-        whole_ref[k, core, 4 * pad : 4 * pad + SMALL, length : 2 * length].astype(WIDE)[4:5]
+        whole_ref[k, core, 2 * pad : 2 * pad + SMALL, length : 2 * length].astype(WIDE)[4:5]
         for k in range(chips)
     ]
     lines.append(jnp.zeros((length - chips, length), WIDE))
@@ -474,7 +555,7 @@
     normed = (inputs * rms_scale(inputs) * total[0:1]).astype(LOW)
     normed_ref[...] = normed
     for k in range(3):
-        proj_ref[k] = dot(normed, joined(whole_ref, k * pad, rows, pad)).astype(LOW)
+        proj_ref[k] = dot(normed, joined(whole_ref, spot_of(k, pad), rows, pad)).astype(LOW)
     spots = lax.broadcasted_iota(jnp.int32, (length, 2 * length), 0)
     onehot = jnp.where(bucket_ref[...] == spots, 1.0, 0.0).astype(LOW)
     table = total[:, :length].astype(LOW)
@@ -483,11 +564,11 @@
     across = lax.broadcasted_iota(jnp.int32, (length, length), 1)
     part_q = jnp.zeros((length, length), jnp.int32)
     part_k = jnp.zeros((length, length), jnp.int32)
-    end = jnp.int32(0)
+    bound = jnp.int32(0)
     for s in range(length_ref.shape[1]):
-        end = end + length_ref[0, s]
-        part_q = part_q + jnp.where(down >= end, 1, 0)
-        part_k = part_k + jnp.where(across >= end, 1, 0)
+        bound = bound + length_ref[0, s]
+        part_q = part_q + jnp.where(down >= bound, 1, 0)
+        part_k = part_k + jnp.where(across >= bound, 1, 0)
     allowed = part_q == part_k
     parts = []
     for h in range(heads):
@@ -502,7 +583,8 @@
         parts.append(dot(probs.astype(LOW), proj_ref[2, :, at]))
     context = jnp.concatenate(parts, axis=1).astype(LOW)
     context_ref[...] = context
-    hidden = inputs + dot(context, joined(whole_ref, 3 * pad, rows, pad))
+    more(1)
+    hidden = inputs + dot(context, joined(whole_ref, spot_of(3, pad), rows, pad))
     hidden_ref[...] = hidden
     ffn_ref[...] = (hidden * rms_scale(hidden) * total[1:2]).astype(LOW)
 
@@ -510,73 +592,53 @@
         return place.at(-lax.div(i, place.inner), -lax.rem(i, place.inner))
 
     def pass_on(i, carry):
-        block = w1_ref.at[moved(i), core]
+        block = w1_ref.at[:, moved(i), core]
         remote(block, block, s_send.at[i], s_recv.at[i], partner).wait_recv()
         remote(block, block, d_send.at[i], d_recv.at[i], partner).start()
         return carry
 
-    local[0].wait()
-    remote(w1_ref.at[chip, core], w1_ref.at[chip, core], d_send.at[0], d_recv.at[0], partner).start()
-    lax.fori_loop(1, chips, pass_on, 0)
+    def strips_on():
+        local[0].wait()
+        block = w1_ref.at[:, chip, core]
+        remote(block, block, d_send.at[0], d_recv.at[0], partner).start()
+        lax.fori_loop(1, chips, pass_on, 0)
 
     def last(i, carry):
         source = moved(i)
-        block = w1_ref.at[source, 1 - core]
-        sent = w1_ref.at[source, core]
+        block = w1_ref.at[:, source, 1 - core]
+        sent = w1_ref.at[:, source, core]
         remote(sent, block, d_send.at[i], d_recv.at[i], partner).wait()
         dup(source).wait_send()
+        if shared:
+            dup_end(source).wait_send()
         return carry
 
-    lax.fori_loop(0, chips, last, 0)
+    def strips_here():
+        lax.fori_loop(0, chips, last, 0)
+        local[1].wait()
+        halves.wait()
 
     def sent(i, carry):
-        remote(
-            strip_ref.at[0], w1_ref.at[chip, core], s_send.at[i], s_recv.at[i], partner
-        ).wait_send()
+        block = w1_ref.at[:, chip, core]
+        remote(block, block, s_send.at[i], s_recv.at[i], partner).wait_send()
+        if shared:
+            give(moved(i), rep).wait_send()
         return carry
 
-    lax.fori_loop(1, chips, sent, 0)
-    gather.finish()
-    local[1].wait()
-    halves.wait()
-
-
-def front(size, tokens, attn_in, attn_out, small, strips, halves, buckets, lengths, heads):
-    chips = size // 2
-    length, width = tokens.shape
-    rows = attn_out.shape[0]
-    pad = strips.shape[1]
-    cols = strips.shape[2]
-    depth = 4 * pad + SMALL
-    sems = [*Gather.sems(size), *[DMA((chips,))] * 6]
-    return pl.pallas_call(
-        functools.partial(front_kernel, size, heads),
-        out_shape=(
-            jax.ShapeDtypeStruct((chips, 2, depth, width), LOW),
-            jax.ShapeDtypeStruct((chips, 2, pad, cols), LOW),
-            jax.ShapeDtypeStruct((2, 2) + halves.shape[1:], LOW),
-            jax.ShapeDtypeStruct((length, width), LOW),
-            jax.ShapeDtypeStruct((3, length, width), LOW),
-            jax.ShapeDtypeStruct((heads, length, length), WIDE),
-            jax.ShapeDtypeStruct((length, width), LOW),
-            jax.ShapeDtypeStruct((length, width), WIDE),
-            jax.ShapeDtypeStruct((length, width), LOW),
-            jax.ShapeDtypeStruct((SMALL, width), WIDE),
-            jax.ShapeDtypeStruct((length, length), WIDE),
-        ),
-        in_specs=[VMEM] * 7 + [SMEM],
-        out_specs=[VMEM] * 11,
-        scratch_shapes=[*sems, DMA, DMA, DMA((2,))],
-        compiler_params=pltpu.CompilerParams(
-            collective_id=0, has_side_effects=True, vmem_limit_bytes=50 << 20
-        ),
-    )(tokens, attn_in, attn_out, small, strips, halves, buckets, lengths)
-
-
-def expert_kernel(
-    size,
+    def finish():
+        lax.fori_loop(1, chips, sent, 0)
+        gather.finish()
+
+    return strips_on, strips_here, finish
+
+
+def expert_part(
+    place,
     reps,
     rows,
+    strips_on,
+    strips_here,
+    u_gather,
     x_ref,
     u_ref,
     w1_ref,
@@ -591,14 +653,11 @@
     us,
     act,
     slope,
-    scaled,
     before_grad,
     ret_part,
     back_part,
     g1_own,
-    g1_got,
     g2_own,
-    g2_got,
     g2_all,
     p_send,
     p_recv,
@@ -607,21 +666,19 @@
     own_sem,
     *rest,
 ):
-    place = Place(size)
     chips, outer, inner = place.chips, place.outer, place.inner
     core, chip = place.core, place.chip
     rep = lax.axis_index("rep")
     length, width = x_ref.shape
-    cols = w1_ref.shape[1]
-    strip = cols // 2
+    strip = w1_ref.shape[4]
+    cols = 2 * strip
     pad = g1_own.shape[2]
-    place.greet(False, reps)
     partner = place.partner()
     x_gather = Gather(place, x_ref, xs, *rest[:5])
-    u_gather = Gather(place, u_ref, us, *rest[5:10])
-    ret_scatter = Scatter(place, ret_part, *rest[10:18])
-    back_scatter = Scatter(place, back_part, *rest[18:26])
+    ret_scatter = Scatter(place, ret_part, *rest[5:13])
+    back_scatter = Scatter(place, back_part, *rest[13:16], rest[8], *rest[16:20])
     x_gather.start()
+    strips_on()
     own = [
         pltpu.make_async_copy(x_ref, xs.at[chip], own_sem.at[0]),
         pltpu.make_async_copy(u_ref, us.at[chip], own_sem.at[1]),
@@ -630,6 +687,17 @@
         copy.start()
     for copy in own:
         copy.wait()
+    strips_here()
+
+    def w1_of(e):
+        if rows == pad:
+            return w1_ref[e].reshape(width, strip)
+        parts = [w1_ref[e, j // 2, j % 2, :rows].astype(WIDE) for j in range(chips * 2)]
+        return jnp.concatenate(parts, axis=0).astype(LOW)
+
+    def w2_of():
+        return w2_ref[...].reshape(cols, width)
+
     lane = lax.broadcasted_iota(jnp.int32, (length, length), 1)
     side = lax.broadcasted_iota(jnp.int32, (length, cols), 1) >= strip
     router = sum_ref[...].astype(LOW)
@@ -640,7 +708,7 @@
     def forward(i, carry):
         j, e = place.pair(i)
         k = x_gather.arrive(j, e)
-        before = dot(xs[k], w1_ref[...])
+        before = jnp.concatenate([dot(xs[k], w1_of(0)), dot(xs[k], w1_of(1))], axis=1)
         keep = jnp.logical_xor(side, route_of(k) < 0.5)
         square = before * before
         bent = jnp.tanh(0.7978845608 * before * (1.0 + 0.044715 * square))
@@ -651,12 +719,16 @@
         active = jnp.where(keep, before * half, 0.0).astype(LOW)
         act[k] = active
         slope[k] = jnp.where(keep, rise, 0.0)
-        ret_part[k] = dot(active, w2_ref[...]).astype(LOW)
+        ret_part[k] = dot(active, w2_of()).astype(LOW)
         return carry
 
     late = chips - 2 * (inner - 1)
-    lax.fori_loop(0, late, forward, 0)
-    u_gather.start()
+    lax.fori_loop(0, late // 2, forward, 0)
+    for j in range(2, outer - 1):
+        u_gather.arrive_z(j)
+    lax.fori_loop(late // 2, late, forward, 0)
+    if outer > 2:
+        u_gather.arrive_z(outer - 1)
     lax.fori_loop(late, chips, forward, 0)
 
     def ret_term(k, at):
@@ -671,26 +743,32 @@
     def back_give():
         back_ref[...] = back_scatter.acc[...]
 
-    for j in range(1, outer):
-        u_gather.arrive_z(j)
+    for j in range(outer - 1, -1, -1):
         for e in range(1, inner):
-            ret_scatter.across(place.line(outer - j), e).start()
-    for e in range(1, inner):
-        ret_scatter.across(place.line(0), e).start()
+            ret_scatter.across(place.line(j), e).start()
 
     def backward(j, e):
         k = place.source(place.line(j), e)
         gate = gate_of(dot(xs[k], router, NT), route_of(k))[2]
         low = (gate * us[k].astype(WIDE)).astype(LOW)
-        scaled[k] = low
-        grad = (dot(low, w2_ref[...], NT) * slope[k]).astype(LOW)
+        us[k] = low
+        grad = (dot(low, w2_of(), NT) * slope[k]).astype(LOW)
         before_grad[k] = grad
-        back_part[k] = dot(grad, w1_ref[...], NT).astype(LOW)
+        back_part[k] = (
+            dot(grad[:, :strip], w1_of(0), NT) + dot(grad[:, strip:], w1_of(1), NT)
+        ).astype(LOW)
+
+    def u_here(n, carry):
+        for e in range(1, inner):
+            u_gather.arrive_y(n, e)
+        return carry
+
+    lax.fori_loop(0, outer, u_here, 0)
+    u_gather.finish()
 
     def back_step(n, carry):
         j = outer - 1 - n
         for e in range(1, inner):
-            u_gather.arrive_y(j, e)
             backward(j, e)
             back_scatter.across(place.line(j), e).start()
 
@@ -706,14 +784,14 @@
     def flat(ref):
         return ref[...].reshape(chips * length, ref.shape[2])
 
-    g2 = dot(flat(act), flat(scaled), TN)
+    g2 = dot(flat(act), flat(us), TN)
     g2_own[...] = g2.astype(LOW).reshape(g2_own.shape)
-    g2_swap = remote(g2_own.at[:, 1 - core], g2_got, p_send.at[0], p_recv.at[0], partner)
+    g2_swap = remote(g2_own.at[:, 1 - core], g2_all.at[rep], p_send.at[0], p_recv.at[0], partner)
     g2_swap.start()
     for j in range(outer - 1, 1, -1):
         back_scatter.collect(j, False, back_term, None)
     g2_swap.wait()
-    g2_all[rep] = (g2_own[:, core].astype(WIDE) + g2_got[...].astype(WIDE)).astype(LOW)
+    g2_all[rep] = (g2_own[:, core].astype(WIDE) + g2_all[rep].astype(WIDE)).astype(LOW)
     swaps = []
     for f in range(1, reps):
         swaps.append(
@@ -728,13 +806,13 @@
         swaps[-1].start()
     g1 = dot(flat(xs), flat(before_grad), TN)
     split(g1_own, 0, rows, pad, g1)
-    g1_swap = remote(g1_own.at[:, 1 - core], g1_got, p_send.at[1], p_recv.at[1], partner)
+    g1_swap = remote(g1_own.at[:, 1 - core], g1_ref, p_send.at[1], p_recv.at[1], partner)
     g1_swap.start()
     if outer > 1:
         back_scatter.collect(1, False, back_term, None)
     ret_scatter.collect(0, True, ret_term, ret_give)
     g1_swap.wait()
-    g1_ref[...] = (g1_own[:, core].astype(WIDE) + g1_got[...].astype(WIDE)).astype(LOW)
+    g1_ref[...] = (g1_own[:, core].astype(WIDE) + g1_ref[...].astype(WIDE)).astype(LOW)
     for copy in swaps:
         copy.wait()
     value = g2_all[0].astype(WIDE)
@@ -742,61 +820,17 @@
         value = value + g2_all[r].astype(WIDE)
     g2_ref[...] = value
     back_scatter.collect(0, True, back_term, back_give)
-    x_gather.finish()
-    u_gather.finish()
-    ret_scatter.finish()
-    back_scatter.finish()
-
-
-def expert(size, reps, rows, pad, x, u, w1, w2, small, routes):
-    chips = size // 2
-    length, width = x.shape
-    cols = w1.shape[1]
-    half = cols // 4
-    block = (chips, length, width)
-    wide = (chips, length, cols)
-    return pl.pallas_call(
-        functools.partial(expert_kernel, size, reps, rows),
-        out_shape=(
-            jax.ShapeDtypeStruct((length, width), WIDE),
-            jax.ShapeDtypeStruct((length, width), WIDE),
-            jax.ShapeDtypeStruct((chips, pad, cols), LOW),
-            jax.ShapeDtypeStruct((2, half, width), WIDE),
-        ),
-        in_specs=[VMEM] * 6,
-        out_specs=[VMEM] * 4,
-        scratch_shapes=[
-            pltpu.VMEM(block, LOW),
-            pltpu.VMEM(block, LOW),
-            pltpu.VMEM(wide, LOW),
-            pltpu.VMEM(wide, WIDE),
-            pltpu.VMEM(block, LOW),
-            pltpu.VMEM(wide, LOW),
-            pltpu.VMEM(block, LOW),
-            pltpu.VMEM(block, LOW),
-            pltpu.VMEM((chips, 2, pad, cols), LOW),
-            pltpu.VMEM((chips, pad, cols), LOW),
-            pltpu.VMEM((2, 2, half, width), LOW),
-            pltpu.VMEM((2, half, width), LOW),
-            pltpu.VMEM((reps, 2, half, width), LOW),
-            DMA((2,)),
-            DMA((2,)),
-            DMA((max(reps - 1, 1),)),
-            DMA((max(reps - 1, 1),)),
-            DMA((2,)),
-            *Gather.sems(size),
-            *Gather.sems(size),
-            *Scatter.buffers(size, (length, width)),
-            *Scatter.buffers(size, (length, width)),
-        ],
-        compiler_params=pltpu.CompilerParams(
-            collective_id=1, has_side_effects=True, vmem_limit_bytes=56 << 20
-        ),
-    )(x, u, w1, w2, small, routes)
-
-
-def back_kernel(
-    size,
+
+    def finish():
+        x_gather.finish()
+        ret_scatter.finish()
+        back_scatter.finish()
+
+    return finish
+
+
+def back_part_of(
+    place,
     reps,
     heads,
     rows,
@@ -817,11 +851,12 @@
     g1_ref,
     layer_ref,
     input_ref,
-    mine_ref,
+    in_out_ref,
+    out_out_ref,
+    small_out_ref,
     g1_out_ref,
-    grads,
     got,
-    kept,
+    x_got,
     rep_all,
     strips,
     s_send,
@@ -832,19 +867,24 @@
     p_recv,
     r_send,
     r_recv,
+    x_send,
+    x_recv,
     own_sem,
     *rest,
 ):
-    place = Place(size)
+    size = place.size
     chips, outer, inner = place.chips, place.outer, place.inner
     core, chip = place.core, place.chip
     rep = lax.axis_index("rep")
     length, width = tok_ref.shape
     head_size = width // heads
-    depth = mine_ref.shape[0]
+    depth = got.shape[1]
     pad = (depth - SMALL) // 4
-    place.greet(True, reps)
+    shared = 0
+    lead = pl.multiple_of(shared * rep, 16) if shared else 0
+    window = pl.ds(lead, depth - shared)
     partner = place.partner()
+    grads = whole_ref
     moves = []
     own = pltpu.make_async_copy(g1_ref.at[chip], strips.at[rep, chip], own_sem)
     own.start()
@@ -892,8 +932,8 @@
         - hidden * (scale * scale * scale) * jnp.mean(bent * hidden, axis=1, keepdims=True)
     )
     attn_grad = hidden_grad.astype(LOW)
-    split(grads, 3 * pad, rows, pad, dot(context_ref[...], attn_grad, TN))
-    context_grad = dot(attn_grad, joined(whole_ref, 3 * pad, rows, pad), NT).astype(LOW)
+    context_grad = dot(attn_grad, joined(whole_ref, spot_of(3, pad), rows, pad), NT).astype(LOW)
+    split(grads, spot_of(3, pad), rows, pad, dot(context_ref[...], attn_grad, TN))
 
     row = lax.broadcasted_iota(jnp.int32, (length, length), 0)
     col = lax.broadcasted_iota(jnp.int32, (length, length), 1)
@@ -926,8 +966,8 @@
     normed_grad = jnp.zeros((length, width), WIDE)
     for k in range(3):
         projected = jnp.concatenate(parts[k], axis=1).astype(LOW)
-        split(grads, k * pad, rows, pad, dot(normed, projected, TN))
-        normed_grad = normed_grad + dot(projected, joined(whole_ref, k * pad, rows, pad), NT)
+        normed_grad = normed_grad + dot(projected, joined(whole_ref, spot_of(k, pad), rows, pad), NT)
+        split(grads, spot_of(k, pad), rows, pad, dot(normed, projected, TN))
     inputs = tok_ref[...].astype(WIDE)
     scale = rms_scale(inputs)
     gain_attn_grad = jnp.sum(normed_grad * inputs * scale, axis=0, keepdims=True)
@@ -943,9 +983,10 @@
         axis=0,
     ).astype(LOW)
     for j in range(size):
-        grads[j // 2, j % 2, 4 * pad : 4 * pad + SMALL, :] = small
-
-    scatter = Scatter(place, kept, *rest)
+        grads[j // 2, j % 2, 2 * pad : 2 * pad + SMALL, :] = small
+
+    kept = got
+    scatter = Scatter(place, kept.at[:, window], *rest)
 
     def swap(k):
         return remote(
@@ -963,6 +1004,48 @@
         - inputs * (scale * scale * scale) * jnp.mean(bent * inputs, axis=1, keepdims=True)
     )
 
+    def item(n):
+        side = max(inner - 1, 1)
+        j = n - outer * (inner - 1)
+        e = jnp.where(j < 0, 1 + lax.rem(n, side), 0)
+        j = outer - 1 - jnp.where(j < 0, lax.div(n, side), j)
+        return place.line(j), e
+
+    def end(who):
+        return pl.ds(pl.multiple_of((depth - shared) * who, 16), shared)
+
+    def give(k):
+        return remote(
+            kept.at[k, end(1 - rep)], x_got.at[k], x_send.at[k], x_recv.at[k], {"rep": 1 - rep}
+        )
+
+    def cross(n, carry):
+        @pl.when(n < chips)
+        def _():
+            far, e = item(n)
+            k = place.source(far, e)
+            swap(k).wait_recv()
+            kept[k] = (grads[k, core].astype(WIDE) + got[k].astype(WIDE)).astype(LOW)
+            if shared:
+                give(k).start()
+
+        @pl.when(n > 1)
+        def _():
+            far, e = item(n - 2)
+            k = place.source(far, e)
+            if shared:
+                give(k).wait_recv()
+                kept[k, end(rep)] = (
+                    kept[k, end(rep)].astype(WIDE) + x_got[k].astype(WIDE)
+                ).astype(LOW)
+
+            @pl.when(e > 0)
+            def _():
+                scatter.across(far, e).start()
+
+        return carry
+
+    lax.fori_loop(0, chips + 2, cross, 0)
     own.wait()
     for copy in moves:
         copy.wait_recv()
@@ -979,34 +1062,20 @@
         )
         turns[-1].start()
 
-    def cross(n, carry):
-        j = outer - 1 - n
-        far = place.line(j)
-        for e in range(1, inner):
-            k = place.source(far, e)
-            swap(k).wait_recv()
-            kept[k] = (grads[k, core].astype(WIDE) + got[k].astype(WIDE)).astype(LOW)
-            scatter.across(far, e).start()
+    def term(k, at):
+        at = pl.ds(pl.multiple_of(lead + at.start, 16), 16)
+        return kept[k, at].astype(WIDE)
+
+    def pass_on(n, carry):
+        scatter.collect(outer - 1 - n, False, term, None)
         return carry
 
-    lax.fori_loop(0, outer, cross, 0)
-
-    def term(k, at):
-        return grads[k, core, at].astype(WIDE) + got[k, at].astype(WIDE)
-
-    def pass_on(n, carry):
-        j = outer - 1 - n
-        swap(place.source(place.line(j), 0)).wait_recv()
-        scatter.collect(j, False, term, None)
-        return carry
-
     lax.fori_loop(0, outer - 1, pass_on, 0)
-    swap(chip).wait_recv()
-
-    def give():
+
+    def give_sum():
         rep_all[rep] = scatter.acc[...].astype(LOW)
 
-    scatter.collect(0, True, term, give)
+    scatter.collect(0, True, term, give_sum)
     swaps = []
     for f in range(1, reps):
         swaps.append(
@@ -1027,56 +1096,229 @@
         for r in range(1, reps):
             value = value + strips[r, k].astype(WIDE)
         for e in range(2):
-            g1_out_ref[e, :, k * strip : (k + 1) * strip] = value[:, e * strip : (e + 1) * strip]
+            g1_out_ref[e, :, k * strip : (k + 1) * strip] = value[
+                :rows, e * strip : (e + 1) * strip
+            ]
     for copy in swaps:
         copy.wait()
-    value = rep_all[0].astype(WIDE)
-    for r in range(1, reps):
-        value = value + rep_all[r].astype(WIDE)
-    mine_ref[...] = value
+    if shared:
+        both = depth - 2 * shared
+        value = jnp.concatenate(
+            [
+                rep_all[0, :shared].astype(WIDE),
+                rep_all[0, shared:].astype(WIDE) + rep_all[1, :both].astype(WIDE),
+                rep_all[1, both:].astype(WIDE),
+            ],
+            axis=0,
+        )
+    else:
+        value = rep_all[0].astype(WIDE)
+        for r in range(1, reps):
+            value = value + rep_all[r].astype(WIDE)
+    for k in range(3):
+        in_out_ref[k] = value[spot_of(k, pad) : spot_of(k, pad) + rows]
+    out_out_ref[...] = value[spot_of(3, pad) : spot_of(3, pad) + rows]
+    small_out_ref[...] = value[2 * pad : 2 * pad + SMALL]
     for copy in moves:
         copy.wait_send()
     for k in range(chips):
         swap(k).wait_send()
+        if shared:
+            give(k).wait_send()
     scatter.finish()
 
 
-def back(size, reps, heads, rows, *operands):
+def layer_kernel(size, reps, heads, counts, *refs):
+    groups = []
+    for count in counts:
+        groups.append(refs[:count])
+        refs = refs[count:]
+    inputs, outputs, loads, load_sem, front, front_sems, expert, u_sems, back = groups
+    tokens, cotangent, attn_in, attn_out, gains, router, table, routes = inputs[:8]
+    strips, halves, buckets, turned, lengths = inputs[8:]
+    layer_out, input_grad, in_out, out_out, small_out, g1_out, g2_out = outputs
+    whole, w1, w2, normed, proj, probs, context, hidden, ffn, totals, columns = front
+    x_local, u_local, returned, norm_grad, g1 = loads
+    place = Place(size)
+    rows = attn_out.shape[0]
+    u_gather = Gather(place, u_local, expert[1], *u_sems)
+    get = [
+        pltpu.make_async_copy(cotangent, u_local, load_sem[0].at[0]),
+        pltpu.make_async_copy(tokens, x_local, load_sem[0].at[1]),
+    ]
+    for copy in get:
+        copy.start()
+
+    def more(stage):
+        if stage == 0:
+            for copy in get:
+                copy.wait()
+            u_gather.start()
+        elif place.outer > 1:
+            u_gather.arrive_z(1)
+
+    strips_on, strips_here, front_finish = front_part(
+        place,
+        reps,
+        heads,
+        more,
+        x_local,
+        attn_in,
+        attn_out,
+        gains,
+        router,
+        table,
+        routes,
+        strips,
+        halves,
+        buckets,
+        lengths,
+        *front,
+        *front_sems,
+    )
+    expert_finish = expert_part(
+        place,
+        reps,
+        rows,
+        strips_on,
+        strips_here,
+        u_gather,
+        ffn,
+        u_local,
+        w1,
+        w2,
+        totals,
+        columns,
+        returned,
+        norm_grad,
+        g1,
+        g2_out,
+        *expert,
+    )
+    front_finish()
+    back_part_of(
+        place,
+        reps,
+        heads,
+        rows,
+        x_local,
+        u_local,
+        hidden,
+        ffn,
+        normed,
+        proj,
+        probs,
+        context,
+        whole,
+        totals,
+        routes,
+        turned,
+        returned,
+        norm_grad,
+        g1,
+        layer_out,
+        input_grad,
+        in_out,
+        out_out,
+        small_out,
+        g1_out,
+        *back,
+    )
+    expert_finish()
+
+
+def layer(size, reps, heads, pad, strip, *operands):
     chips = size // 2
     length, width = operands[0].shape
-    strips = operands[-1]
-    pad, cols = strips.shape[1:]
+    rows = operands[3].shape[0]
+    half = operands[9].shape[1]
+    cols = 2 * strip
     depth = 4 * pad + SMALL
-    block = (chips, depth, width)
+    block = (chips, length, width)
+    wide = (chips, length, cols)
+    row = (length, width)
+    weights = (chips, depth, width)
+    others = max(reps - 1, 1)
+    outputs = (
+        jax.ShapeDtypeStruct(row, LOW),
+        jax.ShapeDtypeStruct(row, WIDE),
+        jax.ShapeDtypeStruct((3, rows, width), WIDE),
+        jax.ShapeDtypeStruct((rows, width), WIDE),
+        jax.ShapeDtypeStruct((SMALL, width), WIDE),
+        jax.ShapeDtypeStruct((2, rows, chips * strip), WIDE),
+        jax.ShapeDtypeStruct((2, half, width), WIDE),
+    )
+    loads = [
+        pltpu.VMEM(row, LOW),
+        pltpu.VMEM(row, LOW),
+        pltpu.VMEM(row, WIDE),
+        pltpu.VMEM(row, WIDE),
+        pltpu.VMEM((chips, pad, cols), LOW),
+    ]
+    front = [
+        pltpu.VMEM((chips, 2, depth, width), LOW),
+        pltpu.VMEM((2, chips, 2, pad, strip), LOW),
+        pltpu.VMEM((2, 2, half, width), LOW),
+        pltpu.VMEM(row, LOW),
+        pltpu.VMEM((3,) + row, LOW),
+        pltpu.VMEM((heads, length, length), WIDE),
+        pltpu.VMEM(row, LOW),
+        pltpu.VMEM(row, WIDE),
+        pltpu.VMEM(row, LOW),
+        pltpu.VMEM((SMALL, width), WIDE),
+        pltpu.VMEM((length, length), WIDE),
+    ]
+    front_sems = [*Gather.sems(size), *[DMA((chips,))] * 10, DMA, DMA, DMA((2,))]
+    expert = [
+        pltpu.VMEM(block, LOW),
+        pltpu.VMEM(block, LOW),
+        pltpu.VMEM(wide, LOW),
+        pltpu.VMEM(wide, WIDE),
+        pltpu.VMEM(wide, LOW),
+        pltpu.VMEM(block, LOW),
+        pltpu.VMEM(block, LOW),
+        pltpu.VMEM((chips, 2, pad, cols), LOW),
+        pltpu.VMEM((2, 2, half, width), LOW),
+        pltpu.VMEM((reps, 2, half, width), LOW),
+        DMA((2,)),
+        DMA((2,)),
+        DMA((others,)),
+        DMA((others,)),
+        DMA((2,)),
+        *Gather.sems(size),
+        *Scatter.buffers(size, row),
+        *[item for n, item in enumerate(Scatter.buffers(size, row)) if n != 3],
+    ]
+    back = [
+        pltpu.VMEM(weights, LOW),
+        pltpu.VMEM((1, 16, width), LOW),
+        pltpu.VMEM((reps, depth, width), LOW),
+        pltpu.VMEM((reps, chips, pad, cols), LOW),
+        DMA((chips,)),
+        DMA((chips,)),
+        DMA((others,)),
+        DMA((others,)),
+        DMA((chips,)),
+        DMA((chips,)),
+        DMA((others,)),
+        DMA((others,)),
+        DMA((chips,)),
+        DMA((chips,)),
+        DMA,
+        *Scatter.buffers(size, (depth, width)),
+    ]
+    load_sem = [DMA((2,))]
+    scratch = [loads, load_sem, front, front_sems, expert, Gather.sems(size), back]
+    counts = [len(operands), len(outputs), *[len(group) for group in scratch]]
+    far = pl.BlockSpec(memory_space=pl.ANY)
     return pl.pallas_call(
-        functools.partial(back_kernel, size, reps, heads, rows),
-        out_shape=(
-            jax.ShapeDtypeStruct((length, width), LOW),
-            jax.ShapeDtypeStruct((length, width), WIDE),
-            jax.ShapeDtypeStruct((depth, width), WIDE),
-            jax.ShapeDtypeStruct((2, pad, chips * cols // 2), WIDE),
-        ),
-        in_specs=[VMEM] * len(operands),
-        out_specs=[VMEM] * 4,
-        scratch_shapes=[
-            pltpu.VMEM((chips, 2, depth, width), LOW),
-            pltpu.VMEM(block, LOW),
-            pltpu.VMEM(block, LOW),
-            pltpu.VMEM((reps, depth, width), LOW),
-            pltpu.VMEM((reps, chips, pad, cols), LOW),
-            DMA((chips,)),
-            DMA((chips,)),
-            DMA((max(reps - 1, 1),)),
-            DMA((max(reps - 1, 1),)),
-            DMA((chips,)),
-            DMA((chips,)),
-            DMA((max(reps - 1, 1),)),
-            DMA((max(reps - 1, 1),)),
-            DMA,
-            *Scatter.buffers(size, (depth, width)),
-        ],
+        functools.partial(layer_kernel, size, reps, heads, counts),
+        out_shape=outputs,
+        in_specs=[far, far, *[VMEM] * 6, far, far, VMEM, VMEM, SMEM],
+        out_specs=[VMEM] * len(outputs),
+        scratch_shapes=[item for group in scratch for item in group],
         compiler_params=pltpu.CompilerParams(
-            collective_id=2, has_side_effects=True, vmem_limit_bytes=56 << 20
+            collective_id=0, has_side_effects=True, vmem_limit_bytes=60 << 20
         ),
     )(*operands)
 
@@ -1108,69 +1350,32 @@
     half = expert_out.shape[1]
     me = lax.axis_index("shard")
 
-    small = jnp.zeros((SMALL, width), LOW)
-    small = lax.dynamic_update_slice(
-        small, jnp.concatenate([gains, router.T], axis=0), (0, me * rows)
-    )
-    table_block = lax.dynamic_update_slice(
-        jnp.zeros((heads, length), LOW), rel_table.T, (0, me * table_rows)
-    )
-    upper = small[:4]
-    lower = jnp.concatenate(
-        [
-            table_block,
-            jnp.broadcast_to(routes.reshape(1, length).astype(LOW), (heads, length)),
-            jnp.zeros((heads, width - 2 * length), LOW),
-        ],
-        axis=1,
-    )
-    small = jnp.concatenate([upper, lower], axis=0)
     buckets = jnp.pad(bucket_ids, (0, 1), constant_values=-1).reshape(1, 2 * length)
     turned = jnp.pad(bucket_ids[::-1], (0, 1), constant_values=-1).reshape(1, 2 * length)
-    strips = jnp.transpose(expert_in.reshape(2, rows, chips, strip), (2, 1, 0, 3))
-    strips = strips.reshape(chips, rows, 2 * strip)
-    strips = jnp.pad(strips, ((0, 0), (0, pad - rows), (0, 0)))
-    whole, w1, w2, normed, projected, probs, context, hidden, ffn, totals, columns = front(
+    strips = expert_in
+    if strip % 128 or pad != rows:
+        strips = jnp.transpose(expert_in.reshape(2, rows, chips, strip), (2, 0, 1, 3))
+        strips = jnp.pad(strips, ((0, 0), (0, 0), (0, pad - rows), (0, 0)))
+    layer_out, input_grad, in_shard, out_shard, sums, expert_in_grad, expert_out_grad = layer(
         size,
+        reps,
+        heads,
+        pad,
+        strip,
         tokens,
+        cotangent,
         attn_in,
         attn_out,
-        small,
+        gains,
+        router,
+        rel_table,
+        routes,
         strips,
         expert_out,
         buckets,
+        turned,
         lengths,
-        heads,
     )
-    w1 = w1[:, :, :rows].reshape(width, 2 * strip)
-    w2 = w2.reshape(2 * strip, width)
-    returned, norm_grad, strip_grad, expert_out_grad = expert(
-        size, reps, rows, pad, ffn, cotangent, w1, w2, totals, columns
-    )
-    layer_out, input_grad, mine, expert_in_grad = back(
-        size,
-        reps,
-        heads,
-        rows,
-        tokens,
-        cotangent,
-        hidden,
-        ffn,
-        normed,
-        projected,
-        probs,
-        context,
-        whole,
-        totals,
-        routes,
-        turned,
-        returned,
-        norm_grad,
-        strip_grad,
-    )
-    in_shard = mine[: 3 * pad].reshape(3, pad, width)[:, :rows]
-    out_shard = mine[3 * pad : 3 * pad + rows]
-    sums = mine[4 * pad :]
     picked = lax.dynamic_slice(sums, (0, me * rows), (4, rows))
     table_shard = lax.dynamic_slice(sums, (4, me * table_rows), (heads, table_rows)).T
     return (
@@ -1181,7 +1386,7 @@
         picked[:2],
         picked[2:].T,
         table_shard,
-        expert_in_grad[:, :rows],
+        expert_in_grad,
         expert_out_grad,
     )
 

time: 233 us -> 191 us (0.82)
  Pallas kernels: 211 us -> 173 us
  local copies, waits for them, and re-layouts: 19.7 us -> 15.8 us
    pallas_call x3 -> x1, Pallas kernels: 211 us -> 173 us  [layer(): pl.pallas_call(functools.partial(layer_kernel, size, reps, heads, counts)...]
    slice x4 -> x0, local copies, waits for them, and re-layouts: 4.32 us -> none  [the longest x1 1.93 us: shards(): in_shard = mine[:3 * pad].reshape(3, pad, width)[:, :rows]]
    unnamed x46 -> x19, local copies, waits for them, and re-layouts: 12.6 us -> 11.9 us
where the time goes in v3:
time: 191 us; the launch traced here: 190 us
  Pallas kernels  173 us (91%)
  local copies, waits for them, and re-layouts  15.8 us (8%)
    pallas_call x1, Pallas kernels, layer(): pl.pallas_call(functools.partial(layer_kernel, size, reps, heads, counts)...  173 us
    unnamed x19, local copies, waits for them, and re-layouts  11.9 us

profile of v3, /device:TPU:0, one launch (start us, length us, event | category | flops | bytes accessed | tf_op | source)
XLA Modules:
  0.0 190.0 jit_solution(17673754415396163281)
XLA Ops:
  0.6 0.8 reverse
  1.4 0.1 slice.9
  1.5 0.6 pad.8
  2.1 1.2 pad.7
  3.3 1.3 copy.21.refs_5_
  4.6 1.4 copy.22.refs_7_
  6.0 173.4 %shard_map.187 = (bf16[128,768]{1,0:T(8,128)(2,1)}, f32[128,768]{1,0:T(8,128)}, f32[3,48,768]{2,1,0:T(8,128)}, f32[48,768]{1,0:T(8,128)}, f32[16,768]{1,0:T(8,12...) custom-call(bf16[128,768]{1,0:T(8,128)(2,1)} %refs_0_.1, bf16[128,768]{1,0:T(8,128)(2,1)} %refs_1_.1, ...), custom_call_target="tpu_custom_call" | custom-call | tf_op jit(solution)/shard_map/pallas_call | solution.py:1314
  179.5 0.0 copy-start.2
  179.5 0.0 copy-start.3
  179.5 0.8 constant_dynamic-slice_fusion
  180.3 0.8 dynamic-slice_bitcast_fusion
  181.1 0.6 copy.23
  181.8 0.6 slice_bitcast_fusion
  182.3 0.0 copy-start.1
  182.3 1.7 copy.30
  184.1 1.8 copy.31
  185.8 0.0 copy-done.2
  185.8 0.8 copy.32
  186.6 0.0 copy-done.3
  186.6 0.7 copy.33
  187.2 0.0 copy-done.1
  187.3 1.0 copy.34
  188.3 0.7 copy-done
  188.9 1.0 copy.35
  (1 shorter events, 0.0 us)
Async XLA Ops:
  179.5 6.3 %copy-start.2 = (f32[3,48,768]{2,1,0:T(8,128)S(1)}, f32[3,48,768]{2,1,0:T(8,128)}, u32[]{:S(2)}) copy-start(f32[3,48,768]{2,1,0:T(8,128)} %get-tuple-element.45) | copy-start | bytes 1327108
  179.5 7.1 %copy-start.3 = (f32[48,768]{1,0:T(8,128)S(1)}, f32[48,768]{1,0:T(8,128)}, u32[]{:S(2)}) copy-start(f32[48,768]{1,0:T(8,128)} %get-tuple-element.46) | copy-start | bytes 442372
  182.3 4.9 %copy-start.1 = (f32[2,48,3072]{2,1,0:T(8,128)S(1)}, f32[2,48,3072]{2,1,0:T(8,128)}, u32[]{:S(2)}) copy-start(f32[2,48,3072]{2,1,0:T(8,128)} %get-tuple-element.50) | copy-start | bytes 3538948
  187.3 1.7 copy-start

commit v4 on v3

--- a/solution.py
+++ b/solution.py
@@ -367,6 +367,15 @@
 
 def spot_of(section, pad):
     return section * pad + (SMALL if section > 1 else 0)
+
+
+def padded(ref):
+    return jnp.concatenate([ref[...], jnp.full((1, 1), -1, jnp.int32)], axis=1)
+
+
+def column(line):
+    count = line.shape[1]
+    return jnp.transpose(jnp.broadcast_to(line, (count, count)))[:, :1]
 
 
 def placing(count, width, first):
@@ -415,6 +424,10 @@
     x_recv,
     s_send,
     s_recv,
+    f_send,
+    f_recv,
+    n_send,
+    n_recv,
     d_send,
     d_recv,
     h_send,
@@ -437,17 +450,17 @@
     whole_ref[chip, core, spot_of(3, pad) : spot_of(3, pad) + rows, :] = out_ref[...]
     spot = placing(rows, width, place.index * rows)
     table_rows = table_ref.shape[0]
-    here = jnp.broadcast_to(here_ref[...].astype(WIDE), (length, length))
+    here = jnp.broadcast_to(here_ref[...].astype(WIDE), (heads, length))
     lower = jnp.concatenate(
         [
             dot(table_ref[...], placing(table_rows, length, place.index * table_rows), TN),
-            jnp.transpose(here)[:heads],
+            here,
             jnp.zeros((heads, width - 2 * length), WIDE),
         ],
         axis=1,
     )
     small = jnp.concatenate(
-        [dot(gain_ref[...], spot), dot(router_ref[...], spot, TN), lower], axis=0
+        [dot(gain_ref[...], spot), dot(router_ref[...], spot), lower], axis=0
     )
     whole_ref[chip, core, 2 * pad : 2 * pad + SMALL, :] = small.astype(LOW)
     place.greet(True, reps)
@@ -472,16 +485,21 @@
         target = {"rep": 1 - rep}
         return remote(block, block, x_send.at[source], x_recv.at[source], target)
 
-    def strip_of(k):
+    swapped = shared and strip % 128 == 0 and rows == pad
+
+    def strip_of(k, which):
         if strip % 128 == 0 and rows == pad:
-            return strip_ref.at[:, :, pl.ds(pl.multiple_of(k * strip, 128), strip)]
+            return strip_ref.at[which, :, pl.ds(pl.multiple_of(k * strip, 128), strip)]
         return strip_ref.at[k]
+
+    mine = rep if swapped else slice(None)
+    theirs = 1 - rep
 
     dup(chip).start()
     if shared:
         dup_end(chip).start()
     local = [
-        pltpu.make_async_copy(strip_of(chip), w1_ref.at[:, chip, core], own_sem.at[0]),
+        pltpu.make_async_copy(strip_of(chip, slice(None)), w1_ref.at[:, chip, core], own_sem.at[0]),
         pltpu.make_async_copy(half_ref, w2_ref.at[:, core], own_sem.at[1]),
     ]
     for copy in local:
@@ -516,8 +534,8 @@
         if i > 0:
             target = place.at(d, e)
             copy = remote(
-                strip_of(target),
-                w1_ref.at[:, chip, core],
+                strip_of(target, mine),
+                w1_ref.at[mine, chip, core],
                 s_send.at[i],
                 s_recv.at[i],
                 place.device(target),
@@ -557,7 +575,7 @@
     for k in range(3):
         proj_ref[k] = dot(normed, joined(whole_ref, spot_of(k, pad), rows, pad)).astype(LOW)
     spots = lax.broadcasted_iota(jnp.int32, (length, 2 * length), 0)
-    onehot = jnp.where(bucket_ref[...] == spots, 1.0, 0.0).astype(LOW)
+    onehot = jnp.where(padded(bucket_ref) == spots, 1.0, 0.0).astype(LOW)
     table = total[:, :length].astype(LOW)
     bias = dot(table, onehot)
     down = lax.broadcasted_iota(jnp.int32, (length, length), 0)
@@ -570,8 +588,73 @@
         part_q = part_q + jnp.where(down >= bound, 1, 0)
         part_k = part_k + jnp.where(across >= bound, 1, 0)
     allowed = part_q == part_k
+    def moved(i):
+        return place.at(-lax.div(i, place.inner), -lax.rem(i, place.inner))
+
+    def along_x(i, which):
+        block = w1_ref.at[which, moved(i), core]
+        return remote(block, block, f_send.at[i], f_recv.at[i], {"rep": theirs})
+
+    def to_partner(block, i, send, recv):
+        return remote(block, block, send.at[i], recv.at[i], partner)
+
+    def pass_on(i, carry):
+        block = w1_ref.at[mine, moved(i), core]
+        remote(block, block, s_send.at[i], s_recv.at[i], partner).wait_recv()
+        if swapped:
+            along_x(i, rep).start()
+        to_partner(block, i, d_send, d_recv).start()
+        return carry
+
+    def pass_last(i, carry):
+        along_x(i, theirs).wait_recv()
+        to_partner(w1_ref.at[theirs, moved(i), core], i, n_send, n_recv).start()
+        return carry
+
+    def strips_on(stage):
+        if stage == 0:
+            local[0].wait()
+            to_partner(w1_ref.at[:, chip, core], 0, d_send, d_recv).start()
+            lax.fori_loop(1, chips, pass_on, 0)
+        elif swapped:
+            lax.fori_loop(1, chips, pass_last, 0)
+
+    def last(i, carry):
+        source = moved(i)
+
+        @pl.when(i > 0)
+        def _():
+            to_partner(w1_ref.at[mine, source, core], i, d_send, d_recv).wait_send()
+            to_partner(w1_ref.at[mine, source, 1 - core], i, d_send, d_recv).wait_recv()
+            if swapped:
+                to_partner(w1_ref.at[theirs, source, core], i, n_send, n_recv).wait_send()
+                to_partner(w1_ref.at[theirs, source, 1 - core], i, n_send, n_recv).wait_recv()
+
+        dup(source).wait_send()
+        if shared:
+            dup_end(source).wait_send()
+        return carry
+
+    def strips_here():
+        to_partner(w1_ref.at[:, chip, core], 0, d_send, d_recv).wait_send()
+        to_partner(w1_ref.at[:, chip, 1 - core], 0, d_send, d_recv).wait_recv()
+        lax.fori_loop(0, chips, last, 0)
+        local[1].wait()
+        halves.wait()
+
+    def sent(i, carry):
+        block = w1_ref.at[mine, chip, core]
+        remote(block, block, s_send.at[i], s_recv.at[i], partner).wait_send()
+        if shared:
+            give(moved(i), rep).wait_send()
+        if swapped:
+            along_x(i, rep).wait_send()
+        return carry
+
     parts = []
     for h in range(heads):
+        if h == 2 * heads // 3:
+            more(1, strips_on)
         at = slice(h * head_size, (h + 1) * head_size)
         raw = dot(proj_ref[0, :, at], proj_ref[1, :, at], NT)
         spread = jnp.broadcast_to(bias[4 + h : 5 + h, :], (length, 2 * length))
@@ -583,47 +666,9 @@
         parts.append(dot(probs.astype(LOW), proj_ref[2, :, at]))
     context = jnp.concatenate(parts, axis=1).astype(LOW)
     context_ref[...] = context
-    more(1)
     hidden = inputs + dot(context, joined(whole_ref, spot_of(3, pad), rows, pad))
     hidden_ref[...] = hidden
     ffn_ref[...] = (hidden * rms_scale(hidden) * total[1:2]).astype(LOW)
-
-    def moved(i):
-        return place.at(-lax.div(i, place.inner), -lax.rem(i, place.inner))
-
-    def pass_on(i, carry):
-        block = w1_ref.at[:, moved(i), core]
-        remote(block, block, s_send.at[i], s_recv.at[i], partner).wait_recv()
-        remote(block, block, d_send.at[i], d_recv.at[i], partner).start()
-        return carry
-
-    def strips_on():
-        local[0].wait()
-        block = w1_ref.at[:, chip, core]
-        remote(block, block, d_send.at[0], d_recv.at[0], partner).start()
-        lax.fori_loop(1, chips, pass_on, 0)
-
-    def last(i, carry):
-        source = moved(i)
-        block = w1_ref.at[:, source, 1 - core]
-        sent = w1_ref.at[:, source, core]
-        remote(sent, block, d_send.at[i], d_recv.at[i], partner).wait()
-        dup(source).wait_send()
-        if shared:
-            dup_end(source).wait_send()
-        return carry
-
-    def strips_here():
-        lax.fori_loop(0, chips, last, 0)
-        local[1].wait()
-        halves.wait()
-
-    def sent(i, carry):
-        block = w1_ref.at[:, chip, core]
-        remote(block, block, s_send.at[i], s_recv.at[i], partner).wait_send()
-        if shared:
-            give(moved(i), rep).wait_send()
-        return carry
 
     def finish():
         lax.fori_loop(1, chips, sent, 0)
@@ -647,6 +692,7 @@
     route_ref,
     ret_ref,
     back_ref,
+    router_ref,
     g1_ref,
     g2_ref,
     xs,
@@ -675,10 +721,10 @@
     pad = g1_own.shape[2]
     partner = place.partner()
     x_gather = Gather(place, x_ref, xs, *rest[:5])
-    ret_scatter = Scatter(place, ret_part, *rest[5:13])
-    back_scatter = Scatter(place, back_part, *rest[13:16], rest[8], *rest[16:20])
+    back_scatter = Scatter(place, back_part, *rest[5:13])
+    ret_scatter = Scatter(place, ret_part, *rest[13:16], rest[8], *rest[16:20])
     x_gather.start()
-    strips_on()
+    strips_on(1)
     own = [
         pltpu.make_async_copy(x_ref, xs.at[chip], own_sem.at[0]),
         pltpu.make_async_copy(u_ref, us.at[chip], own_sem.at[1]),
@@ -687,6 +733,8 @@
         copy.start()
     for copy in own:
         copy.wait()
+    for j in range(2, outer - 1):
+        u_gather.arrive_z(j)
     strips_here()
 
     def w1_of(e):
@@ -724,12 +772,9 @@
 
     late = chips - 2 * (inner - 1)
     lax.fori_loop(0, late // 2, forward, 0)
-    for j in range(2, outer - 1):
-        u_gather.arrive_z(j)
-    lax.fori_loop(late // 2, late, forward, 0)
     if outer > 2:
         u_gather.arrive_z(outer - 1)
-    lax.fori_loop(late, chips, forward, 0)
+    lax.fori_loop(late // 2, chips, forward, 0)
 
     def ret_term(k, at):
         return ret_part[k, at].astype(WIDE)
@@ -743,26 +788,42 @@
     def back_give():
         back_ref[...] = back_scatter.acc[...]
 
-    for j in range(outer - 1, -1, -1):
-        for e in range(1, inner):
-            ret_scatter.across(place.line(j), e).start()
+    def ret_collect(j):
+        ret_scatter.collect(j, j == 0, ret_term, ret_give)
+
 
     def backward(j, e):
         k = place.source(place.line(j), e)
-        gate = gate_of(dot(xs[k], router, NT), route_of(k))[2]
-        low = (gate * us[k].astype(WIDE)).astype(LOW)
-        us[k] = low
-        grad = (dot(low, w2_of(), NT) * slope[k]).astype(LOW)
+        route = route_of(k)
+        first, second, gate = gate_of(dot(xs[k], router, NT), route)
+        pulled = dot(us[k], w2_of(), NT)
+        us[k] = (gate * us[k].astype(WIDE)).astype(LOW)
+        gate_grad = jnp.sum(act[k].astype(WIDE) * pulled, axis=1, keepdims=True)
+        grad = (gate * pulled * slope[k]).astype(LOW)
         before_grad[k] = grad
+        shared = gate * gate_grad
+        first = first * (jnp.where(route > 0.5, 0.0, gate_grad) - shared)
+        second = second * (jnp.where(route > 0.5, gate_grad, 0.0) - shared)
+        tokens = xs[k].astype(WIDE)
+        router_ref[0:1] += jnp.sum(tokens * first, axis=0, keepdims=True)
+        router_ref[1:2] += jnp.sum(tokens * second, axis=0, keepdims=True)
         back_part[k] = (
-            dot(grad[:, :strip], w1_of(0), NT) + dot(grad[:, strip:], w1_of(1), NT)
+            dot(grad[:, :strip], w1_of(0), NT)
+            + dot(grad[:, strip:], w1_of(1), NT)
+            + first * sum_ref[2:3, :]
+            + second * sum_ref[3:4, :]
         ).astype(LOW)
+
+    router_ref[...] = jnp.zeros_like(router_ref)
 
     def u_here(n, carry):
         for e in range(1, inner):
             u_gather.arrive_y(n, e)
         return carry
 
+    early = outer - 1 if outer > 1 else 0
+    for e in range(1, inner):
+        ret_scatter.across(place.line(early), e).start()
     lax.fori_loop(0, outer, u_here, 0)
     u_gather.finish()
 
@@ -771,15 +832,13 @@
         for e in range(1, inner):
             backward(j, e)
             back_scatter.across(place.line(j), e).start()
-
-        @pl.when(j > 0)
-        def _():
-            ret_scatter.collect(j, False, ret_term, None)
-
         backward(j, 0)
         return carry
 
     lax.fori_loop(0, outer, back_step, 0)
+    for j in range(early - 1, -1, -1):
+        for e in range(1, inner):
+            ret_scatter.across(place.line(j), e).start()
 
     def flat(ref):
         return ref[...].reshape(chips * length, ref.shape[2])
@@ -810,23 +869,22 @@
     g1_swap.start()
     if outer > 1:
         back_scatter.collect(1, False, back_term, None)
-    ret_scatter.collect(0, True, ret_term, ret_give)
+    back_scatter.collect(0, True, back_term, back_give)
     g1_swap.wait()
     g1_ref[...] = (g1_own[:, core].astype(WIDE) + g1_ref[...].astype(WIDE)).astype(LOW)
-    for copy in swaps:
-        copy.wait()
-    value = g2_all[0].astype(WIDE)
-    for r in range(1, reps):
-        value = value + g2_all[r].astype(WIDE)
-    g2_ref[...] = value
-    back_scatter.collect(0, True, back_term, back_give)
 
     def finish():
+        for copy in swaps:
+            copy.wait()
+        value = g2_all[0].astype(WIDE)
+        for r in range(1, reps):
+            value = value + g2_all[r].astype(WIDE)
+        g2_ref[...] = value
         x_gather.finish()
         ret_scatter.finish()
         back_scatter.finish()
 
-    return finish
+    return ret_collect, finish
 
 
 def back_part_of(
@@ -845,9 +903,11 @@
     whole_ref,
     sum_ref,
     route_ref,
-    turned_ref,
+    bucket_ref,
+    ret_collect,
     ret_ref,
     norm_ref,
+    router_ref,
     g1_ref,
     layer_ref,
     input_ref,
@@ -857,6 +917,7 @@
     g1_out_ref,
     got,
     x_got,
+    g1_got,
     rep_all,
     strips,
     s_send,
@@ -885,44 +946,51 @@
     window = pl.ds(lead, depth - shared)
     partner = place.partner()
     grads = whole_ref
+    strip = g1_ref.shape[2] // 2
+    swapped = reps == 2 and strip % 128 == 0
+
+    def half(which):
+        return pl.ds(pl.multiple_of(which * strip, 128), strip)
+
+    g1_swap = remote(
+        g1_ref.at[:, :, half(1 - rep)] if swapped else g1_ref,
+        g1_got if swapped else g1_ref,
+        x_send.at[0],
+        x_recv.at[0],
+        {"rep": lax.rem(rep + 1, reps)},
+    )
+    if swapped:
+        g1_swap.start()
     moves = []
-    own = pltpu.make_async_copy(g1_ref.at[chip], strips.at[rep, chip], own_sem)
-    own.start()
+    origin = g1_got if swapped else g1_ref
+    own = pltpu.make_async_copy(origin.at[chip], strips.at[rep, chip], own_sem)
     for i, (d, e) in enumerate(place.pairs()):
         if i > 0:
             target = place.at(d, e)
             moves.append(
                 remote(
-                    g1_ref.at[target],
+                    origin.at[target],
                     strips.at[rep, chip],
                     s_send.at[i],
                     s_recv.at[i],
                     place.device(target),
                 )
             )
-            moves[-1].start()
-
-    router = sum_ref[2:4, :]
+
+    def strips_off():
+        if swapped:
+            g1_swap.wait()
+            g1_got[...] = (
+                g1_got[...].astype(WIDE) + g1_ref[:, :, half(rep)].astype(WIDE)
+            ).astype(LOW)
+        for copy in [own, *moves]:
+            copy.start()
+
     upstream = u_ref[...].astype(WIDE)
     hidden = hidden_ref[...]
-    returned = ret_ref[...]
-    route = route_ref[...].astype(WIDE)
-    logits = dot(ffn_ref[...], sum_ref[...].astype(LOW), NT)
-    first, second, gate = gate_of(logits, route)
-    layer_ref[...] = (hidden + gate * returned).astype(LOW)
-    gate_grad = jnp.sum(upstream * returned, axis=1, keepdims=True)
-    scaled = gate * gate_grad
-    first_grad = first * (jnp.where(route > 0.5, 0.0, gate_grad) - scaled)
-    second_grad = second * (jnp.where(route > 0.5, gate_grad, 0.0) - scaled)
-    ffn = ffn_ref[...].astype(WIDE)
-    router_grad = jnp.concatenate(
-        [
-            jnp.sum(ffn * first_grad, axis=0, keepdims=True),
-            jnp.sum(ffn * second_grad, axis=0, keepdims=True),
-        ],
-        axis=0,
-    )
-    norm_grad = norm_ref[...] + first_grad * router[0:1] + second_grad * router[1:2]
+    route = column(route_ref[...].astype(WIDE))
+    gate = gate_of(dot(ffn_ref[...], sum_ref[...].astype(LOW), NT), route)[2]
+    norm_grad = norm_ref[...]
     scale = rms_scale(hidden)
     gain_ffn_grad = jnp.sum(norm_grad * hidden * scale, axis=0, keepdims=True)
     bent = norm_grad * sum_ref[1:2, :]
@@ -942,13 +1010,15 @@
     parts = [[], [], []]
     diagonals = []
     for h in range(heads):
+        if h in (heads // 3, 5 * heads // 6) and outer > 2:
+            ret_collect(outer - 1 if h == heads // 3 else outer - 2)
         at = slice(h * head_size, (h + 1) * head_size)
         grad = context_grad[:, at]
         probs = probs_ref[h]
         prob_grad = dot(grad, proj_ref[2, :, at], NT)
         summed = jnp.sum(probs * prob_grad, axis=1, keepdims=True)
         low = (probs * (prob_grad - summed)).astype(LOW)
-        flipped = dot(low, mirror)
+        flipped = dot(mirror, low)
         skewed = pltpu.roll(
             jnp.concatenate([flipped, blank], axis=1), 0, 1, stride=1, stride_axis=0
         )
@@ -958,7 +1028,7 @@
         parts[2].append(dot(probs.astype(LOW), grad, TN))
     diagonal = jnp.concatenate(diagonals, axis=0)
     spots = lax.broadcasted_iota(jnp.int32, (length, 2 * length), 0)
-    onehot = jnp.where(turned_ref[...] == spots, 1.0, 0.0).astype(LOW)
+    onehot = jnp.where(padded(bucket_ref) == spots, 1.0, 0.0).astype(LOW)
     high = diagonal.astype(LOW)
     below = (diagonal - high.astype(WIDE)).astype(LOW)
     table_grad = dot(high, onehot, NT) + dot(below, onehot, NT)
@@ -975,7 +1045,7 @@
         [
             gain_attn_grad,
             gain_ffn_grad,
-            router_grad,
+            router_ref[0:2, :],
             jnp.concatenate(
                 [table_grad, jnp.zeros((heads, width - length), WIDE)], axis=1
             ),
@@ -1045,7 +1115,11 @@
 
         return carry
 
+    strips_off()
     lax.fori_loop(0, chips + 2, cross, 0)
+    for j in range(outer - 3 if outer > 2 else outer - 1, -1, -1):
+        ret_collect(j)
+    layer_ref[...] = (hidden + gate * ret_ref[...]).astype(LOW)
     own.wait()
     for copy in moves:
         copy.wait_recv()
@@ -1090,8 +1164,11 @@
         swaps[-1].start()
     for copy in turns:
         copy.wait()
-    strip = g1_ref.shape[2] // 2
     for k in range(chips):
+        if swapped:
+            for e in range(2):
+                g1_out_ref[e, :, k * strip : (k + 1) * strip] = strips[e, k].astype(WIDE)
+            continue
         value = strips[0, k].astype(WIDE)
         for r in range(1, reps):
             value = value + strips[r, k].astype(WIDE)
@@ -1135,10 +1212,10 @@
         refs = refs[count:]
     inputs, outputs, loads, load_sem, front, front_sems, expert, u_sems, back = groups
     tokens, cotangent, attn_in, attn_out, gains, router, table, routes = inputs[:8]
-    strips, halves, buckets, turned, lengths = inputs[8:]
+    strips, halves, buckets, lengths = inputs[8:]
     layer_out, input_grad, in_out, out_out, small_out, g1_out, g2_out = outputs
     whole, w1, w2, normed, proj, probs, context, hidden, ffn, totals, columns = front
-    x_local, u_local, returned, norm_grad, g1 = loads
+    x_local, u_local, returned, norm_grad, router_grad, g1 = loads
     place = Place(size)
     rows = attn_out.shape[0]
     u_gather = Gather(place, u_local, expert[1], *u_sems)
@@ -1149,13 +1226,15 @@
     for copy in get:
         copy.start()
 
-    def more(stage):
+    def more(stage, strips_on=None):
         if stage == 0:
             for copy in get:
                 copy.wait()
             u_gather.start()
         elif place.outer > 1:
             u_gather.arrive_z(1)
+        if stage == 1:
+            strips_on(0)
 
     strips_on, strips_here, front_finish = front_part(
         place,
@@ -1176,7 +1255,7 @@
         *front,
         *front_sems,
     )
-    expert_finish = expert_part(
+    ret_collect, expert_finish = expert_part(
         place,
         reps,
         rows,
@@ -1191,6 +1270,7 @@
         columns,
         returned,
         norm_grad,
+        router_grad,
         g1,
         g2_out,
         *expert,
@@ -1212,9 +1292,11 @@
         whole,
         totals,
         routes,
-        turned,
+        buckets,
+        ret_collect,
         returned,
         norm_grad,
+        router_grad,
         g1,
         layer_out,
         input_grad,
@@ -1239,6 +1321,7 @@
     row = (length, width)
     weights = (chips, depth, width)
     others = max(reps - 1, 1)
+    swapped = reps == 2 and strip % 128 == 0
     outputs = (
         jax.ShapeDtypeStruct(row, LOW),
         jax.ShapeDtypeStruct(row, WIDE),
@@ -1253,6 +1336,7 @@
         pltpu.VMEM(row, LOW),
         pltpu.VMEM(row, WIDE),
         pltpu.VMEM(row, WIDE),
+        pltpu.VMEM((8, width), WIDE),
         pltpu.VMEM((chips, pad, cols), LOW),
     ]
     front = [
@@ -1268,7 +1352,7 @@
         pltpu.VMEM((SMALL, width), WIDE),
         pltpu.VMEM((length, length), WIDE),
     ]
-    front_sems = [*Gather.sems(size), *[DMA((chips,))] * 10, DMA, DMA, DMA((2,))]
+    front_sems = [*Gather.sems(size), *[DMA((chips,))] * 14, DMA, DMA, DMA((2,))]
     expert = [
         pltpu.VMEM(block, LOW),
         pltpu.VMEM(block, LOW),
@@ -1292,8 +1376,9 @@
     back = [
         pltpu.VMEM(weights, LOW),
         pltpu.VMEM((1, 16, width), LOW),
+        pltpu.VMEM((chips, pad, strip) if swapped else (1, 16, 128), LOW),
         pltpu.VMEM((reps, depth, width), LOW),
-        pltpu.VMEM((reps, chips, pad, cols), LOW),
+        pltpu.VMEM((reps, chips, pad, strip if swapped else cols), LOW),
         DMA((chips,)),
         DMA((chips,)),
         DMA((others,)),
@@ -1314,11 +1399,11 @@
     return pl.pallas_call(
         functools.partial(layer_kernel, size, reps, heads, counts),
         out_shape=outputs,
-        in_specs=[far, far, *[VMEM] * 6, far, far, VMEM, VMEM, SMEM],
+        in_specs=[far, far, *[VMEM] * 6, far, far, VMEM, SMEM],
         out_specs=[VMEM] * len(outputs),
         scratch_shapes=[item for group in scratch for item in group],
         compiler_params=pltpu.CompilerParams(
-            collective_id=0, has_side_effects=True, vmem_limit_bytes=60 << 20
+            collective_id=0, has_side_effects=True, vmem_limit_bytes=62 << 20
         ),
     )(*operands)
 
@@ -1350,8 +1435,6 @@
     half = expert_out.shape[1]
     me = lax.axis_index("shard")
 
-    buckets = jnp.pad(bucket_ids, (0, 1), constant_values=-1).reshape(1, 2 * length)
-    turned = jnp.pad(bucket_ids[::-1], (0, 1), constant_values=-1).reshape(1, 2 * length)
     strips = expert_in
     if strip % 128 or pad != rows:
         strips = jnp.transpose(expert_in.reshape(2, rows, chips, strip), (2, 0, 1, 3))
@@ -1367,13 +1450,12 @@
         attn_in,
         attn_out,
         gains,
-        router,
+        router.T,
         rel_table,
-        routes,
+        routes.reshape(1, -1),
         strips,
         expert_out,
-        buckets,
-        turned,
+        bucket_ids.reshape(1, -1),
         lengths,
     )
     picked = lax.dynamic_slice(sums, (0, me * rows), (4, rows))

time: 191 us -> 176 us (0.921)
  Pallas kernels: 173 us -> 164 us
  local copies, waits for them, and re-layouts: 15.8 us -> 10.4 us
    pallas_call x1, Pallas kernels: 173 us -> 164 us  [layer(): pl.pallas_call(functools.partial(layer_kernel, size, reps, heads, counts)...]
    unnamed x19 -> x15, local copies, waits for them, and re-layouts: 11.9 us -> 8.27 us
where the time goes in v4:
time: 176 us; the launch traced here: 175 us
  Pallas kernels  164 us (93%)
  local copies, waits for them, and re-layouts  10.4 us (6%)
    pallas_call x1, Pallas kernels, layer(): pl.pallas_call(functools.partial(layer_kernel, size, reps, heads, counts)...  164 us
    unnamed x15, local copies, waits for them, and re-layouts  8.27 us

profile of v4, /device:TPU:0, one launch (start us, length us, event | category | flops | bytes accessed | tf_op | source)
XLA Modules:
  0.0 175.3 jit_solution(15251897271015711002)
XLA Ops:
  0.7 164.2 %shard_map.187 = (bf16[128,768]{1,0:T(8,128)(2,1)}, f32[128,768]{1,0:T(8,128)}, f32[3,48,768]{2,1,0:T(8,128)}, f32[48,768]{1,0:T(8,128)}, f32[16,768]{1,0:T(8,12...) custom-call(bf16[128,768]{1,0:T(8,128)(2,1)} %refs_0_.1, bf16[128,768]{1,0:T(8,128)(2,1)} %refs_1_.1, ...), custom_call_target="tpu_custom_call" | custom-call | tf_op jit(solution)/shard_map/pallas_call | solution.py:1399
  164.9 0.0 copy-start.2
  164.9 0.0 copy-start.3
  164.9 0.8 constant_dynamic-slice_fusion
  165.7 0.8 dynamic-slice_bitcast_fusion
  166.5 0.6 copy.21
  167.1 0.6 slice_bitcast_fusion
  167.7 0.0 copy-start.1
  167.7 1.7 copy.28
  169.4 1.8 %copy.29 = f32[128,768]{1,0:T(8,128)} copy(f32[128,768]{1,0:T(8,128)} %get-tuple-element.44) | data formatting | bytes 786432
  171.2 0.0 copy-done.2
  171.2 0.8 copy.30
  171.9 0.0 copy-done.3
  171.9 0.7 copy.31
  172.6 0.0 copy-done.1
  172.6 0.0 copy-start
  172.6 1.0 copy.32
  173.6 0.7 copy-done
  174.3 1.0 copy.33
Async XLA Ops:
  164.9 6.3 %copy-start.2 = (f32[3,48,768]{2,1,0:T(8,128)S(1)}, f32[3,48,768]{2,1,0:T(8,128)}, u32[]{:S(2)}) copy-start(f32[3,48,768]{2,1,0:T(8,128)} %get-tuple-element.45) | copy-start | bytes 1327108
  164.9 7.1 %copy-start.3 = (f32[48,768]{1,0:T(8,128)S(1)}, f32[48,768]{1,0:T(8,128)}, u32[]{:S(2)}) copy-start(f32[48,768]{1,0:T(8,128)} %get-tuple-element.46) | copy-start | bytes 442372
  167.7 4.9 %copy-start.1 = (f32[2,48,3072]{2,1,0:T(8,128)S(1)}, f32[2,48,3072]{2,1,0:T(8,128)}, u32[]{:S(2)}) copy-start(f32[2,48,3072]{2,1,0:T(8,128)} %get-tuple-element.50) | copy-start | bytes 3538948
  172.6 1.7 copy-start

commit v5 on v4

--- a/solution.py
+++ b/solution.py
@@ -843,26 +843,31 @@
     def flat(ref):
         return ref[...].reshape(chips * length, ref.shape[2])
 
-    g2 = dot(flat(act), flat(us), TN)
-    g2_own[...] = g2.astype(LOW).reshape(g2_own.shape)
     g2_swap = remote(g2_own.at[:, 1 - core], g2_all.at[rep], p_send.at[0], p_recv.at[0], partner)
-    g2_swap.start()
+    swaps = []
+
+    def g2_start():
+        g2 = dot(flat(act), flat(us), TN)
+        g2_own[...] = g2.astype(LOW).reshape(g2_own.shape)
+        g2_swap.start()
+
+    def g2_spread():
+        g2_swap.wait()
+        g2_all[rep] = (g2_own[:, core].astype(WIDE) + g2_all[rep].astype(WIDE)).astype(LOW)
+        for f in range(1, reps):
+            swaps.append(
+                remote(
+                    g2_all.at[rep],
+                    g2_all.at[rep],
+                    r_send.at[f - 1],
+                    r_recv.at[f - 1],
+                    {"rep": lax.rem(rep + f, reps)},
+                )
+            )
+            swaps[-1].start()
+
     for j in range(outer - 1, 1, -1):
         back_scatter.collect(j, False, back_term, None)
-    g2_swap.wait()
-    g2_all[rep] = (g2_own[:, core].astype(WIDE) + g2_all[rep].astype(WIDE)).astype(LOW)
-    swaps = []
-    for f in range(1, reps):
-        swaps.append(
-            remote(
-                g2_all.at[rep],
-                g2_all.at[rep],
-                r_send.at[f - 1],
-                r_recv.at[f - 1],
-                {"rep": lax.rem(rep + f, reps)},
-            )
-        )
-        swaps[-1].start()
     g1 = dot(flat(xs), flat(before_grad), TN)
     split(g1_own, 0, rows, pad, g1)
     g1_swap = remote(g1_own.at[:, 1 - core], g1_ref, p_send.at[1], p_recv.at[1], partner)
@@ -884,7 +889,7 @@
         ret_scatter.finish()
         back_scatter.finish()
 
-    return ret_collect, finish
+    return ret_collect, (g2_start, g2_spread), finish
 
 
 def back_part_of(
@@ -905,6 +910,7 @@
     route_ref,
     bucket_ref,
     ret_collect,
+    g2_steps,
     ret_ref,
     norm_ref,
     router_ref,
@@ -1117,9 +1123,11 @@
 
     strips_off()
     lax.fori_loop(0, chips + 2, cross, 0)
+    g2_steps[0]()
     for j in range(outer - 3 if outer > 2 else outer - 1, -1, -1):
         ret_collect(j)
     layer_ref[...] = (hidden + gate * ret_ref[...]).astype(LOW)
+    g2_steps[1]()
     own.wait()
     for copy in moves:
         copy.wait_recv()
@@ -1255,7 +1263,7 @@
         *front,
         *front_sems,
     )
-    ret_collect, expert_finish = expert_part(
+    ret_collect, g2_steps, expert_finish = expert_part(
         place,
         reps,
         rows,
@@ -1294,6 +1302,7 @@
         routes,
         buckets,
         ret_collect,
+        g2_steps,
         returned,
         norm_grad,
         router_grad,

time: 176 us -> 174 us (0.989)
  Pallas kernels: 164 us -> 162 us
    pallas_call x1, Pallas kernels: 164 us -> 162 us  [layer(): pl.pallas_call(functools.partial(layer_kernel, size, reps, heads, counts)...]
where the time goes in v5:
time: 174 us; the launch traced here: 173 us
  Pallas kernels  162 us (93%)
  local copies, waits for them, and re-layouts  10.4 us (6%)
    pallas_call x1, Pallas kernels, layer(): pl.pallas_call(functools.partial(layer_kernel, size, reps, heads, counts)...  162 us
    unnamed x15, local copies, waits for them, and re-layouts  8.27 us

profile of v5, /device:TPU:0, one launch (start us, length us, event | category | flops | bytes accessed | tf_op | source)
XLA Modules:
  0.0 173.5 jit_solution(455395617806062280)
XLA Ops:
  0.7 162.4 %shard_map.187 = (bf16[128,768]{1,0:T(8,128)(2,1)}, f32[128,768]{1,0:T(8,128)}, f32[3,48,768]{2,1,0:T(8,128)}, f32[48,768]{1,0:T(8,128)}, f32[16,768]{1,0:T(8,12...) custom-call(bf16[128,768]{1,0:T(8,128)(2,1)} %refs_0_.1, bf16[128,768]{1,0:T(8,128)(2,1)} %refs_1_.1, ...), custom_call_target="tpu_custom_call" | custom-call | tf_op jit(solution)/shard_map/pallas_call | solution.py:1408
  163.0 0.0 copy-start.2
  163.0 0.0 copy-start.3
  163.0 0.8 constant_dynamic-slice_fusion
  163.9 0.8 dynamic-slice_bitcast_fusion
  164.6 0.6 copy.21
  165.3 0.6 slice_bitcast_fusion
  165.9 0.0 copy-start.1
  165.9 1.7 copy.28
  167.6 1.8 %copy.29 = f32[128,768]{1,0:T(8,128)} copy(f32[128,768]{1,0:T(8,128)} %get-tuple-element.44) | data formatting | bytes 786432
  169.3 0.0 copy-done.2
  169.3 0.8 copy.30
  170.1 0.0 copy-done.3
  170.1 0.7 copy.31
  170.8 0.0 copy-done.1
  170.8 0.0 copy-start
  170.8 1.0 copy.32
  171.8 0.7 copy-done
  172.5 1.0 copy.33
Async XLA Ops:
  163.0 6.3 %copy-start.2 = (f32[3,48,768]{2,1,0:T(8,128)S(1)}, f32[3,48,768]{2,1,0:T(8,128)}, u32[]{:S(2)}) copy-start(f32[3,48,768]{2,1,0:T(8,128)} %get-tuple-element.45) | copy-start | bytes 1327108
  163.0 7.1 %copy-start.3 = (f32[48,768]{1,0:T(8,128)S(1)}, f32[48,768]{1,0:T(8,128)}, u32[]{:S(2)}) copy-start(f32[48,768]{1,0:T(8,128)} %get-tuple-element.46) | copy-start | bytes 442372
  165.9 4.9 %copy-start.1 = (f32[2,48,3072]{2,1,0:T(8,128)S(1)}, f32[2,48,3072]{2,1,0:T(8,128)}, u32[]{:S(2)}) copy-start(f32[2,48,3072]{2,1,0:T(8,128)} %get-tuple-element.50) | copy-start | bytes 3538948
  170.8 1.7 copy-start
